TPU v7x, 256 devices: a whole 4x4x8 slice. The times are simulated.
256 devices in a mesh: group: 4 (over x), tile: 64 (over z, y, core).
Axes of the slice: x: 4, y: 4, z: 8, core: 2. Of those that a mesh axis runs over, the one named last changes fastest.
Arguments:
- embeddings: bfloat16 [32768, 1024], P(('group', 'tile')), may hold values from -15 to 15
- row_group: int32 [32768, 1], P(('group', 'tile')), may hold values from 0 to 3, as said below
Outputs:
- max_similarity: float32 [32768], P(('group', 'tile'))
- soft_count: float32 [32768], P(('group', 'tile'))
Inputs may be any that keep to these rules, and one draw needn't show every extreme that they name: `row_group`: among the rows of one storage shard (aligned blocks of 128 rows) at most 64 name the same cluster, some cluster is named by exactly 64 of them, and every cluster is named by at least one of them.
All inputs are finite; a program needn't handle non-finite values.
Results may differ from a plain program's by a relative error of at most 0.0003.
Values may be sent and summed in bfloat16 or wider, within the bound.
No kernel may reach another device: no remote copies, remote signals or barrier semaphores. Data moves between devices by JAX's collectives and lax.ppermute only.
A program may use at most 128 MiB of HBM per device.

v0:
```python
import math

import jax
import jax.numpy as jnp
from jax import lax
from jax.sharding import PartitionSpec as P

CAP = 64


lowest = -1e30
offset = 3.0


def pair_stats(query, query_mark, query_place, keys, key_mark, key_place):
    scale = 1.0 / math.sqrt(query.shape[1])
    score = (
        lax.dot_general(query, keys, (((1,), (1,)), ((), ())), preferred_element_type=jnp.float32)
        * scale
    )
    same = (
        (query_mark[:, None] > 0)
        & (key_mark[None, :] > 0)
        & (query_place[:, None] != key_place[None, :])
    )
    weight = jnp.where(same, jnp.exp(score - offset), 0.0)
    masked = jnp.where(same, score, lowest)
    rowwise = (jnp.max(masked, 1), jnp.sum(weight, 1))
    colwise = (jnp.max(masked, 0), jnp.sum(weight, 0))
    return (rowwise, colwise)


def combine(first, second):
    return (jnp.maximum(first[0], second[0]), first[1] + second[1])


def empty_stats(length):
    return (jnp.full((length,), lowest, jnp.float32), jnp.zeros((length,), jnp.float32))


def fold_keys(carry, query, query_mark, query_place, keys, key_mark, key_place):
    length = keys.shape[0]

    def advance(inner, index):
        start = index * 2048
        rowwise, ignored = pair_stats(
            query,
            query_mark,
            query_place,
            lax.dynamic_slice_in_dim(keys, start, 2048, 0),
            lax.dynamic_slice_in_dim(key_mark, start, 2048, 0),
            lax.dynamic_slice_in_dim(key_place, start, 2048, 0),
        )
        return (combine(inner, rowwise), None)

    carry, ignored = lax.scan(advance, carry, jnp.arange(length // 2048, dtype=jnp.int32))
    return carry


def per_device(embeddings, row_group):
    groups = lax.axis_size("group")
    width = embeddings.shape[1]
    target_group = row_group[:, 0]
    onehot = (target_group[:, None] == jnp.arange(groups, dtype=jnp.int32)[None, :]).astype(
        jnp.int32
    )
    before = jnp.cumsum(onehot, 0) - onehot
    ranking = jnp.sum(before * onehot, 1)
    slot_of = target_group * CAP + ranking
    send_rows = jnp.zeros((groups * CAP, width), jnp.bfloat16).at[slot_of].set(embeddings)
    send_mark = jnp.zeros((groups * CAP,), jnp.int32).at[slot_of].set(1)
    arrived, arrived_mark = (
        lax.all_to_all(send_rows, "group", split_axis=0, concat_axis=0, tiled=True),
        lax.all_to_all(send_mark, "group", split_axis=0, concat_axis=0, tiled=True),
    )
    slots = arrived.shape[0]
    position = lax.axis_index("tile")
    own_place = position * slots + jnp.arange(slots, dtype=jnp.int32)
    keys = lax.all_gather(arrived, "tile", axis=0, tiled=True)
    key_mark = lax.all_gather(arrived_mark, "tile", axis=0, tiled=True)
    key_place = jnp.arange(keys.shape[0], dtype=jnp.int32)
    stats = fold_keys(
        empty_stats(slots), arrived, arrived_mark, own_place, keys, key_mark, key_place
    )
    top, total = stats
    soft = jnp.log1p(total)
    back_best, back_soft = (
        lax.all_to_all(top, "group", split_axis=0, concat_axis=0, tiled=True),
        lax.all_to_all(soft, "group", split_axis=0, concat_axis=0, tiled=True),
    )
    return (back_best[slot_of], back_soft[slot_of])


def solution(mesh):
    in_specs = (P(("group", "tile"), None), P(("group", "tile"), None))
    out_specs = (P(("group", "tile")), P(("group", "tile")))
    return jax.shard_map(
        per_device, mesh=mesh, in_specs=in_specs, out_specs=out_specs, check_vma=False
    )
```

profile of v0, /device:TPU:1, one launch (start us, length us, event | category | flops | bytes accessed | tf_op | source)
XLA Modules:
  0.0 237.0 jit_solution(8504820744847342677)
XLA Ops:
  7.2 0.7 fusion.13
  8.1 0.8 select_reduce_fusion.2
  9.0 0.7 fusion.14
  9.6 1.7 scatter_custom_fusion.1
  11.4 12.7 %all_to_all.48 = bf16[4,64,1024]{2,1,0:T(8,128)(2,1)} all-to-all(bf16[4,64,1024]{2,1,0:T(8,128)(2,1)S(1)} %bitcast.27), channel_id=1, replica_groups=mesh['group'=4,'tile'=64] {'group'}, dimensions={0} | all-to-all | bytes 1048576 | tf_op jit(solution)/shard_map/all_to_all | solution.py:73
  24.1 1.0 scatter_custom_fusion
  25.0 0.7 all_to_all.32
  25.7 3.2 %all-to-all-start = ((s32[4,64,1]{1,2,0:T(1,128)}), s32[4,64,1]{1,2,0:T(1,128)S(1)}, u32[]{:S(2)}, u32[]{:S(2)}) async-start(s32[4,64,1]{1,2,0:T(1,128)} %bitcast.3), calls=%async_computation | async-start | bytes 4096 | tf_op jit(solution)/shard_map/all_to_all | solution.py:74
  29.0 4.0 %all-to-all-done = s32[4,64,1]{1,2,0:T(1,128)S(1)} async-done(((s32[4,64,1]{1,2,0:T(1,128)}), s32[4,64,1]{1,2,0:T(1,128)S(1)}, u32[]{:S(2)}, u32[]{:S(2)}) %all-to-all-start) | async-done | bytes 1056 | tf_op jit(solution)/shard_map/all_to_all | solution.py:74
  33.6 0.7 reduce.11
  34.4 50.4 %all-gather = s32[64,1,256]{2,1,0:T(1,128)S(1)} all-gather(s32[1,1,256]{2,1,0:T(1,128)S(1)} %reshape.56), channel_id=1, replica_groups=mesh['group'=4,'tile'=64] {'tile'}, dimensions={0}, use_global_device_ids=true | all-gather | bytes 66560 | tf_op jit(solution)/shard_map/all_gather | solution.py:80
  84.8 85.4 %all-gather.3.cloned.1.call-done = bf16[16384,1024]{1,0:T(8,128)(2,1)} async-done(((bf16[256,1024]{1,0:T(8,128)(2,1)}), bf16[16384,1024]{1,0:T(8,128)(2,1)}) %all-gather.3.cloned.1.call-update) | async-done | bytes 33554448 | tf_op jit(solution)/shard_map/all_gather | solution.py:79
  170.2 39.8 %while.15 = (s32[]{:T(128)}, f32[256]{0:T(256)S(1)}, f32[256]{0:T(256)S(1)}, s32[256]{0:T(256)S(1)}, s32[8]{0:T(128)S(1)}, /*index=5*/s32[16384]{0:T(1024)S(1)},...) while((s32[]{:T(128)}, f32[256]{0:T(256)S(1)}, ...), condition=%wide.region_7.8_spmd.clone, body=%wide.region_4.7_spmd.clone.sunk | while | flops 1078463488 | bytes 4767449 | solution.py:56
  171.5 3.6 %select_reduce_fusion.4 = (f32[256]{0:T(256)S(1)}, f32[256]{0:T(256)S(1)}) fusion(s32[256]{0:T(256)S(1)} %iota_add_fusion.2, s32[2048]{0:T(1024)S(1)} %dynamic_slice.45, pred[256]{0:T(512)(128)(4,1)S(1)} %broadcast_compare_fusion.2, pred[2048]{0:T(1024)(128)(4,1)S(1)} %dynamic-slice_compare_fusion.2, bf16[256,1024]{1,0:T(8,128)(2,1)} %get-tuple-element.295, ...), kind=kOutput, calls=%fused_computation.9.clone.1 | convolution fusion | flops 1078459904 | bytes 4732164 | tf_op jit(solution)/shard_map/while/body/eval_jaxpr/dot_general | solution.py:18
  175.2 0.6 dynamic_slice.44
  176.5 3.6 %select_reduce_fusion.4 = (f32[256]{0:T(256)S(1)}, f32[256]{0:T(256)S(1)}) fusion(s32[256]{0:T(256)S(1)} %iota_add_fusion.2, s32[2048]{0:T(1024)S(1)} %dynamic_slice.45, pred[256]{0:T(512)(128)(4,1)S(1)} %broadcast_compare_fusion.2, pred[2048]{0:T(1024)(128)(4,1)S(1)} %dynamic-slice_compare_fusion.2, bf16[256,1024]{1,0:T(8,128)(2,1)} %get-tuple-element.295, ...), kind=kOutput, calls=%fused_computation.9.clone.1 | convolution fusion | flops 1078459904 | bytes 4732164 | tf_op jit(solution)/shard_map/while/body/eval_jaxpr/dot_general | solution.py:18
  181.5 3.6 %select_reduce_fusion.4 = (f32[256]{0:T(256)S(1)}, f32[256]{0:T(256)S(1)}) fusion(s32[256]{0:T(256)S(1)} %iota_add_fusion.2, s32[2048]{0:T(1024)S(1)} %dynamic_slice.45, pred[256]{0:T(512)(128)(4,1)S(1)} %broadcast_compare_fusion.2, pred[2048]{0:T(1024)(128)(4,1)S(1)} %dynamic-slice_compare_fusion.2, bf16[256,1024]{1,0:T(8,128)(2,1)} %get-tuple-element.295, ...), kind=kOutput, calls=%fused_computation.9.clone.1 | convolution fusion | flops 1078459904 | bytes 4732164 | tf_op jit(solution)/shard_map/while/body/eval_jaxpr/dot_general | solution.py:18
  186.4 3.6 %select_reduce_fusion.4 = (f32[256]{0:T(256)S(1)}, f32[256]{0:T(256)S(1)}) fusion(s32[256]{0:T(256)S(1)} %iota_add_fusion.2, s32[2048]{0:T(1024)S(1)} %dynamic_slice.45, pred[256]{0:T(512)(128)(4,1)S(1)} %broadcast_compare_fusion.2, pred[2048]{0:T(1024)(128)(4,1)S(1)} %dynamic-slice_compare_fusion.2, bf16[256,1024]{1,0:T(8,128)(2,1)} %get-tuple-element.295, ...), kind=kOutput, calls=%fused_computation.9.clone.1 | convolution fusion | flops 1078459904 | bytes 4732164 | tf_op jit(solution)/shard_map/while/body/eval_jaxpr/dot_general | solution.py:18
  191.4 3.6 %select_reduce_fusion.4 = (f32[256]{0:T(256)S(1)}, f32[256]{0:T(256)S(1)}) fusion(s32[256]{0:T(256)S(1)} %iota_add_fusion.2, s32[2048]{0:T(1024)S(1)} %dynamic_slice.45, pred[256]{0:T(512)(128)(4,1)S(1)} %broadcast_compare_fusion.2, pred[2048]{0:T(1024)(128)(4,1)S(1)} %dynamic-slice_compare_fusion.2, bf16[256,1024]{1,0:T(8,128)(2,1)} %get-tuple-element.295, ...), kind=kOutput, calls=%fused_computation.9.clone.1 | convolution fusion | flops 1078459904 | bytes 4732164 | tf_op jit(solution)/shard_map/while/body/eval_jaxpr/dot_general | solution.py:18
  196.4 3.6 %select_reduce_fusion.4 = (f32[256]{0:T(256)S(1)}, f32[256]{0:T(256)S(1)}) fusion(s32[256]{0:T(256)S(1)} %iota_add_fusion.2, s32[2048]{0:T(1024)S(1)} %dynamic_slice.45, pred[256]{0:T(512)(128)(4,1)S(1)} %broadcast_compare_fusion.2, pred[2048]{0:T(1024)(128)(4,1)S(1)} %dynamic-slice_compare_fusion.2, bf16[256,1024]{1,0:T(8,128)(2,1)} %get-tuple-element.295, ...), kind=kOutput, calls=%fused_computation.9.clone.1 | convolution fusion | flops 1078459904 | bytes 4732164 | tf_op jit(solution)/shard_map/while/body/eval_jaxpr/dot_general | solution.py:18
  201.3 3.6 %select_reduce_fusion.4 = (f32[256]{0:T(256)S(1)}, f32[256]{0:T(256)S(1)}) fusion(s32[256]{0:T(256)S(1)} %iota_add_fusion.2, s32[2048]{0:T(1024)S(1)} %dynamic_slice.45, pred[256]{0:T(512)(128)(4,1)S(1)} %broadcast_compare_fusion.2, pred[2048]{0:T(1024)(128)(4,1)S(1)} %dynamic-slice_compare_fusion.2, bf16[256,1024]{1,0:T(8,128)(2,1)} %get-tuple-element.295, ...), kind=kOutput, calls=%fused_computation.9.clone.1 | convolution fusion | flops 1078459904 | bytes 4732164 | tf_op jit(solution)/shard_map/while/body/eval_jaxpr/dot_general | solution.py:18
  206.3 3.6 %select_reduce_fusion.4 = (f32[256]{0:T(256)S(1)}, f32[256]{0:T(256)S(1)}) fusion(s32[256]{0:T(256)S(1)} %iota_add_fusion.2, s32[2048]{0:T(1024)S(1)} %dynamic_slice.45, pred[256]{0:T(512)(128)(4,1)S(1)} %broadcast_compare_fusion.2, pred[2048]{0:T(1024)(128)(4,1)S(1)} %dynamic-slice_compare_fusion.2, bf16[256,1024]{1,0:T(8,128)(2,1)} %get-tuple-element.295, ...), kind=kOutput, calls=%fused_computation.9.clone.1 | convolution fusion | flops 1078459904 | bytes 4732164 | tf_op jit(solution)/shard_map/while/body/eval_jaxpr/dot_general | solution.py:18
  210.0 0.7 all_to_all.41
  210.7 4.0 %all-to-all-start.3 = ((f32[4,64,1]{1,2,0:T(1,128)}), f32[4,64,1]{1,2,0:T(1,128)S(1)}, u32[]{:S(2)}, u32[]{:S(2)}) async-start(f32[4,64,1]{1,2,0:T(1,128)} %bitcast.8), calls=%async_computation.3 | async-start | bytes 4096 | tf_op jit(solution)/shard_map/all_to_all | solution.py:89
  214.6 0.7 all_to_all.38
  215.3 3.3 %all-to-all-done.3 = f32[4,64,1]{1,2,0:T(1,128)S(1)} async-done(((f32[4,64,1]{1,2,0:T(1,128)}), f32[4,64,1]{1,2,0:T(1,128)S(1)}, u32[]{:S(2)}, u32[]{:S(2)}) %all-to-all-start.3) | async-done | bytes 1056 | tf_op jit(solution)/shard_map/all_to_all | solution.py:89
  218.6 3.2 %all-to-all-start.2 = ((f32[4,64,1]{1,2,0:T(1,128)}), f32[4,64,1]{1,2,0:T(1,128)S(1)}, u32[]{:S(2)}, u32[]{:S(2)}) async-start(f32[4,64,1]{1,2,0:T(1,128)} %bitcast.7), calls=%async_computation.2 | async-start | bytes 4096 | tf_op jit(solution)/shard_map/all_to_all | solution.py:88
  222.4 0.7 reduce.13
  223.1 2.8 %all-to-all-done.2 = f32[4,64,1]{1,2,0:T(1,128)S(1)} async-done(((f32[4,64,1]{1,2,0:T(1,128)}), f32[4,64,1]{1,2,0:T(1,128)S(1)}, u32[]{:S(2)}, u32[]{:S(2)}) %all-to-all-start.2) | async-done | bytes 1056 | tf_op jit(solution)/shard_map/all_to_all | solution.py:88
  225.9 0.7 reduce.12
  226.7 1.8 gather_fusion.1
  228.4 1.8 gather_fusion
  (63 shorter events, 6.1 us)
Async XLA Ops:
  7.2 163.0 %all-gather.3.cloned.1.call-start = ((), (), s32[]{:S(2)}) async-start(), calls=%async_computation.4 | async-start | bytes 34078720 | tf_op jit(solution)/shard_map/all_gather | solution.py:79
  25.7 7.3 %all-to-all-start = ((s32[4,64,1]{1,2,0:T(1,128)}), s32[4,64,1]{1,2,0:T(1,128)S(1)}, u32[]{:S(2)}, u32[]{:S(2)}) async-start(s32[4,64,1]{1,2,0:T(1,128)} %bitcast.3), calls=%async_computation | async-start | bytes 4096 | tf_op jit(solution)/shard_map/all_to_all | solution.py:74
  210.7 7.9 %all-to-all-start.3 = ((f32[4,64,1]{1,2,0:T(1,128)}), f32[4,64,1]{1,2,0:T(1,128)S(1)}, u32[]{:S(2)}, u32[]{:S(2)}) async-start(f32[4,64,1]{1,2,0:T(1,128)} %bitcast.8), calls=%async_computation.3 | async-start | bytes 4096 | tf_op jit(solution)/shard_map/all_to_all | solution.py:89
  218.6 7.3 %all-to-all-start.2 = ((f32[4,64,1]{1,2,0:T(1,128)}), f32[4,64,1]{1,2,0:T(1,128)S(1)}, u32[]{:S(2)}, u32[]{:S(2)}) async-start(f32[4,64,1]{1,2,0:T(1,128)} %bitcast.7), calls=%async_computation.2 | async-start | bytes 4096 | tf_op jit(solution)/shard_map/all_to_all | solution.py:88
Sparse Core Ops, SparseCore 0:
  24.2 145.9 all-gather.2
where the time goes:
time: 238 us; the launch traced here: 237 us
  waiting for transfers between devices  95.5 us (40%)
  blocking collectives  63.1 us (27%)
  matrix products  29 us (12%)
  local copies, waits for them, and re-layouts  14.4 us (6%)
  between operations  14.1 us (6%)
  starting transfers between devices  10.5 us (4%)
  loops' own time  5.72 us (2%)
  other arithmetic  4.69 us (2%)
    all_gather x1, waiting for transfers between devices, per_device(): keys = lax.all_gather(arrived, 'tile', axis=0, tiled=True)  85.4 us
    all_gather x1, blocking collectives, per_device(): key_mark = lax.all_gather(arrived_mark, 'tile', axis=0, tiled=True)  50.4 us
    dot_general x8, matrix products, pair_stats(): lax.dot_general(query, keys, (((1,), (1,)), ((), ())), preferred_element_...  29 us
    all_to_all x1, blocking collectives, per_device(): lax.all_to_all(send_rows, 'group', split_axis=0, concat_axis=0, tiled=True)  12.7 us
    another operation x1, loops' own time, fold_keys(): lax.scan(advance, carry, jnp.arange(length // 2048, dtype=jnp.int32))  5.72 us
  transfers between devices with their start and end apart: 4, of which 4 were waited for; matrix products, arithmetic and copies ran while one was open for 1% of the time, Pallas kernels for 0%

commit v1 on v0

v1 whole, which is shorter than its diff:
```python
import functools
import math

import jax
import jax.numpy as jnp
from jax import lax
from jax.experimental import pallas as pl
from jax.experimental.pallas import tpu as pltpu
from jax.sharding import Mesh, PartitionSpec as P

NX, NZ, NY, NC = 4, 8, 4, 2
AXES = ("x", "z", "y", "c")
ROWS = 128
WIDTH = 1024
PAIR = 2 * ROWS
EXTRA = 16
SLOT = ROWS + EXTRA
CHUNK = PAIR + EXTRA
LOWEST = -1e30
SCALE = 1.0 / math.sqrt(WIDTH)
LOG2E = math.log2(math.e)
OFFSET = 3.0
ANY = pl.BlockSpec(memory_space=pl.ANY)
VM = pl.BlockSpec(memory_space=pltpu.VMEM)
SM = pl.BlockSpec(memory_space=pltpu.SMEM)


def device_index(x, z, y, c):
    return (((x % NX) * NZ + z % NZ) * NY + y % NY) * NC + c


def shift(value, move):
    pairs = []
    for x in range(NX):
        for z in range(NZ):
            for y in range(NY):
                for c in range(NC):
                    dx, dz, dy, dc = move(c)
                    target = device_index(x + dx, z + dz, y + dy, (c + dc) % NC)
                    pairs.append((device_index(x, z, y, c), target))
    return lax.ppermute(value, AXES, pairs)


def swap(value):
    return shift(value, lambda c: (0, 0, 0, 1))


def along_z(value):
    return shift(value, lambda c: (0, 1, 0, 0) if c == 0 else (0, -1, 0, 0))


def first_axis(value, step):
    return shift(value, lambda c: (step, 0, 0, 0) if c == 0 else (0, 0, step, 0))


def second_axis(value, step):
    return shift(value, lambda c: (0, 0, step, 0) if c == 0 else (step, 0, 0, 0))


def bf16(*shape):
    return jax.ShapeDtypeStruct(shape, jnp.bfloat16)


def f32(*shape):
    return jax.ShapeDtypeStruct(shape, jnp.float32)


def prepare_kernel(rows_ref, mark_ref, out_ref):
    out_ref[0:ROWS, :] = rows_ref[...]
    wide = jnp.broadcast_to(mark_ref[...].astype(jnp.float32), (ROWS, 128))
    for g in range(0, 8, 2):
        lane = lax.broadcasted_iota(jnp.int32, (16, 128), 1)
        both = jnp.where(lane < 64, wide[16 * g : 16 * g + 16], wide[16 * g + 16 : 16 * g + 32])
        out_ref[ROWS:SLOT, 64 * g : 64 * g + 128] = both.astype(jnp.bfloat16)
    out_ref[ROWS:SLOT, 512:640] = wide.T[0:16].astype(jnp.bfloat16)
    out_ref[ROWS:SLOT, 640:] = jnp.zeros((16, WIDTH - 640), jnp.bfloat16)


def prepare(rows, mark):
    return pl.pallas_call(
        prepare_kernel, out_shape=bf16(SLOT, WIDTH), in_specs=[VM, VM], out_specs=VM, name="prepare"
    )(rows, mark)


def pack_keys_kernel(a_ref, b_ref, out_ref):
    out_ref[0:ROWS] = a_ref[0:ROWS]
    out_ref[ROWS:PAIR] = b_ref[0:ROWS]
    out_ref[PAIR:, 0:512] = a_ref[ROWS:, 0:512]
    out_ref[PAIR:, 512:] = b_ref[ROWS:, 0:512]


def pack_queries_kernel(a_ref, b_ref, out_ref):
    out_ref[0:ROWS] = a_ref[0:ROWS]
    out_ref[ROWS:PAIR] = b_ref[0:ROWS]
    out_ref[PAIR:, 0:128] = a_ref[ROWS:, 512:640]
    out_ref[PAIR:, 128:256] = b_ref[ROWS:, 512:640]
    out_ref[PAIR:, 256:] = jnp.zeros((EXTRA, WIDTH - 256), jnp.bfloat16)


def pack(kernel, a, b, name):
    return pl.pallas_call(
        kernel, out_shape=bf16(CHUNK, WIDTH), in_specs=[VM, VM], out_specs=VM, name=name
    )(a, b)


def stage_kernel(key_rows, n_query, own, *refs):
    n_key = len(key_rows)
    q_refs, k_refs = refs[:n_query], refs[n_query : n_query + n_key]
    top_ref, total_ref, q_buf, k_buf, mark_buf, column, q_sem, k_sem, m_sem = refs[n_query + n_key :]
    starts = [sum(key_rows[:i]) for i in range(n_key)]
    length = sum(key_rows)

    copies = []
    for i in range(n_query):
        copies.append(pltpu.make_async_copy(q_refs[i], q_buf.at[i], q_sem.at[i]))
    for i, rows in enumerate(key_rows):
        copies.append(
            pltpu.make_async_copy(
                k_refs[i].at[pl.ds(0, rows)], k_buf.at[pl.ds(starts[i], rows)], k_sem.at[i]
            )
        )
        copies.append(
            pltpu.make_async_copy(k_refs[i].at[pl.ds(rows, EXTRA)], mark_buf.at[i], m_sem.at[i])
        )
    for copy in copies:
        copy.start()
    for copy in copies:
        copy.wait()

    for i, rows in enumerate(key_rows):
        for g in range(rows // 16):
            lane = 64 * (g if rows == PAIR else g + 8)
            values = mark_buf[i, :, lane : lane + 1].astype(jnp.float32)
            column[pl.ds(starts[i] + 16 * g, 16), :] = jnp.broadcast_to(values, (16, 128))

    def block(q, start, carry, diagonal):
        score = lax.dot_general(
            k_buf[pl.ds(start, PAIR), :],
            q_buf[q, 0:PAIR, :],
            (((1,), (1,)), ((), ())),
            preferred_element_type=jnp.float32,
        )
        column_mark = column[pl.ds(start, PAIR), :]
        marks = q_buf[q, PAIR:CHUNK, 0:256].astype(jnp.float32)[0:1]
        tops, totals = [], []
        for half in range(2):
            part = score[:, 128 * half : 128 * half + 128]
            same = column_mark == marks[:, 128 * half : 128 * half + 128]
            if diagonal and half == 0:
                row = lax.broadcasted_iota(jnp.int32, (PAIR, 128), 0)
                lane = lax.broadcasted_iota(jnp.int32, (PAIR, 128), 1)
                same = same & (row != lane)
            part = jnp.where(same, part, LOWEST)
            weight = jnp.exp2(part * (SCALE * LOG2E) - OFFSET * LOG2E)
            tops.append(jnp.max(part.reshape(PAIR // 8, 8, 128), 0))
            totals.append(jnp.sum(weight.reshape(PAIR // 8, 8, 128), 0))
        top, total = carry
        return (
            jnp.maximum(top, jnp.concatenate(tops, 1)),
            total + jnp.concatenate(totals, 1),
        )

    empty = (jnp.full((8, PAIR), LOWEST, jnp.float32), jnp.zeros((8, PAIR), jnp.float32))

    def query(q, first, carry):
        def body(k, carry):
            return block(q, pl.multiple_of(k * PAIR, PAIR), carry, False)

        carry = lax.fori_loop(first, length // PAIR, body, carry)
        top_ref[q], total_ref[q] = carry

    if own:
        query(0, 1, block(0, 0, empty, True))

    def outer(q, _):
        query(q, 0, empty)
        return 0

    lax.fori_loop(1 if own else 0, n_query, outer, 0)


def stage(queries, keys, own, name):
    n_query, n_key = len(queries), len(keys)
    key_rows = tuple(k.shape[0] - EXTRA for k in keys)
    length = sum(key_rows)
    return pl.pallas_call(
        functools.partial(stage_kernel, key_rows, n_query, own),
        out_shape=(f32(n_query, 8, PAIR), f32(n_query, 8, PAIR)),
        in_specs=[ANY] * (n_query + n_key),
        out_specs=(VM, VM),
        scratch_shapes=[
            pltpu.VMEM((n_query, CHUNK, WIDTH), jnp.bfloat16),
            pltpu.VMEM((length, WIDTH), jnp.bfloat16),
            pltpu.VMEM((n_key, EXTRA, WIDTH), jnp.bfloat16),
            pltpu.VMEM((length, 128), jnp.float32),
            pltpu.SemaphoreType.DMA((n_query,)),
            pltpu.SemaphoreType.DMA((n_key,)),
            pltpu.SemaphoreType.DMA((n_key,)),
        ],
        compiler_params=pltpu.CompilerParams(vmem_limit_bytes=24 << 20),
        cost_estimate=pl.CostEstimate(
            flops=2 * n_query * PAIR * length * WIDTH,
            bytes_accessed=2 * (n_query * PAIR + length) * WIDTH,
            transcendentals=n_query * PAIR * length,
        ),
        name=name,
    )(*queries, *keys)


def collect_kernel(plan, place_ref, *refs):
    out_ref = refs[-1]
    for chunk, sources in enumerate(plan):
        top = functools.reduce(jnp.maximum, [refs[2 * s][i] for s, i in sources])
        total = functools.reduce(jnp.add, [refs[2 * s + 1][i] for s, i in sources])
        top = jnp.max(top, 0, keepdims=True)
        total = jnp.sum(total, 0, keepdims=True)
        for half in range(2):
            place = place_ref[2 * chunk + half] * 2
            out_ref[pl.ds(place, 1), :] = top[:, 128 * half : 128 * half + 128]
            out_ref[pl.ds(place + 1, 1), :] = total[:, 128 * half : 128 * half + 128]


def collect(plan, places, stages):
    flat = [a for pair in stages for a in pair]
    return pl.pallas_call(
        functools.partial(collect_kernel, plan),
        out_shape=f32(2 * NX * NY, 128),
        in_specs=[SM] + [VM] * len(flat),
        out_specs=VM,
        name="collect",
    )(places, *flat)


def finish_kernel(parts_ref, top_ref, soft_ref):
    top = parts_ref[0:1, :]
    total = parts_ref[1:2, :]
    for i in range(1, NX * NY):
        top = jnp.maximum(top, parts_ref[2 * i : 2 * i + 1, :])
        total = total + parts_ref[2 * i + 1 : 2 * i + 2, :]
    top_ref[...] = top * SCALE
    soft_ref[...] = jnp.log1p(total)


def finish(parts):
    return pl.pallas_call(
        finish_kernel, out_shape=(f32(1, ROWS), f32(1, ROWS)), in_specs=[VM], out_specs=(VM, VM), name="finish"
    )(parts)


def per_device(rows, mark):
    mine = prepare(rows, mark)
    other = swap(mine)
    a = first_axis(mine, 1)
    b = first_axis(mine, -1)
    z0 = pack(pack_keys_kernel, mine, other, "pack_keys")
    t1 = along_z(z0)
    x1 = pack(pack_queries_kernel, mine, a, "pack_near")
    d = first_axis(a, 1)
    e1 = second_axis(x1, 1)
    f1 = second_axis(x1, -1)
    x2 = pack(pack_queries_kernel, b, d, "pack_far")
    t2 = along_z(t1)
    u1 = swap(t1)
    e2 = second_axis(x2, 1)
    f2 = second_axis(x2, -1)
    t3 = along_z(t2)
    u2 = swap(t2)
    g1 = second_axis(e1, 1)
    g2 = second_axis(f2, -1)
    t4 = along_z(t3[ROWS:])
    u3 = swap(t3)
    u4 = swap(t4)

    s1 = stage([x1, x2], [z0, t1, u1], True, "stage_own")
    s2 = stage([x1, x2], [t2, u2, t3, u3], False, "stage_keys")
    s3 = stage([e1, f1, e2, f2], [z0, t1, u1, t2, u2, t3, u3], False, "stage_queries")
    s4 = stage([x1, x2, e1, f1, e2, f2], [t4, u4], False, "stage_last_keys")
    s5 = stage([g1, g2], [z0, t1, u1, t2, u2, t3, u3, t4, u4], False, "stage_last_queries")

    near, far = ((0, 0), (-1, 0)), ((1, 0), (-2, 0))
    move = lambda pair, step: tuple((p, step) for p, _ in pair)
    chunks = [near, far, move(near, -1), move(near, 1), move(far, -1), move(far, 1), move(near, -2), move(far, 2)]
    plan = [[(0, 0), (1, 0), (3, 0)], [(0, 1), (1, 1), (3, 1)]]
    plan += [[(2, i), (3, i + 2)] for i in range(4)]
    plan += [[(4, i)] for i in range(2)]
    steps = jnp.array([s for pair in chunks for s in pair], jnp.int32)
    core = lax.axis_index("c")
    first, second = steps[:, 0], steps[:, 1]
    dx = jnp.where(core == 0, first, second)
    dy = jnp.where(core == 0, second, first)
    px = (lax.axis_index("x") + dx + NX) % NX
    py = (lax.axis_index("y") + dy + NY) % NY
    places = px * NY + py

    parts = collect(plan, places, [s1, s2, s3, s4, s5])
    parts = lax.all_to_all(parts, ("x", "y"), split_axis=0, concat_axis=0, tiled=True)
    top, soft = finish(parts)
    return top.reshape(ROWS), soft.reshape(ROWS)


def solution(mesh):
    fine = Mesh(mesh.devices.reshape(NX, NZ, NY, NC), AXES)
    return jax.shard_map(
        per_device,
        mesh=fine,
        in_specs=(P(AXES, None), P(AXES, None)),
        out_specs=(P(AXES), P(AXES)),
        check_vma=False,
    )
```

time: 238 us -> 121 us (0.51)
  waiting for transfers between devices: 95.5 us -> 22.3 us
  blocking collectives: 63.1 us -> 10.5 us
  Pallas kernels: 0 us -> 42.8 us
  matrix products: 29 us -> 0 us
  starting transfers between devices: 10.5 us -> 30.6 us
  between operations: 14.1 us -> 0.79 us
  loops' own time: 5.72 us -> 0 us
  other arithmetic: 4.69 us -> 0.52 us
  local copies, waits for them, and re-layouts: 14.4 us -> 11.9 us
    all_gather x1 -> x0, waiting for transfers between devices: 85.4 us -> none  [per_device(): keys = lax.all_gather(arrived, 'tile', axis=0, tiled=True)]
    all_gather x1 -> x0, blocking collectives: 50.4 us -> none  [per_device(): key_mark = lax.all_gather(arrived_mark, 'tile', axis=0, tiled=True)]
    pallas_call x0 -> x11, Pallas kernels: none -> 42.8 us  [the longest x5 32.4 us: stage(): pl.pallas_call(functools.partial(stage_kernel, key_rows, n_query, own), o...]
    ppermute x0 -> x18, starting transfers between devices: none -> 30.6 us  [shift(): return lax.ppermute(value, AXES, pairs)]
    dot_general x8 -> x0, matrix products: 29 us -> none  [pair_stats(): lax.dot_general(query, keys, (((1,), (1,)), ((), ())), preferred_element_...]
    ppermute x0 -> x18, waiting for transfers between devices: none -> 22.3 us  [shift(): return lax.ppermute(value, AXES, pairs)]
    all_to_all x3 -> x0, starting transfers between devices: 10.5 us -> none  [the longest x1 3.97 us: per_device(): lax.all_to_all(soft, 'group', split_axis=0, concat_axis=0, tiled=True)]
    all_to_all x3 -> x0, waiting for transfers between devices: 10.1 us -> none  [the longest x1 4.04 us: per_device(): lax.all_to_all(send_mark, 'group', split_axis=0, concat_axis=0, tiled=True)]
  transfers between devices with their start and end apart: 4 -> 18, of which waited for: 4 -> 7; matrix products, arithmetic and copies ran while one was open for 1% -> 2% of each run, Pallas kernels for 0% -> 24%
where the time goes in v1:
time: 121 us; the launch traced here: 119 us
  Pallas kernels  42.8 us (35%)
  starting transfers between devices  30.6 us (25%)
  waiting for transfers between devices  22.3 us (18%)
  local copies, waits for them, and re-layouts  11.9 us (10%)
  blocking collectives  10.5 us (9%)
    pallas_call x5, Pallas kernels, stage(): pl.pallas_call(functools.partial(stage_kernel, key_rows, n_query, own), o...  32.4 us
    ppermute x18, starting transfers between devices, shift(): return lax.ppermute(value, AXES, pairs)  30.6 us
    ppermute x18, waiting for transfers between devices, shift(): return lax.ppermute(value, AXES, pairs)  22.3 us
    all_to_all x1, blocking collectives, per_device(): lax.all_to_all(parts, ('x', 'y'), split_axis=0, concat_axis=0, tiled=True)  10.5 us
    unnamed x47, local copies, waits for them, and re-layouts  10.2 us
    pallas_call x3, Pallas kernels, pack(): pl.pallas_call(kernel, out_shape=bf16(CHUNK, WIDTH), in_specs=[VM, VM], o...  5.75 us
  transfers between devices with their start and end apart: 18, of which 7 were waited for; matrix products, arithmetic and copies ran while one was open for 2% of the time, Pallas kernels for 24%

profile of v1, /device:TPU:1, one launch (start us, length us, event | category | flops | bytes accessed | tf_op | source)
XLA Modules:
  0.0 119.4 jit_solution(9748230525542883142)
XLA Ops:
  0.6 1.4 %copy.5.mark_ref = s32[128,1]{1,0:T(8,128)} copy(s32[128,1]{0,1:T(1,128)} %param.4) | data formatting | bytes 1024 | tf_op args[1]
  2.0 1.8 %prepare.1.a_ref = bf16[144,1024]{1,0:T(8,128)(2,1)} custom-call(bf16[128,1024]{1,0:T(8,128)(2,1)} %rows_ref.1, s32[128,1]{1,0:T(8,128)} %copy.5.mark_ref), custom_call_target="tpu_custom_call" | custom-call | tf_op jit(solution)/shard_map/prepare/pallas_call | solution.py:80
  3.8 3.2 %collective-permute-start.3 = (bf16[144,1024]{1,0:T(8,128)(2,1)}, bf16[144,1024]{1,0:T(8,128)(2,1)S(1)}, u32[]{:S(2)}, u32[]{:S(2)}) collective-permute-start(bf16[144,1024]{1,0:T(8,128)(2,1)} %prepare.1.a_ref), channel_id=1, source_target_pairs={{0,1},{1,0},{2,3},{3,2},{4,5},{5,4},{6,7},{7,6},{8,9},{9,8},{10,11... | collective-permute-start | bytes 884744 | tf_op jit(solution)/shard_map/ppermute | solution.py:41
  7.0 1.4 %collective-permute-done.3.b_ref = bf16[144,1024]{1,0:T(8,128)(2,1)S(1)} collective-permute-done((bf16[144,1024]{1,0:T(8,128)(2,1)}, bf16[144,1024]{1,0:T(8,128)(2,1)S(1)}, u32[]{:S(2)}, u32[]{:S(2)}) %collective-permute-start.3) | collective-permute-done | bytes 294944 | tf_op jit(solution)/shard_map/ppermute | solution.py:41
  9.2 1.9 %pack_keys.1.refs_2_.refs_4_ = bf16[272,1024]{1,0:T(8,128)(2,1)} custom-call(bf16[144,1024]{1,0:T(8,128)(2,1)} %prepare.1.a_ref, bf16[144,1024]{1,0:T(8,128)(2,1)} %copy-done.20), custom_call_target="tpu_custom_call" | custom-call | tf_op jit(solution)/shard_map/pack_keys/pallas_call | solution.py:101
  11.1 3.8 %collective-permute-start.4 = (bf16[272,1024]{1,0:T(8,128)(2,1)}, bf16[272,1024]{1,0:T(8,128)(2,1)}, u32[]{:S(2)}, u32[]{:S(2)}) collective-permute-start(bf16[272,1024]{1,0:T(8,128)(2,1)} %pack_keys.1.refs_2_.refs_4_), channel_id=1, source_target_pairs={{0,8},{1,57},{2,10},{3,59},{4,12},{5,61},{6,14},{7,63},{8,16},{9,1... | collective-permute-start | bytes 1671176 | tf_op jit(solution)/shard_map/ppermute | solution.py:41
  14.9 6.8 %collective-permute-done.4.refs_3_.refs_5_ = bf16[272,1024]{1,0:T(8,128)(2,1)} collective-permute-done((bf16[272,1024]{1,0:T(8,128)(2,1)}, bf16[272,1024]{1,0:T(8,128)(2,1)}, u32[]{:S(2)}, u32[]{:S(2)}) %collective-permute-start.4) | collective-permute-done | bytes 557088 | tf_op jit(solution)/shard_map/ppermute | solution.py:41
  21.7 3.1 %collective-permute-start.6 = (bf16[272,1024]{1,0:T(8,128)(2,1)}, bf16[272,1024]{1,0:T(8,128)(2,1)}, u32[]{:S(2)}, u32[]{:S(2)}) collective-permute-start(bf16[272,1024]{1,0:T(8,128)(2,1)} %collective-permute-done.4.refs_3_.refs_5_), channel_id=1, source_target_pairs={{0,8},{1,57},{2,10},{3,59},{4,12},{5,61},{6,14},{7,63},{8,16},{9,1... | collective-permute-start | bytes 1671176 | tf_op jit(solution)/shard_map/ppermute | solution.py:41
  24.8 1.3 %collective-permute-start = (bf16[144,1024]{1,0:T(8,128)(2,1)S(1)}, bf16[144,1024]{1,0:T(8,128)(2,1)S(1)}, u32[]{:S(2)}, u32[]{:S(2)}) collective-permute-start(bf16[144,1024]{1,0:T(8,128)(2,1)S(1)} %copy-done.16), channel_id=1, source_target_pairs={{0,64},{1,3},{2,66},{3,5},{4,68},{5,7},{6,70},{7,1},{8,72},{9,11},... | collective-permute-start | bytes 884744 | tf_op jit(solution)/shard_map/ppermute | solution.py:41
  26.1 1.4 %collective-permute-start.1 = (bf16[144,1024]{1,0:T(8,128)(2,1)S(1)}, bf16[144,1024]{1,0:T(8,128)(2,1)S(1)}, u32[]{:S(2)}, u32[]{:S(2)}) collective-permute-start(bf16[144,1024]{1,0:T(8,128)(2,1)S(1)} %copy-done.16), channel_id=1, source_target_pairs={{0,192},{1,7},{2,194},{3,1},{4,196},{5,3},{6,198},{7,5},{8,200},{9... | collective-permute-start | bytes 884744 | tf_op jit(solution)/shard_map/ppermute | solution.py:41
  27.6 4.5 %collective-permute-done.b_ref = bf16[144,1024]{1,0:T(8,128)(2,1)S(1)} collective-permute-done((bf16[144,1024]{1,0:T(8,128)(2,1)S(1)}, bf16[144,1024]{1,0:T(8,128)(2,1)S(1)}, u32[]{:S(2)}, u32[]{:S(2)}) %collective-permute-start) | collective-permute-done | bytes 294944 | tf_op jit(solution)/shard_map/ppermute | solution.py:41
  32.1 2.6 %collective-permute-start.8 = (bf16[272,1024]{1,0:T(8,128)(2,1)}, bf16[272,1024]{1,0:T(8,128)(2,1)}, u32[]{:S(2)}, u32[]{:S(2)}) collective-permute-start(bf16[272,1024]{1,0:T(8,128)(2,1)} %collective-permute-done.6.refs_2_.refs_7_.refs_5_), channel_id=1, source_target_pairs={{0,8},{1,57},{2,10},{3,59},{4,12},{5,61},{6,14},{7,63},{8,16},{9,1... | collective-permute-start | bytes 1671176 | tf_op jit(solution)/shard_map/ppermute | solution.py:41
  34.7 1.9 %pack_near.1.refs_0_ = bf16[272,1024]{1,0:T(8,128)(2,1)} custom-call(bf16[144,1024]{1,0:T(8,128)(2,1)} %prepare.1.a_ref, bf16[144,1024]{1,0:T(8,128)(2,1)} %copy-done.18), custom_call_target="tpu_custom_call" | custom-call | tf_op jit(solution)/shard_map/pack_near/pallas_call | solution.py:101
  37.9 1.4 %collective-permute-done.2.b_ref = bf16[144,1024]{1,0:T(8,128)(2,1)S(1)} collective-permute-done((bf16[144,1024]{1,0:T(8,128)(2,1)S(1)}, bf16[144,1024]{1,0:T(8,128)(2,1)S(1)}, u32[]{:S(2)}, u32[]{:S(2)}) %collective-permute-start.2) | collective-permute-done | bytes 294944 | tf_op jit(solution)/shard_map/ppermute | solution.py:41
  40.0 1.9 %pack_far.1.refs_1_ = bf16[272,1024]{1,0:T(8,128)(2,1)} custom-call(bf16[144,1024]{1,0:T(8,128)(2,1)} %copy-done.17, bf16[144,1024]{1,0:T(8,128)(2,1)} %copy-done.19), custom_call_target="tpu_custom_call" | custom-call | tf_op jit(solution)/shard_map/pack_far/pallas_call | solution.py:101
  41.9 2.5 %collective-permute-start.13 = (bf16[272,1024]{1,0:T(8,128)(2,1)}, bf16[272,1024]{1,0:T(8,128)(2,1)S(1)}, u32[]{:S(2)}, u32[]{:S(2)}) collective-permute-start(bf16[272,1024]{1,0:T(8,128)(2,1)} %pack_far.1.refs_1_), channel_id=1, source_target_pairs={{0,6},{1,193},{2,0},{3,195},{4,2},{5,197},{6,4},{7,199},{8,14},{9,... | collective-permute-start | bytes 1671176 | tf_op jit(solution)/shard_map/ppermute | solution.py:41
  45.5 1.2 %collective-permute-done.10.refs_0_.refs_2_ = bf16[272,1024]{1,0:T(8,128)(2,1)S(1)} collective-permute-done((bf16[272,1024]{1,0:T(8,128)(2,1)}, bf16[272,1024]{1,0:T(8,128)(2,1)S(1)}, u32[]{:S(2)}, u32[]{:S(2)}) %collective-permute-start.10) | collective-permute-done | bytes 557088 | tf_op jit(solution)/shard_map/ppermute | solution.py:41
  46.8 1.3 %collective-permute-start.11 = (bf16[272,1024]{1,0:T(8,128)(2,1)S(1)}, bf16[272,1024]{1,0:T(8,128)(2,1)S(1)}, u32[]{:S(2)}, u32[]{:S(2)}) collective-permute-start(bf16[272,1024]{1,0:T(8,128)(2,1)S(1)} %copy-done), channel_id=1, source_target_pairs={{0,6},{1,193},{2,0},{3,195},{4,2},{5,197},{6,4},{7,199},{8,14},{9,... | collective-permute-start | bytes 1671176 | tf_op jit(solution)/shard_map/ppermute | solution.py:41
  48.0 3.2 %collective-permute-done.13.refs_3_.refs_5_ = bf16[272,1024]{1,0:T(8,128)(2,1)S(1)} collective-permute-done((bf16[272,1024]{1,0:T(8,128)(2,1)}, bf16[272,1024]{1,0:T(8,128)(2,1)S(1)}, u32[]{:S(2)}, u32[]{:S(2)}) %collective-permute-start.13) | collective-permute-done | bytes 557088 | tf_op jit(solution)/shard_map/ppermute | solution.py:41
  52.0 1.7 %slice.12 = bf16[144,1024]{1,0:T(8,128)(2,1)} slice(bf16[272,1024]{1,0:T(8,128)(2,1)} %collective-permute-done.8.refs_4_.refs_9_.refs_7_), slice={[128:272], [0:1024]} | slice | bytes 589824 | tf_op jit(solution)/shard_map/slice | solution.py:270
  55.8 1.2 %collective-permute-start.16 = (bf16[272,1024]{1,0:T(8,128)(2,1)S(1)}, bf16[272,1024]{1,0:T(8,128)(2,1)S(1)}, u32[]{:S(2)}, u32[]{:S(2)}) collective-permute-start(bf16[272,1024]{1,0:T(8,128)(2,1)S(1)} %collective-permute-done.10.refs_0_.refs_2_), channel_id=1, source_target_pairs={{0,2},{1,65},{2,4},{3,67},{4,6},{5,69},{6,0},{7,71},{8,10},{9,73},... | collective-permute-start | bytes 1671176 | tf_op jit(solution)/shard_map/ppermute | solution.py:41
  57.0 3.8 %collective-permute-done.14.refs_6_.refs_9_ = bf16[144,1024]{1,0:T(8,128)(2,1)} collective-permute-done((bf16[144,1024]{1,0:T(8,128)(2,1)}, bf16[144,1024]{1,0:T(8,128)(2,1)}, u32[]{:S(2)}, u32[]{:S(2)}) %collective-permute-start.14) | collective-permute-done | bytes 294944 | tf_op jit(solution)/shard_map/ppermute | solution.py:41
  60.7 2.2 %collective-permute-start.17 = (bf16[272,1024]{1,0:T(8,128)(2,1)S(1)}, bf16[272,1024]{1,0:T(8,128)(2,1)S(1)}, u32[]{:S(2)}, u32[]{:S(2)}) collective-permute-start(bf16[272,1024]{1,0:T(8,128)(2,1)S(1)} %collective-permute-done.13.refs_3_.refs_5_), channel_id=1, source_target_pairs={{0,6},{1,193},{2,0},{3,195},{4,2},{5,197},{6,4},{7,199},{8,14},{9,... | collective-permute-start | bytes 1671176 | tf_op jit(solution)/shard_map/ppermute | solution.py:41
  64.0 3.5 %stage_own.1 = (f32[2,8,256]{2,1,0:T(8,128)S(1)}, f32[2,8,256]{2,1,0:T(8,128)S(1)}) custom-call(bf16[272,1024]{1,0:T(8,128)(2,1)S(1)} %copy-done, bf16[272,1024]{1,0:T(8,128)(2,1)S(1)} %copy-done.1, bf16[272,1024]{1,0:T(8,128)(2,1)S(1)} %copy-done.2, bf16[272,1024]{1,0:T(8,128)(2,1)} %collective-permute-done.4.refs_3_.refs_5_, bf16[272,1024]{1,0:T(8,128)(2,1)S(1)} %copy-done.14), custom_call_target="tpu_custom_call" | custom-call | flops 805306368 | bytes 2621440 | tf_op jit(solution)/shard_map/stage_own/pallas_call | solution.py:186
  68.7 4.7 %collective-permute-start.15 = (bf16[144,1024]{1,0:T(8,128)(2,1)}, bf16[144,1024]{1,0:T(8,128)(2,1)S(1)}, u32[]{:S(2)}, u32[]{:S(2)}) collective-permute-start(bf16[144,1024]{1,0:T(8,128)(2,1)} %collective-permute-done.14.refs_6_.refs_9_), channel_id=1, source_target_pairs={{0,1},{1,0},{2,3},{3,2},{4,5},{5,4},{6,7},{7,6},{8,9},{9,8},{10,11... | collective-permute-start | bytes 884744 | tf_op jit(solution)/shard_map/ppermute | solution.py:41
  73.4 4.8 %stage_keys.1 = (f32[2,8,256]{2,1,0:T(8,128)S(1)}, f32[2,8,256]{2,1,0:T(8,128)S(1)}) custom-call(bf16[272,1024]{1,0:T(8,128)(2,1)S(1)} %copy-done, bf16[272,1024]{1,0:T(8,128)(2,1)S(1)} %copy-done.1, bf16[272,1024]{1,0:T(8,128)(2,1)} %collective-permute-done.6.refs_2_.refs_7_.refs_5_, bf16[272,1024]{1,0:T(8,128)(2,1)} %collective-permute-done.7.refs_3_.refs_8_.refs_6_, ...), custom_call_target="tpu_custom_call" | custom-call | flops 1073741824 | bytes 3145728 | tf_op jit(solution)/shard_map/stage_keys/pallas_call | solution.py:186
  79.4 12.3 %stage_queries.1 = (f32[4,8,256]{2,1,0:T(8,128)S(1)}, f32[4,8,256]{2,1,0:T(8,128)S(1)}) custom-call(bf16[272,1024]{1,0:T(8,128)(2,1)S(1)} %collective-permute-done.10.refs_0_.refs_2_, bf16[272,1024]{1,0:T(8,128)(2,1)S(1)} %collective-permute-done.11.refs_1_.refs_3_, bf16[272,1024]{1,0:T(8,128)(2,1)} %collective-permute-done.12.refs_2_.refs_4_, ...), custom_call_target="tpu_custom_call" | custom-call | flops 3758096384 | bytes 5767168 | tf_op jit(solution)/shard_map/stage_queries/pallas_call | solution.py:186
  91.7 3.7 %stage_last_keys.1 = (f32[6,8,256]{2,1,0:T(8,128)S(1)}, f32[6,8,256]{2,1,0:T(8,128)S(1)}) custom-call(bf16[272,1024]{1,0:T(8,128)(2,1)S(1)} %copy-done, bf16[272,1024]{1,0:T(8,128)(2,1)S(1)} %copy-done.1, bf16[272,1024]{1,0:T(8,128)(2,1)S(1)} %collective-permute-done.10.refs_0_.refs_2_, bf16[272,1024]{1,0:T(8,128)(2,1)S(1)} %collective-permute-done.11.refs_1_.refs_3_, ...), custom_call_target="tpu_custom_call" | custom-call | flops 805306368 | bytes 3670016 | tf_op jit(solution)/shard_map/stage_last_keys/pallas_call | solution.py:186
  96.7 8.1 %stage_last_queries.1 = (f32[2,8,256]{2,1,0:T(8,128)S(1)}, f32[2,8,256]{2,1,0:T(8,128)S(1)}) custom-call(bf16[272,1024]{1,0:T(8,128)(2,1)S(1)} %collective-permute-done.16.refs_0_, bf16[272,1024]{1,0:T(8,128)(2,1)S(1)} %collective-permute-done.17.refs_1_, bf16[272,1024]{1,0:T(8,128)(2,1)S(1)} %copy-done.2, ...), custom_call_target="tpu_custom_call" | custom-call | flops 2147483648 | bytes 5242880 | tf_op jit(solution)/shard_map/stage_last_queries/pallas_call | solution.py:186
  106.1 1.6 %collect.1 = f32[32,128]{1,0:T(8,128)} custom-call(s32[16]{0:T(128)} %fusion.place_ref, f32[2,8,256]{2,1,0:T(8,128)} %copy-done.7, f32[2,8,256]{2,1,0:T(8,128)} %copy-done.8, f32[2,8,256]{2,1,0:T(8,128)} %copy-done.9, f32[2,8,256]{2,1,0:T(8,128)} %copy-done.10, f32[4,8,256]{2,1,0:T(8,128)} %copy-done.5, f32[4,8,256]{2,1,0:T(8,128)} %copy-done.6, ...), custom_call_target="tpu_custom_call" | custom-call | tf_op jit(solution)/shard_map/collect/pallas_call | solution.py:225
  107.6 10.5 %all_to_all.11 = f32[16,2,128]{2,1,0:T(2,128)} all-to-all(f32[16,2,128]{2,1,0:T(2,128)} %bitcast.12), channel_id=1, replica_groups=mesh['x'=4,'z'=8,'y'=4,'c'=2] {'x','y'}, dimensions={0} | all-to-all | bytes 32768 | tf_op jit(solution)/shard_map/all_to_all | solution.py:296
  118.2 1.3 %finish.1 = (f32[1,128]{1,0:T(1,128)}, f32[1,128]{1,0:T(1,128)}) custom-call(f32[32,128]{1,0:T(8,128)} %bitcast.13), custom_call_target="tpu_custom_call" | custom-call | tf_op jit(solution)/shard_map/finish/pallas_call | solution.py:245
  (65 shorter events, 12.5 us)
Async XLA Ops:
  3.8 21.0 %copy-start.16 = (bf16[144,1024]{1,0:T(8,128)(2,1)S(1)}, bf16[144,1024]{1,0:T(8,128)(2,1)}, u32[]{:S(2)}) copy-start(bf16[144,1024]{1,0:T(8,128)(2,1)} %prepare.1.a_ref) | copy-start | bytes 884740
  3.8 4.7 %collective-permute-start.3 = (bf16[144,1024]{1,0:T(8,128)(2,1)}, bf16[144,1024]{1,0:T(8,128)(2,1)S(1)}, u32[]{:S(2)}, u32[]{:S(2)}) collective-permute-start(bf16[144,1024]{1,0:T(8,128)(2,1)} %prepare.1.a_ref), channel_id=1, source_target_pairs={{0,1},{1,0},{2,3},{3,2},{4,5},{5,4},{6,7},{7,6},{8,9},{9,8},{10,11... | collective-permute-start | bytes 884744 | tf_op jit(solution)/shard_map/ppermute | solution.py:41
  8.5 0.7 copy-start.20
  11.1 10.6 %collective-permute-start.4 = (bf16[272,1024]{1,0:T(8,128)(2,1)}, bf16[272,1024]{1,0:T(8,128)(2,1)}, u32[]{:S(2)}, u32[]{:S(2)}) collective-permute-start(bf16[272,1024]{1,0:T(8,128)(2,1)} %pack_keys.1.refs_2_.refs_4_), channel_id=1, source_target_pairs={{0,8},{1,57},{2,10},{3,59},{4,12},{5,61},{6,14},{7,63},{8,16},{9,1... | collective-permute-start | bytes 1671176 | tf_op jit(solution)/shard_map/ppermute | solution.py:41
  21.7 10.4 %collective-permute-start.6 = (bf16[272,1024]{1,0:T(8,128)(2,1)}, bf16[272,1024]{1,0:T(8,128)(2,1)}, u32[]{:S(2)}, u32[]{:S(2)}) collective-permute-start(bf16[272,1024]{1,0:T(8,128)(2,1)} %collective-permute-done.4.refs_3_.refs_5_), channel_id=1, source_target_pairs={{0,8},{1,57},{2,10},{3,59},{4,12},{5,61},{6,14},{7,63},{8,16},{9,1... | collective-permute-start | bytes 1671176 | tf_op jit(solution)/shard_map/ppermute | solution.py:41
  24.8 7.2 %collective-permute-start = (bf16[144,1024]{1,0:T(8,128)(2,1)S(1)}, bf16[144,1024]{1,0:T(8,128)(2,1)S(1)}, u32[]{:S(2)}, u32[]{:S(2)}) collective-permute-start(bf16[144,1024]{1,0:T(8,128)(2,1)S(1)} %copy-done.16), channel_id=1, source_target_pairs={{0,64},{1,3},{2,66},{3,5},{4,68},{5,7},{6,70},{7,1},{8,72},{9,11},... | collective-permute-start | bytes 884744 | tf_op jit(solution)/shard_map/ppermute | solution.py:41
  26.1 11.7 %collective-permute-start.1 = (bf16[144,1024]{1,0:T(8,128)(2,1)S(1)}, bf16[144,1024]{1,0:T(8,128)(2,1)S(1)}, u32[]{:S(2)}, u32[]{:S(2)}) collective-permute-start(bf16[144,1024]{1,0:T(8,128)(2,1)S(1)} %copy-done.16), channel_id=1, source_target_pairs={{0,192},{1,7},{2,194},{3,1},{4,196},{5,3},{6,198},{7,5},{8,200},{9... | collective-permute-start | bytes 884744 | tf_op jit(solution)/shard_map/ppermute | solution.py:41
  32.1 2.7 %copy-start.18 = (bf16[144,1024]{1,0:T(8,128)(2,1)}, bf16[144,1024]{1,0:T(8,128)(2,1)S(1)}, u32[]{:S(2)}) copy-start(bf16[144,1024]{1,0:T(8,128)(2,1)S(1)} %collective-permute-done.b_ref) | copy-start | bytes 884740
  32.1 7.2 %collective-permute-start.2 = (bf16[144,1024]{1,0:T(8,128)(2,1)S(1)}, bf16[144,1024]{1,0:T(8,128)(2,1)S(1)}, u32[]{:S(2)}, u32[]{:S(2)}) collective-permute-start(bf16[144,1024]{1,0:T(8,128)(2,1)S(1)} %collective-permute-done.b_ref), channel_id=1, source_target_pairs={{0,64},{1,3},{2,66},{3,5},{4,68},{5,7},{6,70},{7,1},{8,72},{9,11},... | collective-permute-start | bytes 884744 | tf_op jit(solution)/shard_map/ppermute | solution.py:41
  32.1 12.9 %collective-permute-start.8 = (bf16[272,1024]{1,0:T(8,128)(2,1)}, bf16[272,1024]{1,0:T(8,128)(2,1)}, u32[]{:S(2)}, u32[]{:S(2)}) collective-permute-start(bf16[272,1024]{1,0:T(8,128)(2,1)} %collective-permute-done.6.refs_2_.refs_7_.refs_5_), channel_id=1, source_target_pairs={{0,8},{1,57},{2,10},{3,59},{4,12},{5,61},{6,14},{7,63},{8,16},{9,1... | collective-permute-start | bytes 1671176 | tf_op jit(solution)/shard_map/ppermute | solution.py:41
  36.7 10.1 %copy-start = (bf16[272,1024]{1,0:T(8,128)(2,1)S(1)}, bf16[272,1024]{1,0:T(8,128)(2,1)}, u32[]{:S(2)}) copy-start(bf16[272,1024]{1,0:T(8,128)(2,1)} %pack_near.1.refs_0_) | copy-start | bytes 1671172
  36.7 10.1 %collective-permute-start.10 = (bf16[272,1024]{1,0:T(8,128)(2,1)}, bf16[272,1024]{1,0:T(8,128)(2,1)S(1)}, u32[]{:S(2)}, u32[]{:S(2)}) collective-permute-start(bf16[272,1024]{1,0:T(8,128)(2,1)} %pack_near.1.refs_0_), channel_id=1, source_target_pairs={{0,2},{1,65},{2,4},{3,67},{4,6},{5,69},{6,0},{7,71},{8,10},{9,73},... | collective-permute-start | bytes 1671176 | tf_op jit(solution)/shard_map/ppermute | solution.py:41
  37.9 1.4 %copy-start.17 = (bf16[144,1024]{1,0:T(8,128)(2,1)}, bf16[144,1024]{1,0:T(8,128)(2,1)S(1)}, u32[]{:S(2)}) copy-start(bf16[144,1024]{1,0:T(8,128)(2,1)S(1)} %collective-permute-done.1.a_ref) | copy-start | bytes 884740
  39.3 0.7 copy-start.19
  40.0 22.9 %copy-start.2 = (bf16[272,1024]{1,0:T(8,128)(2,1)S(1)}, bf16[272,1024]{1,0:T(8,128)(2,1)}, u32[]{:S(2)}) copy-start(bf16[272,1024]{1,0:T(8,128)(2,1)} %pack_keys.1.refs_2_.refs_4_) | copy-start | bytes 1671172
  41.9 21.0 %copy-start.1 = (bf16[272,1024]{1,0:T(8,128)(2,1)S(1)}, bf16[272,1024]{1,0:T(8,128)(2,1)}, u32[]{:S(2)}) copy-start(bf16[272,1024]{1,0:T(8,128)(2,1)} %pack_far.1.refs_1_) | copy-start | bytes 1671172
  41.9 9.3 %collective-permute-start.13 = (bf16[272,1024]{1,0:T(8,128)(2,1)}, bf16[272,1024]{1,0:T(8,128)(2,1)S(1)}, u32[]{:S(2)}, u32[]{:S(2)}) collective-permute-start(bf16[272,1024]{1,0:T(8,128)(2,1)} %pack_far.1.refs_1_), channel_id=1, source_target_pairs={{0,6},{1,193},{2,0},{3,195},{4,2},{5,197},{6,4},{7,199},{8,14},{9,... | collective-permute-start | bytes 1671176 | tf_op jit(solution)/shard_map/ppermute | solution.py:41
  44.4 9.3 %collective-permute-start.5 = (bf16[272,1024]{1,0:T(8,128)(2,1)}, bf16[272,1024]{1,0:T(8,128)(2,1)S(1)}, u32[]{:S(2)}, u32[]{:S(2)}) collective-permute-start(bf16[272,1024]{1,0:T(8,128)(2,1)} %collective-permute-done.4.refs_3_.refs_5_), channel_id=1, source_target_pairs={{0,1},{1,0},{2,3},{3,2},{4,5},{5,4},{6,7},{7,6},{8,9},{9,8},{10,11... | collective-permute-start | bytes 1671176 | tf_op jit(solution)/shard_map/ppermute | solution.py:41
  45.0 10.8 %collective-permute-start.7 = (bf16[272,1024]{1,0:T(8,128)(2,1)}, bf16[272,1024]{1,0:T(8,128)(2,1)}, u32[]{:S(2)}, u32[]{:S(2)}) collective-permute-start(bf16[272,1024]{1,0:T(8,128)(2,1)} %collective-permute-done.6.refs_2_.refs_7_.refs_5_), channel_id=1, source_target_pairs={{0,1},{1,0},{2,3},{3,2},{4,5},{5,4},{6,7},{7,6},{8,9},{9,8},{10,11... | collective-permute-start | bytes 1671176 | tf_op jit(solution)/shard_map/ppermute | solution.py:41
  45.0 23.7 %collective-permute-start.9 = (bf16[272,1024]{1,0:T(8,128)(2,1)}, bf16[272,1024]{1,0:T(8,128)(2,1)}, u32[]{:S(2)}, u32[]{:S(2)}) collective-permute-start(bf16[272,1024]{1,0:T(8,128)(2,1)} %collective-permute-done.8.refs_4_.refs_9_.refs_7_), channel_id=1, source_target_pairs={{0,1},{1,0},{2,3},{3,2},{4,5},{5,4},{6,7},{7,6},{8,9},{9,8},{10,11... | collective-permute-start | bytes 1671176 | tf_op jit(solution)/shard_map/ppermute | solution.py:41
  46.8 32.6 %collective-permute-start.11 = (bf16[272,1024]{1,0:T(8,128)(2,1)S(1)}, bf16[272,1024]{1,0:T(8,128)(2,1)S(1)}, u32[]{:S(2)}, u32[]{:S(2)}) collective-permute-start(bf16[272,1024]{1,0:T(8,128)(2,1)S(1)} %copy-done), channel_id=1, source_target_pairs={{0,6},{1,193},{2,0},{3,195},{4,2},{5,197},{6,4},{7,199},{8,14},{9,... | collective-permute-start | bytes 1671176 | tf_op jit(solution)/shard_map/ppermute | solution.py:41
  51.2 28.2 %collective-permute-start.12 = (bf16[272,1024]{1,0:T(8,128)(2,1)}, bf16[272,1024]{1,0:T(8,128)(2,1)}, u32[]{:S(2)}, u32[]{:S(2)}) collective-permute-start(bf16[272,1024]{1,0:T(8,128)(2,1)} %pack_far.1.refs_1_), channel_id=1, source_target_pairs={{0,2},{1,65},{2,4},{3,67},{4,6},{5,69},{6,0},{7,71},{8,10},{9,73},... | collective-permute-start | bytes 1671176 | tf_op jit(solution)/shard_map/ppermute | solution.py:41
  53.7 0.8 copy-start.13
  54.5 6.2 %collective-permute-start.14 = (bf16[144,1024]{1,0:T(8,128)(2,1)}, bf16[144,1024]{1,0:T(8,128)(2,1)}, u32[]{:S(2)}, u32[]{:S(2)}) collective-permute-start(bf16[144,1024]{1,0:T(8,128)(2,1)} %slice.12), channel_id=1, source_target_pairs={{0,8},{1,57},{2,10},{3,59},{4,12},{5,61},{6,14},{7,63},{8,16},{9,1... | collective-permute-start | bytes 884744 | tf_op jit(solution)/shard_map/ppermute | solution.py:41
  54.6 0.7 copy-start.22
  55.8 41.0 %collective-permute-start.16 = (bf16[272,1024]{1,0:T(8,128)(2,1)S(1)}, bf16[272,1024]{1,0:T(8,128)(2,1)S(1)}, u32[]{:S(2)}, u32[]{:S(2)}) collective-permute-start(bf16[272,1024]{1,0:T(8,128)(2,1)S(1)} %collective-permute-done.10.refs_0_.refs_2_), channel_id=1, source_target_pairs={{0,2},{1,65},{2,4},{3,67},{4,6},{5,69},{6,0},{7,71},{8,10},{9,73},... | collective-permute-start | bytes 1671176 | tf_op jit(solution)/shard_map/ppermute | solution.py:41
  60.7 36.0 %collective-permute-start.17 = (bf16[272,1024]{1,0:T(8,128)(2,1)S(1)}, bf16[272,1024]{1,0:T(8,128)(2,1)S(1)}, u32[]{:S(2)}, u32[]{:S(2)}) collective-permute-start(bf16[272,1024]{1,0:T(8,128)(2,1)S(1)} %collective-permute-done.13.refs_3_.refs_5_), channel_id=1, source_target_pairs={{0,6},{1,193},{2,0},{3,195},{4,2},{5,197},{6,4},{7,199},{8,14},{9,... | collective-permute-start | bytes 1671176 | tf_op jit(solution)/shard_map/ppermute | solution.py:41
  62.9 1.1 copy-start.14
  68.7 10.7 %copy-start.15 = (bf16[272,1024]{1,0:T(8,128)(2,1)S(1)}, bf16[272,1024]{1,0:T(8,128)(2,1)}, u32[]{:S(2)}) copy-start(bf16[272,1024]{1,0:T(8,128)(2,1)} %copy-done.13) | copy-start | bytes 1671172
  68.7 23.1 %collective-permute-start.15 = (bf16[144,1024]{1,0:T(8,128)(2,1)}, bf16[144,1024]{1,0:T(8,128)(2,1)S(1)}, u32[]{:S(2)}, u32[]{:S(2)}) collective-permute-start(bf16[144,1024]{1,0:T(8,128)(2,1)} %collective-permute-done.14.refs_6_.refs_9_), channel_id=1, source_target_pairs={{0,1},{1,0},{2,3},{3,2},{4,5},{5,4},{6,7},{7,6},{8,9},{9,8},{10,11... | collective-permute-start | bytes 884744 | tf_op jit(solution)/shard_map/ppermute | solution.py:41
  91.7 3.8 %copy-start.5 = (f32[4,8,256]{2,1,0:T(8,128)}, f32[4,8,256]{2,1,0:T(8,128)S(1)}, u32[]{:S(2)}) copy-start(f32[4,8,256]{2,1,0:T(8,128)S(1)} %get-tuple-element.18.refs_4_) | copy-start | bytes 98308
  91.7 3.8 %copy-start.6 = (f32[4,8,256]{2,1,0:T(8,128)}, f32[4,8,256]{2,1,0:T(8,128)S(1)}, u32[]{:S(2)}) copy-start(f32[4,8,256]{2,1,0:T(8,128)S(1)} %get-tuple-element.19.refs_5_) | copy-start | bytes 98308
  (9 other events, 5.5 us)

commit v2 on v1

v2 whole, which is shorter than its diff:
```python
import functools
import math

import jax
import jax.numpy as jnp
from jax import lax
from jax.experimental import pallas as pl
from jax.experimental.pallas import tpu as pltpu
from jax.sharding import Mesh, PartitionSpec as P

NX, NZ, NY, NC = 4, 8, 4, 2
AXES = ("x", "z", "y", "c")
ROWS = 128
WIDTH = 1024
PAIR = 2 * ROWS
EXTRA = 16
SLOT = ROWS + EXTRA
CHUNK = PAIR + EXTRA
LOWEST = -1e30
SCALE = 1.0 / math.sqrt(WIDTH)
LOG2E = math.log2(math.e)
OFFSET = 3.0
VM = pl.BlockSpec(memory_space=pltpu.VMEM)
SMALL = pltpu.CompilerParams(vmem_limit_bytes=4 << 20)


def device_index(x, z, y, c):
    return (((x % NX) * NZ + z % NZ) * NY + y % NY) * NC + c


def shift(value, move):
    pairs = []
    for x in range(NX):
        for z in range(NZ):
            for y in range(NY):
                for c in range(NC):
                    dx, dz, dy, dc = move(c)
                    target = device_index(x + dx, z + dz, y + dy, (c + dc) % NC)
                    pairs.append((device_index(x, z, y, c), target))
    return lax.ppermute(value, AXES, pairs)


def swap(value):
    return shift(value, lambda c: (0, 0, 0, 1))


def along_z(value, step):
    return shift(value, lambda c: (0, step, 0, 0))


def away(value):
    return shift(value, lambda c: (0, 1, 0, 0) if c == 0 else (0, -1, 0, 0))


def first_axis(value, step):
    return shift(value, lambda c: (step, 0, 0, 0) if c == 0 else (0, 0, step, 0))


def second_axis(value, step):
    return shift(value, lambda c: (0, 0, step, 0) if c == 0 else (step, 0, 0, 0))


def bf16(*shape):
    return jax.ShapeDtypeStruct(shape, jnp.bfloat16)


def f32(*shape):
    return jax.ShapeDtypeStruct(shape, jnp.float32)


def prepare_kernel(rows_ref, mark_ref, out_ref):
    out_ref[0:ROWS, :] = rows_ref[...]
    along = jnp.broadcast_to(mark_ref[...].astype(jnp.float32), (ROWS, 128))
    wide = along.T
    lane = lax.broadcasted_iota(jnp.int32, (16, 128), 1)
    for g in range(0, 8, 2):
        both = jnp.where(lane < 64, wide[16 * g : 16 * g + 16], wide[16 * g + 16 : 16 * g + 32])
        out_ref[ROWS:SLOT, 64 * g : 64 * g + 128] = both.astype(jnp.bfloat16)
    out_ref[ROWS:SLOT, 512:640] = along[0:16].astype(jnp.bfloat16)
    out_ref[ROWS:SLOT, 640:] = jnp.zeros((16, WIDTH - 640), jnp.bfloat16)


def prepare(rows, mark):
    return pl.pallas_call(
        prepare_kernel,
        out_shape=bf16(SLOT, WIDTH),
        in_specs=[VM, VM],
        out_specs=VM,
        compiler_params=SMALL,
        name="prepare",
    )(rows, mark.reshape(1, ROWS))


def pack_keys_kernel(a_ref, b_ref, out_ref):
    out_ref[0:ROWS] = a_ref[0:ROWS]
    out_ref[ROWS:PAIR] = b_ref[0:ROWS]
    out_ref[PAIR:, 0:512] = a_ref[ROWS:, 0:512]
    out_ref[PAIR:, 512:] = b_ref[ROWS:, 0:512]


def pack_far_keys_kernel(low_ref, low_other_ref, high_ref, high_other_ref, out_ref):
    @pl.when(lax.axis_index("c") == 0)
    def _():
        pack_keys_kernel(low_ref, low_other_ref, out_ref)

    @pl.when(lax.axis_index("c") != 0)
    def _():
        pack_keys_kernel(high_ref, high_other_ref, out_ref)


def second_half_kernel(keys_ref, out_ref):
    out_ref[...] = keys_ref[ROWS:]


def second_half(keys):
    return pl.pallas_call(
        second_half_kernel,
        out_shape=bf16(SLOT, WIDTH),
        in_specs=[VM],
        out_specs=VM,
        compiler_params=SMALL,
        name="second_half",
    )(keys)


def pack_queries_kernel(a_ref, b_ref, out_ref):
    out_ref[0:ROWS] = a_ref[0:ROWS]
    out_ref[ROWS:PAIR] = b_ref[0:ROWS]
    out_ref[PAIR:, 0:128] = a_ref[ROWS:, 512:640]
    out_ref[PAIR:, 128:256] = b_ref[ROWS:, 512:640]
    out_ref[PAIR:, 256:] = jnp.zeros((EXTRA, WIDTH - 256), jnp.bfloat16)


def pack(kernel, name, *parts):
    return pl.pallas_call(
        kernel,
        out_shape=bf16(CHUNK, WIDTH),
        in_specs=[VM] * len(parts),
        out_specs=VM,
        compiler_params=SMALL,
        name=name,
    )(*parts)


def stage_kernel(key_rows, n_query, work, own, *refs):
    n_key = len(key_rows)
    q_refs, k_refs = refs[:n_query], refs[n_query : n_query + n_key]
    out_ref, column = refs[n_query + n_key :]

    for i, rows in enumerate(key_rows):
        for g in range(rows // 16):
            lane = 64 * (g if rows == PAIR else g + 8)
            values = k_refs[i][rows : rows + EXTRA, lane : lane + 1].astype(jnp.float32)
            column[i, 16 * g : 16 * g + 16, :] = jnp.broadcast_to(values, (16, 128))

    for q, keys in enumerate(work):
        marks = q_refs[q][PAIR:CHUNK, 0:PAIR].astype(jnp.float32)[0:1]
        top = jnp.full((8, PAIR), LOWEST, jnp.float32)
        total = jnp.zeros((8, PAIR), jnp.float32)
        for k in keys:
            rows = key_rows[k]
            score = lax.dot_general(
                k_refs[k][0:rows, :],
                q_refs[q][0:PAIR, :],
                (((1,), (1,)), ((), ())),
                preferred_element_type=jnp.float32,
            )
            column_mark = column[k, 0:rows, :]
            tops, totals = [], []
            for half in range(2):
                part = score[:, 128 * half : 128 * half + 128]
                same = column_mark == marks[:, 128 * half : 128 * half + 128]
                if own and q == 0 and k == 0 and half == 0:
                    row = lax.broadcasted_iota(jnp.int32, (rows, 128), 0)
                    lane = lax.broadcasted_iota(jnp.int32, (rows, 128), 1)
                    same = same & (row != lane)
                part = jnp.where(same, part, LOWEST)
                weight = jnp.exp2(part * (SCALE * LOG2E) - OFFSET * LOG2E)
                tops.append(jnp.max(part.reshape(rows // 8, 8, 128), 0))
                totals.append(jnp.sum(weight.reshape(rows // 8, 8, 128), 0))
            top = jnp.maximum(top, jnp.concatenate(tops, 1))
            total = total + jnp.concatenate(totals, 1)
        out_ref[q, 0:8] = top
        out_ref[q, 8:16] = total


def stage(queries, keys, work, own, name):
    n_query, n_key = len(queries), len(keys)
    key_rows = tuple(k.shape[0] - EXTRA for k in keys)
    pairs = PAIR * sum(key_rows[k] for each in work for k in each)
    return pl.pallas_call(
        functools.partial(stage_kernel, key_rows, n_query, work, own),
        out_shape=f32(n_query, 16, PAIR),
        in_specs=[VM] * (n_query + n_key),
        out_specs=VM,
        scratch_shapes=[pltpu.VMEM((n_key, PAIR, 128), jnp.float32)],
        compiler_params=pltpu.CompilerParams(vmem_limit_bytes=8 << 20),
        cost_estimate=pl.CostEstimate(
            flops=2 * pairs * WIDTH,
            bytes_accessed=2 * (n_query * PAIR + sum(key_rows)) * WIDTH,
            transcendentals=pairs,
        ),
        name=name,
    )(*queries, *keys)


def collect_kernel(plan, steps, *refs):
    out_ref = refs[-1]
    straight = lax.axis_index("c") == 0
    x, y = lax.axis_index("x"), lax.axis_index("y")
    for chunk, sources in enumerate(plan):
        top = functools.reduce(jnp.maximum, [refs[s][i, 0:8] for s, i in sources])
        total = functools.reduce(jnp.add, [refs[s][i, 8:16] for s, i in sources])
        top = jnp.max(top, 0, keepdims=True)
        total = jnp.sum(total, 0, keepdims=True)
        for half in range(2):
            first, second = steps[2 * chunk + half]
            to_x = lax.rem(x + jnp.where(straight, first, second) + NX, NX)
            to_y = lax.rem(y + jnp.where(straight, second, first) + NY, NY)
            place = (to_x * NY + to_y) * 2
            out_ref[pl.ds(place, 1), :] = top[:, 128 * half : 128 * half + 128]
            out_ref[pl.ds(place + 1, 1), :] = total[:, 128 * half : 128 * half + 128]


def collect(plan, steps, stages):
    return pl.pallas_call(
        functools.partial(collect_kernel, plan, steps),
        out_shape=f32(2 * NX * NY, 128),
        in_specs=[VM] * len(stages),
        out_specs=VM,
        compiler_params=SMALL,
        name="collect",
    )(*stages)


def finish_kernel(parts_ref, top_ref, soft_ref):
    top = parts_ref[0:1, :]
    total = parts_ref[1:2, :]
    for i in range(1, NX * NY):
        top = jnp.maximum(top, parts_ref[2 * i : 2 * i + 1, :])
        total = total + parts_ref[2 * i + 1 : 2 * i + 2, :]
    top_ref[...] = top * SCALE
    soft_ref[...] = jnp.log1p(total)


def finish(parts):
    return pl.pallas_call(
        finish_kernel,
        out_shape=(f32(1, ROWS), f32(1, ROWS)),
        in_specs=[VM],
        out_specs=(VM, VM),
        compiler_params=SMALL,
        name="finish",
    )(parts)


def per_device(rows, mark):
    together = lax.optimization_barrier
    mine = prepare(rows, mark)
    low = along_z(mine, 1)
    high = along_z(mine, -1)
    a = first_axis(mine, 1)
    b = first_axis(mine, -1)
    other = swap(mine)
    z0 = pack(pack_keys_kernel, "pack_keys", mine, other)
    low, high, a, b, z0 = together((low, high, a, b, z0))

    low_other = swap(low)
    high_other = swap(high)
    x1 = pack(pack_queries_kernel, "pack_near", mine, a)
    e1 = second_axis(x1, 1)
    f1 = second_axis(x1, -1)
    d = first_axis(a, 1)
    k1 = pack(pack_far_keys_kernel, "pack_far_keys", low, low_other, high, high_other)
    t2 = away(k1)
    zl = pack(pack_keys_kernel, "pack_low", low, low_other)
    zh = pack(pack_keys_kernel, "pack_high", high, high_other)
    s1 = stage([x1], [z0, zl, zh], ((0, 1, 2),), True, "stage_1")
    t2, e1, f1, d, s1, zl, zh = together((t2, e1, f1, d, s1, zl, zh))

    t3 = away(t2)
    u2 = swap(t2)
    x2 = pack(pack_queries_kernel, "pack_far", b, d)
    e2 = second_axis(x2, 1)
    f2 = second_axis(x2, -1)
    s2 = stage([x1, e1, f1], [z0, zl, zh, t2], ((3,), (0, 1, 2, 3), (0, 1, 2, 3)), False, "stage_2")
    t3, u2, e2, f2, s2 = together((t3, u2, e2, f2, s2))

    t4 = away(second_half(t3))
    u3 = swap(t3)
    g1 = second_axis(e1, 1)
    g2 = second_axis(f2, -1)
    s3 = stage(
        [x1, e1, f1, x2, e2, f2],
        [z0, zl, zh, t2, u2, t3],
        ((4, 5),) * 3 + ((0, 1, 2, 3, 4, 5),) * 3,
        False,
        "stage_3",
    )
    t4, u3, g1, g2, s3 = together((t4, u3, g1, g2, s3))

    u4 = swap(t4)
    s4 = stage(
        [x1, e1, f1, x2, e2, f2, g1, g2],
        [u3, t4, z0, zl, zh, t2, u2, t3],
        ((0, 1),) * 6 + ((0, 1, 2, 3, 4, 5, 6, 7),) * 2,
        False,
        "stage_4",
    )
    s5 = stage([x1, e1, f1, x2, e2, f2, g1, g2], [u4], ((0,),) * 8, False, "stage_5")

    near, far = ((0, 0), (-1, 0)), ((1, 0), (-2, 0))
    move = lambda pair, step: tuple((p, step) for p, _ in pair)
    chunks = [near, move(near, -1), move(near, 1), far, move(far, -1), move(far, 1), move(near, -2), move(far, 2)]
    steps = [s for pair in chunks for s in pair]
    stages = [s1, s2, s3, s4, s5]
    held = [(0,), (0, 1, 2), (0, 1, 2, 3, 4, 5), range(8), range(8)]
    plan = [[(s, q) for s in range(5) if q in held[s]] for q in range(8)]

    parts = collect(plan, steps, stages)
    parts = lax.all_to_all(parts, ("x", "y"), split_axis=0, concat_axis=0, tiled=True)
    top, soft = finish(parts)
    return top.reshape(ROWS), soft.reshape(ROWS)


def solution(mesh):
    fine = Mesh(mesh.devices.reshape(NX, NZ, NY, NC), AXES)
    return jax.shard_map(
        per_device,
        mesh=fine,
        in_specs=(P(AXES, None), P(AXES, None)),
        out_specs=(P(AXES), P(AXES)),
        check_vma=False,
    )
```

time: 121 us -> 75.7 us (0.63)
  Pallas kernels: 42.8 us -> 14.1 us
  local copies, waits for them, and re-layouts: 11.9 us -> 1.6 us
  waiting for transfers between devices: 22.3 us -> 17.3 us
    pallas_call x9 -> x13, Pallas kernels: 39.7 us -> 13.5 us  [the longest x5 13.1 us: stage(): pl.pallas_call(functools.partial(stage_kernel, key_rows, n_query, work, o...]
    unnamed x47 -> x4, local copies, waits for them, and re-layouts: 10.2 us -> 1.6 us
    ppermute x18 -> x20, waiting for transfers between devices: 22.3 us -> 17.3 us  [shift(): return lax.ppermute(value, AXES, pairs)]
    slice x1 -> x0, local copies, waits for them, and re-layouts: 1.7 us -> none  [per_device(): t4 = along_z(t3[ROWS:])]
    pallas_call x1, Pallas kernels: 1.79 us -> 0.11 us  [prepare(): pl.pallas_call(prepare_kernel, out_shape=bf16(SLOT, WIDTH), in_specs=[VM,...]
    ppermute x18 -> x20, starting transfers between devices: 30.6 us -> 30 us  [shift(): return lax.ppermute(value, AXES, pairs)]
  transfers between devices with their start and end apart: 18 -> 20, of which waited for: 7 -> 5; matrix products, arithmetic and copies ran while one was open for 2% -> 0% of each run, Pallas kernels for 24% -> 16%
where the time goes in v2:
time: 75.7 us; the launch traced here: 74.9 us
  starting transfers between devices  30 us (40%)
  waiting for transfers between devices  17.3 us (23%)
  Pallas kernels  14.1 us (19%)
  blocking collectives  11.2 us (15%)
  local copies, waits for them, and re-layouts  1.6 us (2%)
  between operations  0.78 us (1%)
    ppermute x20, starting transfers between devices, shift(): return lax.ppermute(value, AXES, pairs)  30 us
    ppermute x20, waiting for transfers between devices, shift(): return lax.ppermute(value, AXES, pairs)  17.3 us
    pallas_call x5, Pallas kernels, stage(): pl.pallas_call(functools.partial(stage_kernel, key_rows, n_query, work, o...  13.1 us
    all_to_all x1, blocking collectives, per_device(): lax.all_to_all(parts, ('x', 'y'), split_axis=0, concat_axis=0, tiled=True)  11.2 us
    unnamed x4, local copies, waits for them, and re-layouts  1.6 us
  transfers between devices with their start and end apart: 20, of which 5 were waited for; matrix products, arithmetic and copies ran while one was open for 0% of the time, Pallas kernels for 16%

profile of v2, /device:TPU:1, one launch (start us, length us, event | category | flops | bytes accessed | tf_op | source)
XLA Modules:
  0.0 74.9 jit_solution(3972620204784277990)
XLA Ops:
  0.6 0.6 copy-done.1
  1.3 0.9 %copy-done = bf16[128,1024]{1,0:T(8,128)(2,1)S(1)} copy-done((bf16[128,1024]{1,0:T(8,128)(2,1)S(1)}, bf16[128,1024]{1,0:T(8,128)(2,1)}, u32[]{:S(2)}) %copy-start) | copy-done | bytes 262168
  2.2 0.1 prepare.1.a_ref
  2.4 3.3 %collective-permute-start.4 = (bf16[144,1024]{1,0:T(8,128)(2,1)S(1)}, bf16[144,1024]{1,0:T(8,128)(2,1)S(1)}, u32[]{:S(2)}, u32[]{:S(2)}) collective-permute-start(bf16[144,1024]{1,0:T(8,128)(2,1)S(1)} %prepare.1.a_ref), channel_id=1, source_target_pairs={{0,1},{1,0},{2,3},{3,2},{4,5},{5,4},{6,7},{7,6},{8,9},{9,8},{10,11... | collective-permute-start | bytes 884744 | tf_op jit(solution)/shard_map/ppermute | solution.py:40
  5.7 3.8 %collective-permute-start.1 = (bf16[144,1024]{1,0:T(8,128)(2,1)S(1)}, bf16[144,1024]{1,0:T(8,128)(2,1)S(1)}, u32[]{:S(2)}, u32[]{:S(2)}) collective-permute-start(bf16[144,1024]{1,0:T(8,128)(2,1)S(1)} %prepare.1.a_ref), channel_id=1, source_target_pairs={{0,56},{1,57},{2,58},{3,59},{4,60},{5,61},{6,62},{7,63},{8,0},{9,1... | collective-permute-start | bytes 884744 | tf_op jit(solution)/shard_map/ppermute | solution.py:40
  9.5 1.3 %collective-permute-start.2 = (bf16[144,1024]{1,0:T(8,128)(2,1)S(1)}, bf16[144,1024]{1,0:T(8,128)(2,1)S(1)}, u32[]{:S(2)}, u32[]{:S(2)}) collective-permute-start(bf16[144,1024]{1,0:T(8,128)(2,1)S(1)} %prepare.1.a_ref), channel_id=1, source_target_pairs={{0,64},{1,3},{2,66},{3,5},{4,68},{5,7},{6,70},{7,1},{8,72},{9,11},... | collective-permute-start | bytes 884744 | tf_op jit(solution)/shard_map/ppermute | solution.py:40
  10.8 1.4 %collective-permute-start.3 = (bf16[144,1024]{1,0:T(8,128)(2,1)S(1)}, bf16[144,1024]{1,0:T(8,128)(2,1)S(1)}, u32[]{:S(2)}, u32[]{:S(2)}) collective-permute-start(bf16[144,1024]{1,0:T(8,128)(2,1)S(1)} %prepare.1.a_ref), channel_id=1, source_target_pairs={{0,192},{1,7},{2,194},{3,1},{4,196},{5,3},{6,198},{7,5},{8,200},{9... | collective-permute-start | bytes 884744 | tf_op jit(solution)/shard_map/ppermute | solution.py:40
  12.3 4.5 %collective-permute-done.low_ref.a_ref = bf16[144,1024]{1,0:T(8,128)(2,1)S(1)} collective-permute-done((bf16[144,1024]{1,0:T(8,128)(2,1)S(1)}, bf16[144,1024]{1,0:T(8,128)(2,1)S(1)}, u32[]{:S(2)}, u32[]{:S(2)}) %collective-permute-start) | collective-permute-done | bytes 294944 | tf_op jit(solution)/shard_map/ppermute | solution.py:40
  16.8 1.4 %collective-permute-start.5 = (bf16[144,1024]{1,0:T(8,128)(2,1)S(1)}, bf16[144,1024]{1,0:T(8,128)(2,1)S(1)}, u32[]{:S(2)}, u32[]{:S(2)}) collective-permute-start(bf16[144,1024]{1,0:T(8,128)(2,1)S(1)} %collective-permute-done.low_ref.a_ref), channel_id=1, source_target_pairs={{0,1},{1,0},{2,3},{3,2},{4,5},{5,4},{6,7},{7,6},{8,9},{9,8},{10,11... | collective-permute-start | bytes 884744 | tf_op jit(solution)/shard_map/ppermute | solution.py:40
  18.2 1.3 %collective-permute-start.8 = (bf16[272,1024]{1,0:T(8,128)(2,1)S(1)}, bf16[272,1024]{1,0:T(8,128)(2,1)S(1)}, u32[]{:S(2)}, u32[]{:S(2)}) collective-permute-start(bf16[272,1024]{1,0:T(8,128)(2,1)S(1)} %pack_near.1.refs_0_), channel_id=1, source_target_pairs={{0,2},{1,65},{2,4},{3,67},{4,6},{5,69},{6,0},{7,71},{8,10},{9,73},... | collective-permute-start | bytes 1671176 | tf_op jit(solution)/shard_map/ppermute | solution.py:40
  19.5 1.6 %collective-permute-start.9 = (bf16[272,1024]{1,0:T(8,128)(2,1)S(1)}, bf16[272,1024]{1,0:T(8,128)(2,1)S(1)}, u32[]{:S(2)}, u32[]{:S(2)}) collective-permute-start(bf16[272,1024]{1,0:T(8,128)(2,1)S(1)} %pack_near.1.refs_0_), channel_id=1, source_target_pairs={{0,6},{1,193},{2,0},{3,195},{4,2},{5,197},{6,4},{7,199},{8,14},{9,... | collective-permute-start | bytes 1671176 | tf_op jit(solution)/shard_map/ppermute | solution.py:40
  21.1 2.0 %collective-permute-start.7 = (bf16[272,1024]{1,0:T(8,128)(2,1)S(1)}, bf16[272,1024]{1,0:T(8,128)(2,1)S(1)}, u32[]{:S(2)}, u32[]{:S(2)}) collective-permute-start(bf16[272,1024]{1,0:T(8,128)(2,1)S(1)} %pack_far_keys.1), channel_id=1, source_target_pairs={{0,8},{1,57},{2,10},{3,59},{4,12},{5,61},{6,14},{7,63},{8,16},{9,1... | collective-permute-start | bytes 1671176 | tf_op jit(solution)/shard_map/ppermute | solution.py:40
  23.2 1.3 %collective-permute-start.10 = (bf16[144,1024]{1,0:T(8,128)(2,1)S(1)}, bf16[144,1024]{1,0:T(8,128)(2,1)S(1)}, u32[]{:S(2)}, u32[]{:S(2)}) collective-permute-start(bf16[144,1024]{1,0:T(8,128)(2,1)S(1)} %collective-permute-done.2.b_ref), channel_id=1, source_target_pairs={{0,64},{1,3},{2,66},{3,5},{4,68},{5,7},{6,70},{7,1},{8,72},{9,11},... | collective-permute-start | bytes 884744 | tf_op jit(solution)/shard_map/ppermute | solution.py:40
  24.6 0.7 stage_1.1.refs_0_
  25.3 7.1 %collective-permute-done.10.b_ref = bf16[144,1024]{1,0:T(8,128)(2,1)S(1)} collective-permute-done((bf16[144,1024]{1,0:T(8,128)(2,1)S(1)}, bf16[144,1024]{1,0:T(8,128)(2,1)S(1)}, u32[]{:S(2)}, u32[]{:S(2)}) %collective-permute-start.10) | collective-permute-done | bytes 294944 | tf_op jit(solution)/shard_map/ppermute | solution.py:40
  32.3 1.7 %collective-permute-start.11 = (bf16[272,1024]{1,0:T(8,128)(2,1)S(1)}, bf16[272,1024]{1,0:T(8,128)(2,1)S(1)}, u32[]{:S(2)}, u32[]{:S(2)}) collective-permute-start(bf16[272,1024]{1,0:T(8,128)(2,1)S(1)} %collective-permute-done.7.refs_6_.refs_9_.refs_13_), channel_id=1, source_target_pairs={{0,8},{1,57},{2,10},{3,59},{4,12},{5,61},{6,14},{7,63},{8,16},{9,1... | collective-permute-start | bytes 1671176 | tf_op jit(solution)/shard_map/ppermute | solution.py:40
  34.1 0.2 collective-permute-start.13
  34.3 2.6 %collective-permute-start.14 = (bf16[272,1024]{1,0:T(8,128)(2,1)S(1)}, bf16[272,1024]{1,0:T(8,128)(2,1)S(1)}, u32[]{:S(2)}, u32[]{:S(2)}) collective-permute-start(bf16[272,1024]{1,0:T(8,128)(2,1)S(1)} %pack_far.1.refs_3_), channel_id=1, source_target_pairs={{0,6},{1,193},{2,0},{3,195},{4,2},{5,197},{6,4},{7,199},{8,14},{9,... | collective-permute-start | bytes 1671176 | tf_op jit(solution)/shard_map/ppermute | solution.py:40
  36.8 1.7 %stage_2.1.refs_1_ = f32[3,16,256]{2,1,0:T(8,128)S(1)} custom-call(bf16[272,1024]{1,0:T(8,128)(2,1)S(1)} %pack_near.1.refs_0_, bf16[272,1024]{1,0:T(8,128)(2,1)S(1)} %collective-permute-done.8.refs_1_, bf16[272,1024]{1,0:T(8,128)(2,1)S(1)} %collective-permute-done.9.refs_2_, bf16[272,1024]{1,0:T(8,128)(2,1)S(1)} %pack_keys.1.refs_1_.refs_3_.refs_6_.refs_10_, ...), custom_call_target="tpu_custom_call" | custom-call | flops 1207959552 | bytes 3670016 | tf_op jit(solution)/shard_map/stage_2/pallas_call | solution.py:191
  38.6 2.5 %collective-permute-done.11.keys_ref.refs_11_.refs_15_ = bf16[272,1024]{1,0:T(8,128)(2,1)S(1)} collective-permute-done((bf16[272,1024]{1,0:T(8,128)(2,1)S(1)}, bf16[272,1024]{1,0:T(8,128)(2,1)S(1)}, u32[]{:S(2)}, u32[]{:S(2)}) %collective-permute-start.11) | collective-permute-done | bytes 557088 | tf_op jit(solution)/shard_map/ppermute | solution.py:40
  41.1 3.0 %collective-permute-done.13.refs_4_ = bf16[272,1024]{1,0:T(8,128)(2,1)S(1)} collective-permute-done((bf16[272,1024]{1,0:T(8,128)(2,1)S(1)}, bf16[272,1024]{1,0:T(8,128)(2,1)S(1)}, u32[]{:S(2)}, u32[]{:S(2)}) %collective-permute-start.13) | collective-permute-done | bytes 557088 | tf_op jit(solution)/shard_map/ppermute | solution.py:40
  44.1 1.4 %collective-permute-start.16 = (bf16[272,1024]{1,0:T(8,128)(2,1)S(1)}, bf16[272,1024]{1,0:T(8,128)(2,1)S(1)}, u32[]{:S(2)}, u32[]{:S(2)}) collective-permute-start(bf16[272,1024]{1,0:T(8,128)(2,1)S(1)} %collective-permute-done.11.keys_ref.refs_11_.refs_15_), channel_id=1, source_target_pairs={{0,1},{1,0},{2,3},{3,2},{4,5},{5,4},{6,7},{7,6},{8,9},{9,8},{10,11... | collective-permute-start | bytes 1671176 | tf_op jit(solution)/shard_map/ppermute | solution.py:40
  45.4 1.4 %collective-permute-start.18 = (bf16[272,1024]{1,0:T(8,128)(2,1)S(1)}, bf16[272,1024]{1,0:T(8,128)(2,1)S(1)}, u32[]{:S(2)}, u32[]{:S(2)}) collective-permute-start(bf16[272,1024]{1,0:T(8,128)(2,1)S(1)} %collective-permute-done.14.refs_5_), channel_id=1, source_target_pairs={{0,6},{1,193},{2,0},{3,195},{4,2},{5,197},{6,4},{7,199},{8,14},{9,... | collective-permute-start | bytes 1671176 | tf_op jit(solution)/shard_map/ppermute | solution.py:40
  46.8 2.7 %collective-permute-start.15 = (bf16[144,1024]{1,0:T(8,128)(2,1)S(1)}, bf16[144,1024]{1,0:T(8,128)(2,1)S(1)}, u32[]{:S(2)}, u32[]{:S(2)}) collective-permute-start(bf16[144,1024]{1,0:T(8,128)(2,1)S(1)} %second_half.1), channel_id=1, source_target_pairs={{0,8},{1,57},{2,10},{3,59},{4,12},{5,61},{6,14},{7,63},{8,16},{9,1... | collective-permute-start | bytes 884744 | tf_op jit(solution)/shard_map/ppermute | solution.py:40
  49.5 4.3 %stage_3.1.refs_2_ = f32[6,16,256]{2,1,0:T(8,128)S(1)} custom-call(bf16[272,1024]{1,0:T(8,128)(2,1)S(1)} %pack_near.1.refs_0_, bf16[272,1024]{1,0:T(8,128)(2,1)S(1)} %collective-permute-done.8.refs_1_, bf16[272,1024]{1,0:T(8,128)(2,1)S(1)} %collective-permute-done.9.refs_2_, bf16[272,1024]{1,0:T(8,128)(2,1)S(1)} %pack_far.1.refs_3_, ...), custom_call_target="tpu_custom_call" | custom-call | flops 3221225472 | bytes 6291456 | tf_op jit(solution)/shard_map/stage_3/pallas_call | solution.py:191
  53.9 0.2 collective-permute-done.18.refs_7_
  54.1 2.6 %collective-permute-start.19 = (bf16[144,1024]{1,0:T(8,128)(2,1)S(1)}, bf16[144,1024]{1,0:T(8,128)(2,1)S(1)}, u32[]{:S(2)}, u32[]{:S(2)}) collective-permute-start(bf16[144,1024]{1,0:T(8,128)(2,1)S(1)} %collective-permute-done.15.refs_9_), channel_id=1, source_target_pairs={{0,1},{1,0},{2,3},{3,2},{4,5},{5,4},{6,7},{7,6},{8,9},{9,8},{10,11... | collective-permute-start | bytes 884744 | tf_op jit(solution)/shard_map/ppermute | solution.py:40
  56.7 4.8 %stage_4.1.refs_3_ = f32[8,16,256]{2,1,0:T(8,128)S(1)} custom-call(bf16[272,1024]{1,0:T(8,128)(2,1)S(1)} %pack_near.1.refs_0_, bf16[272,1024]{1,0:T(8,128)(2,1)S(1)} %collective-permute-done.8.refs_1_, bf16[272,1024]{1,0:T(8,128)(2,1)S(1)} %collective-permute-done.9.refs_2_, bf16[272,1024]{1,0:T(8,128)(2,1)S(1)} %pack_far.1.refs_3_, ...), custom_call_target="tpu_custom_call" | custom-call | flops 3221225472 | bytes 8126464 | tf_op jit(solution)/shard_map/stage_4/pallas_call | solution.py:191
  61.5 1.6 %stage_5.1.refs_4_ = f32[8,16,256]{2,1,0:T(8,128)S(1)} custom-call(bf16[272,1024]{1,0:T(8,128)(2,1)S(1)} %pack_near.1.refs_0_, bf16[272,1024]{1,0:T(8,128)(2,1)S(1)} %collective-permute-done.8.refs_1_, bf16[272,1024]{1,0:T(8,128)(2,1)S(1)} %collective-permute-done.9.refs_2_, bf16[272,1024]{1,0:T(8,128)(2,1)S(1)} %pack_far.1.refs_3_, ...), custom_call_target="tpu_custom_call" | custom-call | flops 536870912 | bytes 4456448 | tf_op jit(solution)/shard_map/stage_5/pallas_call | solution.py:191
  63.1 0.1 collect.1
  63.2 11.2 %all_to_all.11 = f32[16,2,128]{2,1,0:T(2,128)S(1)} all-to-all(f32[16,2,128]{2,1,0:T(2,128)S(1)} %bitcast.5), channel_id=1, replica_groups=mesh['x'=4,'z'=8,'y'=4,'c'=2] {'x','y'}, dimensions={0} | all-to-all | bytes 32768 | tf_op jit(solution)/shard_map/all_to_all | solution.py:321
  74.4 0.5 finish.1
  (28 shorter events, 0.3 us)
Async XLA Ops:
  0.6 0.7 copy-start.1
  1.3 0.9 %copy-start = (bf16[128,1024]{1,0:T(8,128)(2,1)S(1)}, bf16[128,1024]{1,0:T(8,128)(2,1)}, u32[]{:S(2)}) copy-start(bf16[128,1024]{1,0:T(8,128)(2,1)} %rows_ref.1) | copy-start | bytes 786436
  2.4 9.9 %collective-permute-start.4 = (bf16[144,1024]{1,0:T(8,128)(2,1)S(1)}, bf16[144,1024]{1,0:T(8,128)(2,1)S(1)}, u32[]{:S(2)}, u32[]{:S(2)}) collective-permute-start(bf16[144,1024]{1,0:T(8,128)(2,1)S(1)} %prepare.1.a_ref), channel_id=1, source_target_pairs={{0,1},{1,0},{2,3},{3,2},{4,5},{5,4},{6,7},{7,6},{8,9},{9,8},{10,11... | collective-permute-start | bytes 884744 | tf_op jit(solution)/shard_map/ppermute | solution.py:40
  5.7 11.1 %collective-permute-start = (bf16[144,1024]{1,0:T(8,128)(2,1)S(1)}, bf16[144,1024]{1,0:T(8,128)(2,1)S(1)}, u32[]{:S(2)}, u32[]{:S(2)}) collective-permute-start(bf16[144,1024]{1,0:T(8,128)(2,1)S(1)} %prepare.1.a_ref), channel_id=1, source_target_pairs={{0,8},{1,9},{2,10},{3,11},{4,12},{5,13},{6,14},{7,15},{8,16},{9,17... | collective-permute-start | bytes 884744 | tf_op jit(solution)/shard_map/ppermute | solution.py:40
  5.7 11.1 %collective-permute-start.1 = (bf16[144,1024]{1,0:T(8,128)(2,1)S(1)}, bf16[144,1024]{1,0:T(8,128)(2,1)S(1)}, u32[]{:S(2)}, u32[]{:S(2)}) collective-permute-start(bf16[144,1024]{1,0:T(8,128)(2,1)S(1)} %prepare.1.a_ref), channel_id=1, source_target_pairs={{0,56},{1,57},{2,58},{3,59},{4,60},{5,61},{6,62},{7,63},{8,0},{9,1... | collective-permute-start | bytes 884744 | tf_op jit(solution)/shard_map/ppermute | solution.py:40
  9.5 7.3 %collective-permute-start.2 = (bf16[144,1024]{1,0:T(8,128)(2,1)S(1)}, bf16[144,1024]{1,0:T(8,128)(2,1)S(1)}, u32[]{:S(2)}, u32[]{:S(2)}) collective-permute-start(bf16[144,1024]{1,0:T(8,128)(2,1)S(1)} %prepare.1.a_ref), channel_id=1, source_target_pairs={{0,64},{1,3},{2,66},{3,5},{4,68},{5,7},{6,70},{7,1},{8,72},{9,11},... | collective-permute-start | bytes 884744 | tf_op jit(solution)/shard_map/ppermute | solution.py:40
  10.8 6.0 %collective-permute-start.3 = (bf16[144,1024]{1,0:T(8,128)(2,1)S(1)}, bf16[144,1024]{1,0:T(8,128)(2,1)S(1)}, u32[]{:S(2)}, u32[]{:S(2)}) collective-permute-start(bf16[144,1024]{1,0:T(8,128)(2,1)S(1)} %prepare.1.a_ref), channel_id=1, source_target_pairs={{0,192},{1,7},{2,194},{3,1},{4,196},{5,3},{6,198},{7,5},{8,200},{9... | collective-permute-start | bytes 884744 | tf_op jit(solution)/shard_map/ppermute | solution.py:40
  16.8 4.3 %collective-permute-start.5 = (bf16[144,1024]{1,0:T(8,128)(2,1)S(1)}, bf16[144,1024]{1,0:T(8,128)(2,1)S(1)}, u32[]{:S(2)}, u32[]{:S(2)}) collective-permute-start(bf16[144,1024]{1,0:T(8,128)(2,1)S(1)} %collective-permute-done.low_ref.a_ref), channel_id=1, source_target_pairs={{0,1},{1,0},{2,3},{3,2},{4,5},{5,4},{6,7},{7,6},{8,9},{9,8},{10,11... | collective-permute-start | bytes 884744 | tf_op jit(solution)/shard_map/ppermute | solution.py:40
  18.2 2.9 %collective-permute-start.6 = (bf16[144,1024]{1,0:T(8,128)(2,1)S(1)}, bf16[144,1024]{1,0:T(8,128)(2,1)S(1)}, u32[]{:S(2)}, u32[]{:S(2)}) collective-permute-start(bf16[144,1024]{1,0:T(8,128)(2,1)S(1)} %collective-permute-done.1.high_ref.a_ref), channel_id=1, source_target_pairs={{0,1},{1,0},{2,3},{3,2},{4,5},{5,4},{6,7},{7,6},{8,9},{9,8},{10,11... | collective-permute-start | bytes 884744 | tf_op jit(solution)/shard_map/ppermute | solution.py:40
  18.2 14.1 %collective-permute-start.8 = (bf16[272,1024]{1,0:T(8,128)(2,1)S(1)}, bf16[272,1024]{1,0:T(8,128)(2,1)S(1)}, u32[]{:S(2)}, u32[]{:S(2)}) collective-permute-start(bf16[272,1024]{1,0:T(8,128)(2,1)S(1)} %pack_near.1.refs_0_), channel_id=1, source_target_pairs={{0,2},{1,65},{2,4},{3,67},{4,6},{5,69},{6,0},{7,71},{8,10},{9,73},... | collective-permute-start | bytes 1671176 | tf_op jit(solution)/shard_map/ppermute | solution.py:40
  19.5 12.8 %collective-permute-start.9 = (bf16[272,1024]{1,0:T(8,128)(2,1)S(1)}, bf16[272,1024]{1,0:T(8,128)(2,1)S(1)}, u32[]{:S(2)}, u32[]{:S(2)}) collective-permute-start(bf16[272,1024]{1,0:T(8,128)(2,1)S(1)} %pack_near.1.refs_0_), channel_id=1, source_target_pairs={{0,6},{1,193},{2,0},{3,195},{4,2},{5,197},{6,4},{7,199},{8,14},{9,... | collective-permute-start | bytes 1671176 | tf_op jit(solution)/shard_map/ppermute | solution.py:40
  21.1 11.2 %collective-permute-start.7 = (bf16[272,1024]{1,0:T(8,128)(2,1)S(1)}, bf16[272,1024]{1,0:T(8,128)(2,1)S(1)}, u32[]{:S(2)}, u32[]{:S(2)}) collective-permute-start(bf16[272,1024]{1,0:T(8,128)(2,1)S(1)} %pack_far_keys.1), channel_id=1, source_target_pairs={{0,8},{1,57},{2,10},{3,59},{4,12},{5,61},{6,14},{7,63},{8,16},{9,1... | collective-permute-start | bytes 1671176 | tf_op jit(solution)/shard_map/ppermute | solution.py:40
  23.2 9.2 %collective-permute-start.10 = (bf16[144,1024]{1,0:T(8,128)(2,1)S(1)}, bf16[144,1024]{1,0:T(8,128)(2,1)S(1)}, u32[]{:S(2)}, u32[]{:S(2)}) collective-permute-start(bf16[144,1024]{1,0:T(8,128)(2,1)S(1)} %collective-permute-done.2.b_ref), channel_id=1, source_target_pairs={{0,64},{1,3},{2,66},{3,5},{4,68},{5,7},{6,70},{7,1},{8,72},{9,11},... | collective-permute-start | bytes 884744 | tf_op jit(solution)/shard_map/ppermute | solution.py:40
  32.3 8.8 %collective-permute-start.11 = (bf16[272,1024]{1,0:T(8,128)(2,1)S(1)}, bf16[272,1024]{1,0:T(8,128)(2,1)S(1)}, u32[]{:S(2)}, u32[]{:S(2)}) collective-permute-start(bf16[272,1024]{1,0:T(8,128)(2,1)S(1)} %collective-permute-done.7.refs_6_.refs_9_.refs_13_), channel_id=1, source_target_pairs={{0,8},{1,57},{2,10},{3,59},{4,12},{5,61},{6,14},{7,63},{8,16},{9,1... | collective-permute-start | bytes 1671176 | tf_op jit(solution)/shard_map/ppermute | solution.py:40
  34.0 7.1 %collective-permute-start.12 = (bf16[272,1024]{1,0:T(8,128)(2,1)S(1)}, bf16[272,1024]{1,0:T(8,128)(2,1)S(1)}, u32[]{:S(2)}, u32[]{:S(2)}) collective-permute-start(bf16[272,1024]{1,0:T(8,128)(2,1)S(1)} %collective-permute-done.7.refs_6_.refs_9_.refs_13_), channel_id=1, source_target_pairs={{0,1},{1,0},{2,3},{3,2},{4,5},{5,4},{6,7},{7,6},{8,9},{9,8},{10,11... | collective-permute-start | bytes 1671176 | tf_op jit(solution)/shard_map/ppermute | solution.py:40
  34.1 10.0 %collective-permute-start.13 = (bf16[272,1024]{1,0:T(8,128)(2,1)S(1)}, bf16[272,1024]{1,0:T(8,128)(2,1)S(1)}, u32[]{:S(2)}, u32[]{:S(2)}) collective-permute-start(bf16[272,1024]{1,0:T(8,128)(2,1)S(1)} %pack_far.1.refs_3_), channel_id=1, source_target_pairs={{0,2},{1,65},{2,4},{3,67},{4,6},{5,69},{6,0},{7,71},{8,10},{9,73},... | collective-permute-start | bytes 1671176 | tf_op jit(solution)/shard_map/ppermute | solution.py:40
  34.3 9.8 %collective-permute-start.14 = (bf16[272,1024]{1,0:T(8,128)(2,1)S(1)}, bf16[272,1024]{1,0:T(8,128)(2,1)S(1)}, u32[]{:S(2)}, u32[]{:S(2)}) collective-permute-start(bf16[272,1024]{1,0:T(8,128)(2,1)S(1)} %pack_far.1.refs_3_), channel_id=1, source_target_pairs={{0,6},{1,193},{2,0},{3,195},{4,2},{5,197},{6,4},{7,199},{8,14},{9,... | collective-permute-start | bytes 1671176 | tf_op jit(solution)/shard_map/ppermute | solution.py:40
  36.8 17.0 %collective-permute-start.17 = (bf16[272,1024]{1,0:T(8,128)(2,1)S(1)}, bf16[272,1024]{1,0:T(8,128)(2,1)S(1)}, u32[]{:S(2)}, u32[]{:S(2)}) collective-permute-start(bf16[272,1024]{1,0:T(8,128)(2,1)S(1)} %collective-permute-done.8.refs_1_), channel_id=1, source_target_pairs={{0,2},{1,65},{2,4},{3,67},{4,6},{5,69},{6,0},{7,71},{8,10},{9,73},... | collective-permute-start | bytes 1671176 | tf_op jit(solution)/shard_map/ppermute | solution.py:40
  44.1 9.8 %collective-permute-start.16 = (bf16[272,1024]{1,0:T(8,128)(2,1)S(1)}, bf16[272,1024]{1,0:T(8,128)(2,1)S(1)}, u32[]{:S(2)}, u32[]{:S(2)}) collective-permute-start(bf16[272,1024]{1,0:T(8,128)(2,1)S(1)} %collective-permute-done.11.keys_ref.refs_11_.refs_15_), channel_id=1, source_target_pairs={{0,1},{1,0},{2,3},{3,2},{4,5},{5,4},{6,7},{7,6},{8,9},{9,8},{10,11... | collective-permute-start | bytes 1671176 | tf_op jit(solution)/shard_map/ppermute | solution.py:40
  45.4 8.7 %collective-permute-start.18 = (bf16[272,1024]{1,0:T(8,128)(2,1)S(1)}, bf16[272,1024]{1,0:T(8,128)(2,1)S(1)}, u32[]{:S(2)}, u32[]{:S(2)}) collective-permute-start(bf16[272,1024]{1,0:T(8,128)(2,1)S(1)} %collective-permute-done.14.refs_5_), channel_id=1, source_target_pairs={{0,6},{1,193},{2,0},{3,195},{4,2},{5,197},{6,4},{7,199},{8,14},{9,... | collective-permute-start | bytes 1671176 | tf_op jit(solution)/shard_map/ppermute | solution.py:40
  46.8 7.0 %collective-permute-start.15 = (bf16[144,1024]{1,0:T(8,128)(2,1)S(1)}, bf16[144,1024]{1,0:T(8,128)(2,1)S(1)}, u32[]{:S(2)}, u32[]{:S(2)}) collective-permute-start(bf16[144,1024]{1,0:T(8,128)(2,1)S(1)} %second_half.1), channel_id=1, source_target_pairs={{0,8},{1,57},{2,10},{3,59},{4,12},{5,61},{6,14},{7,63},{8,16},{9,1... | collective-permute-start | bytes 884744 | tf_op jit(solution)/shard_map/ppermute | solution.py:40
  54.1 7.4 %collective-permute-start.19 = (bf16[144,1024]{1,0:T(8,128)(2,1)S(1)}, bf16[144,1024]{1,0:T(8,128)(2,1)S(1)}, u32[]{:S(2)}, u32[]{:S(2)}) collective-permute-start(bf16[144,1024]{1,0:T(8,128)(2,1)S(1)} %collective-permute-done.15.refs_9_), channel_id=1, source_target_pairs={{0,1},{1,0},{2,3},{3,2},{4,5},{5,4},{6,7},{7,6},{8,9},{9,8},{10,11... | collective-permute-start | bytes 884744 | tf_op jit(solution)/shard_map/ppermute | solution.py:40

commit v3 on v2

--- a/solution.py
+++ b/solution.py
@@ -48,8 +48,8 @@
     return shift(value, lambda c: (0, step, 0, 0))
 
 
-def away(value):
-    return shift(value, lambda c: (0, 1, 0, 0) if c == 0 else (0, -1, 0, 0))
+def away(value, step=1):
+    return shift(value, lambda c: (0, step, 0, 0) if c == 0 else (0, -step, 0, 0))
 
 
 def first_axis(value, step):
@@ -68,8 +68,9 @@
     return jax.ShapeDtypeStruct(shape, jnp.float32)
 
 
-def prepare_kernel(rows_ref, mark_ref, out_ref):
-    out_ref[0:ROWS, :] = rows_ref[...]
+def prepare_kernel(rows_ref, mark_ref, out_ref, sem):
+    copy = pltpu.make_async_copy(rows_ref, out_ref.at[pl.ds(0, ROWS)], sem)
+    copy.start()
     along = jnp.broadcast_to(mark_ref[...].astype(jnp.float32), (ROWS, 128))
     wide = along.T
     lane = lax.broadcasted_iota(jnp.int32, (16, 128), 1)
@@ -78,14 +79,16 @@
         out_ref[ROWS:SLOT, 64 * g : 64 * g + 128] = both.astype(jnp.bfloat16)
     out_ref[ROWS:SLOT, 512:640] = along[0:16].astype(jnp.bfloat16)
     out_ref[ROWS:SLOT, 640:] = jnp.zeros((16, WIDTH - 640), jnp.bfloat16)
+    copy.wait()
 
 
 def prepare(rows, mark):
     return pl.pallas_call(
         prepare_kernel,
         out_shape=bf16(SLOT, WIDTH),
-        in_specs=[VM, VM],
+        in_specs=[pl.BlockSpec(memory_space=pl.ANY), VM],
         out_specs=VM,
+        scratch_shapes=[pltpu.SemaphoreType.DMA],
         compiler_params=SMALL,
         name="prepare",
     )(rows, mark.reshape(1, ROWS))
@@ -98,43 +101,25 @@
     out_ref[PAIR:, 512:] = b_ref[ROWS:, 0:512]
 
 
-def pack_far_keys_kernel(low_ref, low_other_ref, high_ref, high_other_ref, out_ref):
-    @pl.when(lax.axis_index("c") == 0)
-    def _():
-        pack_keys_kernel(low_ref, low_other_ref, out_ref)
-
-    @pl.when(lax.axis_index("c") != 0)
-    def _():
-        pack_keys_kernel(high_ref, high_other_ref, out_ref)
-
-
-def second_half_kernel(keys_ref, out_ref):
-    out_ref[...] = keys_ref[ROWS:]
-
-
-def second_half(keys):
-    return pl.pallas_call(
-        second_half_kernel,
-        out_shape=bf16(SLOT, WIDTH),
-        in_specs=[VM],
-        out_specs=VM,
-        compiler_params=SMALL,
-        name="second_half",
-    )(keys)
-
-
-def pack_queries_kernel(a_ref, b_ref, out_ref):
-    out_ref[0:ROWS] = a_ref[0:ROWS]
-    out_ref[ROWS:PAIR] = b_ref[0:ROWS]
-    out_ref[PAIR:, 0:128] = a_ref[ROWS:, 512:640]
-    out_ref[PAIR:, 128:256] = b_ref[ROWS:, 512:640]
-    out_ref[PAIR:, 256:] = jnp.zeros((EXTRA, WIDTH - 256), jnp.bfloat16)
-
-
-def pack(kernel, name, *parts):
+def pack_queries_kernel(*refs):
+    out_ref = refs[-1]
+    last = ROWS * (len(refs) - 1)
+    for i, ref in enumerate(refs[:-1]):
+        out_ref[ROWS * i : ROWS * (i + 1)] = ref[0:ROWS]
+        out_ref[last:, 128 * i : 128 * i + 128] = ref[ROWS:, 512:640]
+    out_ref[last:, last:] = jnp.zeros((EXTRA, WIDTH - last), jnp.bfloat16)
+
+
+def half_queries_kernel(half, whole_ref, out_ref):
+    out_ref[0:PAIR] = whole_ref[PAIR * half : PAIR * half + PAIR]
+    out_ref[PAIR:, 0:PAIR] = whole_ref[2 * PAIR :, PAIR * half : PAIR * half + PAIR]
+    out_ref[PAIR:, PAIR:] = jnp.zeros((EXTRA, WIDTH - PAIR), jnp.bfloat16)
+
+
+def pack(kernel, name, rows, *parts):
     return pl.pallas_call(
         kernel,
-        out_shape=bf16(CHUNK, WIDTH),
+        out_shape=bf16(rows + EXTRA, WIDTH),
         in_specs=[VM] * len(parts),
         out_specs=VM,
         compiler_params=SMALL,
@@ -142,8 +127,8 @@
     )(*parts)
 
 
-def stage_kernel(key_rows, n_query, work, own, *refs):
-    n_key = len(key_rows)
+def stage_kernel(key_rows, chunk_counts, work, own, *refs):
+    n_key, n_query = len(key_rows), len(chunk_counts)
     q_refs, k_refs = refs[:n_query], refs[n_query : n_query + n_key]
     out_ref, column = refs[n_query + n_key :]
 
@@ -153,15 +138,17 @@
             values = k_refs[i][rows : rows + EXTRA, lane : lane + 1].astype(jnp.float32)
             column[i, 16 * g : 16 * g + 16, :] = jnp.broadcast_to(values, (16, 128))
 
-    for q, keys in enumerate(work):
-        marks = q_refs[q][PAIR:CHUNK, 0:PAIR].astype(jnp.float32)[0:1]
+    places = [(i, c) for i, count in enumerate(chunk_counts) for c in range(count)]
+    for q, ((i, c), keys) in enumerate(zip(places, work, strict=True)):
+        rows = PAIR * chunk_counts[i]
+        marks = q_refs[i][rows : rows + EXTRA, PAIR * c : PAIR * c + PAIR].astype(jnp.float32)[0:1]
         top = jnp.full((8, PAIR), LOWEST, jnp.float32)
         total = jnp.zeros((8, PAIR), jnp.float32)
         for k in keys:
             rows = key_rows[k]
             score = lax.dot_general(
                 k_refs[k][0:rows, :],
-                q_refs[q][0:PAIR, :],
+                q_refs[i][PAIR * c : PAIR * c + PAIR, :],
                 (((1,), (1,)), ((), ())),
                 preferred_element_type=jnp.float32,
             )
@@ -184,22 +171,18 @@
         out_ref[q, 8:16] = total
 
 
-def stage(queries, keys, work, own, name):
-    n_query, n_key = len(queries), len(keys)
+def stage(queries, keys, work, own, name, cost=0):
+    n_key = len(keys)
     key_rows = tuple(k.shape[0] - EXTRA for k in keys)
-    pairs = PAIR * sum(key_rows[k] for each in work for k in each)
-    return pl.pallas_call(
-        functools.partial(stage_kernel, key_rows, n_query, work, own),
-        out_shape=f32(n_query, 16, PAIR),
-        in_specs=[VM] * (n_query + n_key),
+    chunk_counts = tuple((q.shape[0] - EXTRA) // PAIR for q in queries)
+    return pl.pallas_call(
+        functools.partial(stage_kernel, key_rows, chunk_counts, work, own),
+        out_shape=f32(sum(chunk_counts), 16, PAIR),
+        in_specs=[VM] * (len(queries) + n_key),
         out_specs=VM,
         scratch_shapes=[pltpu.VMEM((n_key, PAIR, 128), jnp.float32)],
         compiler_params=pltpu.CompilerParams(vmem_limit_bytes=8 << 20),
-        cost_estimate=pl.CostEstimate(
-            flops=2 * pairs * WIDTH,
-            bytes_accessed=2 * (n_query * PAIR + sum(key_rows)) * WIDTH,
-            transcendentals=pairs,
-        ),
+        cost_estimate=pl.CostEstimate(flops=cost, bytes_accessed=0, transcendentals=0),
         name=name,
     )(*queries, *keys)
 
@@ -257,65 +240,53 @@
 def per_device(rows, mark):
     together = lax.optimization_barrier
     mine = prepare(rows, mark)
-    low = along_z(mine, 1)
-    high = along_z(mine, -1)
     a = first_axis(mine, 1)
     b = first_axis(mine, -1)
     other = swap(mine)
-    z0 = pack(pack_keys_kernel, "pack_keys", mine, other)
-    low, high, a, b, z0 = together((low, high, a, b, z0))
-
-    low_other = swap(low)
-    high_other = swap(high)
-    x1 = pack(pack_queries_kernel, "pack_near", mine, a)
-    e1 = second_axis(x1, 1)
-    f1 = second_axis(x1, -1)
-    d = first_axis(a, 1)
-    k1 = pack(pack_far_keys_kernel, "pack_far_keys", low, low_other, high, high_other)
-    t2 = away(k1)
-    zl = pack(pack_keys_kernel, "pack_low", low, low_other)
-    zh = pack(pack_keys_kernel, "pack_high", high, high_other)
-    s1 = stage([x1], [z0, zl, zh], ((0, 1, 2),), True, "stage_1")
-    t2, e1, f1, d, s1, zl, zh = together((t2, e1, f1, d, s1, zl, zh))
+    z0 = pack(pack_keys_kernel, "pack_keys", PAIR, mine, other)
+    t1 = away(z0)
+    d = first_axis(mine, 2)
+    t1, a, b, d = together((t1, a, b, d))
+
+    t2 = away(t1)
+    x = pack(pack_queries_kernel, "pack_line", 2 * PAIR, mine, a, b, d)
+    e = second_axis(x, 1)
+    f = second_axis(x, -1)
+    s1 = stage([x], [z0, t1], ((0, 1),) * 2, True, "stage_1")
+    t2, s1 = together((t2, s1))
 
     t3 = away(t2)
+    u1 = swap(t1)
     u2 = swap(t2)
-    x2 = pack(pack_queries_kernel, "pack_far", b, d)
-    e2 = second_axis(x2, 1)
-    f2 = second_axis(x2, -1)
-    s2 = stage([x1, e1, f1], [z0, zl, zh, t2], ((3,), (0, 1, 2, 3), (0, 1, 2, 3)), False, "stage_2")
-    t3, u2, e2, f2, s2 = together((t3, u2, e2, f2, s2))
-
-    t4 = away(second_half(t3))
+    s2 = stage([x], [t2], ((0,),) * 2, False, "stage_2")
+    e, f, u1, u2, s2 = together((e, f, u1, u2, s2))
+
+    g1 = second_axis(pack(functools.partial(half_queries_kernel, 0), "half_near", PAIR, e), 1)
+    g2 = second_axis(pack(functools.partial(half_queries_kernel, 1), "half_far", PAIR, f), -1)
+    s3 = stage(
+        [x, e, f], [u1, u2, z0, t1, t2], ((0, 1),) * 2 + ((0, 1, 2, 3, 4),) * 4, False, "stage_3"
+    )
+    t4 = away(t3)
     u3 = swap(t3)
-    g1 = second_axis(e1, 1)
-    g2 = second_axis(f2, -1)
-    s3 = stage(
-        [x1, e1, f1, x2, e2, f2],
-        [z0, zl, zh, t2, u2, t3],
-        ((4, 5),) * 3 + ((0, 1, 2, 3, 4, 5),) * 3,
+    s4 = stage([x, e, f], [t3], ((0,),) * 6, False, "stage_4")
+    g1, g2, u3, s3, s4 = together((g1, g2, u3, s3, s4))
+
+    s5 = stage(
+        [x, e, f, g1, g2],
+        [u3, z0, t1, u1, t2, u2, t3],
+        ((0,),) * 6 + ((0, 1, 2, 3, 4, 5, 6),) * 2,
         False,
-        "stage_3",
+        "stage_5",
     )
-    t4, u3, g1, g2, s3 = together((t4, u3, g1, g2, s3))
-
-    u4 = swap(t4)
-    s4 = stage(
-        [x1, e1, f1, x2, e2, f2, g1, g2],
-        [u3, t4, z0, zl, zh, t2, u2, t3],
-        ((0, 1),) * 6 + ((0, 1, 2, 3, 4, 5, 6, 7),) * 2,
-        False,
-        "stage_4",
-    )
-    s5 = stage([x1, e1, f1, x2, e2, f2, g1, g2], [u4], ((0,),) * 8, False, "stage_5")
+    t4, s5 = together((t4, s5))
+    s6 = stage([x, e, f, g1, g2], [t4], ((0,),) * 8, False, "stage_6")
 
     near, far = ((0, 0), (-1, 0)), ((1, 0), (-2, 0))
     move = lambda pair, step: tuple((p, step) for p, _ in pair)
-    chunks = [near, move(near, -1), move(near, 1), far, move(far, -1), move(far, 1), move(near, -2), move(far, 2)]
+    chunks = [near, far, move(near, -1), move(far, -1), move(near, 1), move(far, 1), move(near, -2), move(far, 2)]
     steps = [s for pair in chunks for s in pair]
-    stages = [s1, s2, s3, s4, s5]
-    held = [(0,), (0, 1, 2), (0, 1, 2, 3, 4, 5), range(8), range(8)]
-    plan = [[(s, q) for s in range(5) if q in held[s]] for q in range(8)]
+    stages = [s1, s2, s3, s4, s5, s6]
+    plan = [[(i, q) for i, s in enumerate(stages) if q < s.shape[0]] for q in range(8)]
 
     parts = collect(plan, steps, stages)
     parts = lax.all_to_all(parts, ("x", "y"), split_axis=0, concat_axis=0, tiled=True)

time: 75.7 us -> 68.9 us (0.910)
  the two profiles are of different devices: /device:TPU:1 before, /device:TPU:64 now
where the time goes in v3:
time: 68.9 us; the launch traced here: 68.7 us
  starting transfers between devices  20.6 us (30%)
  waiting for transfers between devices  19.5 us (28%)
  blocking collectives  13.2 us (19%)
  Pallas kernels  13 us (19%)
  local copies, waits for them, and re-layouts  1.6 us (2%)
  between operations  0.76 us (1%)
    ppermute x15, starting transfers between devices, shift(): return lax.ppermute(value, AXES, pairs)  20.6 us
    ppermute x15, waiting for transfers between devices, shift(): return lax.ppermute(value, AXES, pairs)  19.5 us
    all_to_all x1, blocking collectives, per_device(): lax.all_to_all(parts, ('x', 'y'), split_axis=0, concat_axis=0, tiled=True)  13.2 us
    pallas_call x6, Pallas kernels, stage(): pl.pallas_call(functools.partial(stage_kernel, key_rows, chunk_counts, wo...  12.1 us
    unnamed x4, local copies, waits for them, and re-layouts  1.6 us
  transfers between devices with their start and end apart: 15, of which 9 were waited for; matrix products, arithmetic and copies ran while one was open for 0% of the time, Pallas kernels for 16%

profile of v3, /device:TPU:64, one launch (start us, length us, event | category | flops | bytes accessed | tf_op | source)
XLA Modules:
  0.0 68.7 jit_solution(2901511619869196589)
XLA Ops:
  0.6 0.9 %copy-done = bf16[128,1024]{1,0:T(8,128)(2,1)S(1)} copy-done((bf16[128,1024]{1,0:T(8,128)(2,1)S(1)}, bf16[128,1024]{1,0:T(8,128)(2,1)}, u32[]{:S(2)}) %copy-start) | copy-done | bytes 262168
  1.6 0.7 copy-done.1
  2.2 0.1 prepare.1.a_ref.refs_0_
  2.5 1.6 %collective-permute-done.b_ref = bf16[144,1024]{1,0:T(8,128)(2,1)S(1)} collective-permute-done((bf16[144,1024]{1,0:T(8,128)(2,1)S(1)}, bf16[144,1024]{1,0:T(8,128)(2,1)S(1)}, u32[]{:S(2)}, u32[]{:S(2)}) %collective-permute-start) | collective-permute-done | bytes 294944 | tf_op jit(solution)/shard_map/ppermute | solution.py:40
  4.1 2.0 %collective-permute-start.1 = (bf16[272,1024]{1,0:T(8,128)(2,1)S(1)}, bf16[272,1024]{1,0:T(8,128)(2,1)S(1)}, u32[]{:S(2)}, u32[]{:S(2)}) collective-permute-start(bf16[272,1024]{1,0:T(8,128)(2,1)S(1)} %pack_keys.1.refs_1_.refs_5_.refs_6_), channel_id=1, source_target_pairs={{0,8},{1,57},{2,10},{3,59},{4,12},{5,61},{6,14},{7,63},{8,16},{9,1... | collective-permute-start | bytes 1671176 | tf_op jit(solution)/shard_map/ppermute | solution.py:40
  6.1 1.5 %collective-permute-start.2 = (bf16[144,1024]{1,0:T(8,128)(2,1)S(1)}, bf16[144,1024]{1,0:T(8,128)(2,1)S(1)}, u32[]{:S(2)}, u32[]{:S(2)}) collective-permute-start(bf16[144,1024]{1,0:T(8,128)(2,1)S(1)} %prepare.1.a_ref.refs_0_), channel_id=1, source_target_pairs={{0,64},{1,3},{2,66},{3,5},{4,68},{5,7},{6,70},{7,1},{8,72},{9,11},... | collective-permute-start | bytes 884744 | tf_op jit(solution)/shard_map/ppermute | solution.py:40
  7.6 1.7 %collective-permute-start.3 = (bf16[144,1024]{1,0:T(8,128)(2,1)S(1)}, bf16[144,1024]{1,0:T(8,128)(2,1)S(1)}, u32[]{:S(2)}, u32[]{:S(2)}) collective-permute-start(bf16[144,1024]{1,0:T(8,128)(2,1)S(1)} %prepare.1.a_ref.refs_0_), channel_id=1, source_target_pairs={{0,192},{1,7},{2,194},{3,1},{4,196},{5,3},{6,198},{7,5},{8,200},{9... | collective-permute-start | bytes 884744 | tf_op jit(solution)/shard_map/ppermute | solution.py:40
  9.3 1.8 %collective-permute-start.4 = (bf16[144,1024]{1,0:T(8,128)(2,1)S(1)}, bf16[144,1024]{1,0:T(8,128)(2,1)S(1)}, u32[]{:S(2)}, u32[]{:S(2)}) collective-permute-start(bf16[144,1024]{1,0:T(8,128)(2,1)S(1)} %prepare.1.a_ref.refs_0_), channel_id=1, source_target_pairs={{0,128},{1,5},{2,130},{3,7},{4,132},{5,1},{6,134},{7,3},{8,136},{9... | collective-permute-start | bytes 884744 | tf_op jit(solution)/shard_map/ppermute | solution.py:40
  11.1 2.9 %collective-permute-done.2.refs_1_ = bf16[144,1024]{1,0:T(8,128)(2,1)S(1)} collective-permute-done((bf16[144,1024]{1,0:T(8,128)(2,1)S(1)}, bf16[144,1024]{1,0:T(8,128)(2,1)S(1)}, u32[]{:S(2)}, u32[]{:S(2)}) %collective-permute-start.2) | collective-permute-done | bytes 294944 | tf_op jit(solution)/shard_map/ppermute | solution.py:40
  14.0 2.7 %collective-permute-done.3.refs_2_ = bf16[144,1024]{1,0:T(8,128)(2,1)S(1)} collective-permute-done((bf16[144,1024]{1,0:T(8,128)(2,1)S(1)}, bf16[144,1024]{1,0:T(8,128)(2,1)S(1)}, u32[]{:S(2)}, u32[]{:S(2)}) %collective-permute-start.3) | collective-permute-done | bytes 294944 | tf_op jit(solution)/shard_map/ppermute | solution.py:40
  16.7 1.4 %collective-permute-done.4.refs_3_ = bf16[144,1024]{1,0:T(8,128)(2,1)S(1)} collective-permute-done((bf16[144,1024]{1,0:T(8,128)(2,1)S(1)}, bf16[144,1024]{1,0:T(8,128)(2,1)S(1)}, u32[]{:S(2)}, u32[]{:S(2)}) %collective-permute-start.4) | collective-permute-done | bytes 294944 | tf_op jit(solution)/shard_map/ppermute | solution.py:40
  18.2 3.1 %collective-permute-start.5 = (bf16[272,1024]{1,0:T(8,128)(2,1)S(1)}, bf16[272,1024]{1,0:T(8,128)(2,1)S(1)}, u32[]{:S(2)}, u32[]{:S(2)}) collective-permute-start(bf16[272,1024]{1,0:T(8,128)(2,1)S(1)} %collective-permute-done.1.refs_2_.refs_6_.refs_7_), channel_id=1, source_target_pairs={{0,8},{1,57},{2,10},{3,59},{4,12},{5,61},{6,14},{7,63},{8,16},{9,1... | collective-permute-start | bytes 1671176 | tf_op jit(solution)/shard_map/ppermute | solution.py:40
  21.4 1.7 %collective-permute-start.6 = (bf16[528,1024]{1,0:T(8,128)(2,1)S(1)}, bf16[528,1024]{1,0:T(8,128)(2,1)S(1)}, u32[]{:S(2)}, u32[]{:S(2)}) collective-permute-start(bf16[528,1024]{1,0:T(8,128)(2,1)S(1)} %pack_line.1.refs_0_), channel_id=1, source_target_pairs={{0,2},{1,65},{2,4},{3,67},{4,6},{5,69},{6,0},{7,71},{8,10},{9,73},... | collective-permute-start | bytes 3244040 | tf_op jit(solution)/shard_map/ppermute | solution.py:40
  23.0 1.7 %collective-permute-start.7 = (bf16[528,1024]{1,0:T(8,128)(2,1)S(1)}, bf16[528,1024]{1,0:T(8,128)(2,1)S(1)}, u32[]{:S(2)}, u32[]{:S(2)}) collective-permute-start(bf16[528,1024]{1,0:T(8,128)(2,1)S(1)} %pack_line.1.refs_0_), channel_id=1, source_target_pairs={{0,6},{1,193},{2,0},{3,195},{4,2},{5,197},{6,4},{7,199},{8,14},{9,... | collective-permute-start | bytes 3244040 | tf_op jit(solution)/shard_map/ppermute | solution.py:40
  24.7 0.9 %stage_1.1.refs_0_ = f32[2,16,256]{2,1,0:T(8,128)S(1)} custom-call(bf16[528,1024]{1,0:T(8,128)(2,1)S(1)} %pack_line.1.refs_0_, bf16[272,1024]{1,0:T(8,128)(2,1)S(1)} %pack_keys.1.refs_1_.refs_5_.refs_6_, bf16[272,1024]{1,0:T(8,128)(2,1)S(1)} %collective-permute-done.1.refs_2_.refs_6_.refs_7_), custom_call_target="tpu_custom_call" | custom-call | tf_op jit(solution)/shard_map/stage_1/pallas_call | solution.py:178
  25.7 2.7 %collective-permute-done.5.refs_1_.refs_7_.refs_9_ = bf16[272,1024]{1,0:T(8,128)(2,1)S(1)} collective-permute-done((bf16[272,1024]{1,0:T(8,128)(2,1)S(1)}, bf16[272,1024]{1,0:T(8,128)(2,1)S(1)}, u32[]{:S(2)}, u32[]{:S(2)}) %collective-permute-start.5) | collective-permute-done | bytes 557088 | tf_op jit(solution)/shard_map/ppermute | solution.py:40
  28.3 2.5 %collective-permute-start.12 = (bf16[272,1024]{1,0:T(8,128)(2,1)S(1)}, bf16[272,1024]{1,0:T(8,128)(2,1)S(1)}, u32[]{:S(2)}, u32[]{:S(2)}) collective-permute-start(bf16[272,1024]{1,0:T(8,128)(2,1)S(1)} %collective-permute-done.5.refs_1_.refs_7_.refs_9_), channel_id=1, source_target_pairs={{0,8},{1,57},{2,10},{3,59},{4,12},{5,61},{6,14},{7,63},{8,16},{9,1... | collective-permute-start | bytes 1671176 | tf_op jit(solution)/shard_map/ppermute | solution.py:40
  30.8 0.5 stage_2.1.refs_1_
  31.4 6.4 %collective-permute-done.6.whole_ref.refs_1_ = bf16[528,1024]{1,0:T(8,128)(2,1)S(1)} collective-permute-done((bf16[528,1024]{1,0:T(8,128)(2,1)S(1)}, bf16[528,1024]{1,0:T(8,128)(2,1)S(1)}, u32[]{:S(2)}, u32[]{:S(2)}) %collective-permute-start.6) | collective-permute-done | bytes 1081376 | tf_op jit(solution)/shard_map/ppermute | solution.py:40
  37.8 0.4 collective-permute-done.7.whole_ref.refs_2_
  38.2 1.8 %collective-permute-start.10 = (bf16[272,1024]{1,0:T(8,128)(2,1)S(1)}, bf16[272,1024]{1,0:T(8,128)(2,1)S(1)}, u32[]{:S(2)}, u32[]{:S(2)}) collective-permute-start(bf16[272,1024]{1,0:T(8,128)(2,1)S(1)} %half_near.1), channel_id=1, source_target_pairs={{0,2},{1,65},{2,4},{3,67},{4,6},{5,69},{6,0},{7,71},{8,10},{9,73},... | collective-permute-start | bytes 1671176 | tf_op jit(solution)/shard_map/ppermute | solution.py:40
  40.0 1.6 %collective-permute-start.11 = (bf16[272,1024]{1,0:T(8,128)(2,1)S(1)}, bf16[272,1024]{1,0:T(8,128)(2,1)S(1)}, u32[]{:S(2)}, u32[]{:S(2)}) collective-permute-start(bf16[272,1024]{1,0:T(8,128)(2,1)S(1)} %half_far.1), channel_id=1, source_target_pairs={{0,6},{1,193},{2,0},{3,195},{4,2},{5,197},{6,4},{7,199},{8,14},{9,... | collective-permute-start | bytes 1671176 | tf_op jit(solution)/shard_map/ppermute | solution.py:40
  41.7 1.0 %collective-permute-start.14 = (bf16[272,1024]{1,0:T(8,128)(2,1)S(1)}, bf16[272,1024]{1,0:T(8,128)(2,1)S(1)}, u32[]{:S(2)}, u32[]{:S(2)}) collective-permute-start(bf16[272,1024]{1,0:T(8,128)(2,1)S(1)} %collective-permute-done.12.refs_3_.refs_11_), channel_id=1, source_target_pairs={{0,8},{1,57},{2,10},{3,59},{4,12},{5,61},{6,14},{7,63},{8,16},{9,1... | collective-permute-start | bytes 1671176 | tf_op jit(solution)/shard_map/ppermute | solution.py:40
  42.7 4.3 %stage_3.1.refs_2_ = f32[6,16,256]{2,1,0:T(8,128)S(1)} custom-call(bf16[528,1024]{1,0:T(8,128)(2,1)S(1)} %pack_line.1.refs_0_, bf16[528,1024]{1,0:T(8,128)(2,1)S(1)} %collective-permute-done.6.whole_ref.refs_1_, bf16[528,1024]{1,0:T(8,128)(2,1)S(1)} %collective-permute-done.7.whole_ref.refs_2_, bf16[272,1024]{1,0:T(8,128)(2,1)S(1)} %collective-permute-done.8.refs_3_.refs_8_, ...), custom_call_target="tpu_custom_call" | custom-call | tf_op jit(solution)/shard_map/stage_3/pallas_call | solution.py:178
  47.0 1.2 %stage_4.1.refs_3_ = f32[6,16,256]{2,1,0:T(8,128)S(1)} custom-call(bf16[528,1024]{1,0:T(8,128)(2,1)S(1)} %pack_line.1.refs_0_, bf16[528,1024]{1,0:T(8,128)(2,1)S(1)} %collective-permute-done.6.whole_ref.refs_1_, bf16[528,1024]{1,0:T(8,128)(2,1)S(1)} %collective-permute-done.7.whole_ref.refs_2_, bf16[272,1024]{1,0:T(8,128)(2,1)S(1)} %collective-permute-done.12.refs_3_.refs_11_), custom_call_target="tpu_custom_call" | custom-call | tf_op jit(solution)/shard_map/stage_4/pallas_call | solution.py:178
  48.2 0.8 %collective-permute-done.10.refs_3_ = bf16[272,1024]{1,0:T(8,128)(2,1)S(1)} collective-permute-done((bf16[272,1024]{1,0:T(8,128)(2,1)S(1)}, bf16[272,1024]{1,0:T(8,128)(2,1)S(1)}, u32[]{:S(2)}, u32[]{:S(2)}) %collective-permute-start.10) | collective-permute-done | bytes 557088 | tf_op jit(solution)/shard_map/ppermute | solution.py:40
  49.0 0.6 collective-permute-done.11.refs_4_
  49.6 3.6 %stage_5.1.refs_4_ = f32[8,16,256]{2,1,0:T(8,128)S(1)} custom-call(bf16[528,1024]{1,0:T(8,128)(2,1)S(1)} %pack_line.1.refs_0_, bf16[528,1024]{1,0:T(8,128)(2,1)S(1)} %collective-permute-done.6.whole_ref.refs_1_, bf16[528,1024]{1,0:T(8,128)(2,1)S(1)} %collective-permute-done.7.whole_ref.refs_2_, bf16[272,1024]{1,0:T(8,128)(2,1)S(1)} %collective-permute-done.10.refs_3_, ...), custom_call_target="tpu_custom_call" | custom-call | tf_op jit(solution)/shard_map/stage_5/pallas_call | solution.py:178
  53.3 1.6 %stage_6.1.refs_5_ = f32[8,16,256]{2,1,0:T(8,128)S(1)} custom-call(bf16[528,1024]{1,0:T(8,128)(2,1)S(1)} %pack_line.1.refs_0_, bf16[528,1024]{1,0:T(8,128)(2,1)S(1)} %collective-permute-done.6.whole_ref.refs_1_, bf16[528,1024]{1,0:T(8,128)(2,1)S(1)} %collective-permute-done.7.whole_ref.refs_2_, bf16[272,1024]{1,0:T(8,128)(2,1)S(1)} %collective-permute-done.10.refs_3_, ...), custom_call_target="tpu_custom_call" | custom-call | tf_op jit(solution)/shard_map/stage_6/pallas_call | solution.py:178
  54.8 0.1 collect.1
  54.9 13.2 %all_to_all.11 = f32[16,2,128]{2,1,0:T(2,128)S(1)} all-to-all(f32[16,2,128]{2,1,0:T(2,128)S(1)} %bitcast.5), channel_id=1, replica_groups=mesh['x'=4,'z'=8,'y'=4,'c'=2] {'x','y'}, dimensions={0} | all-to-all | bytes 32768 | tf_op jit(solution)/shard_map/all_to_all | solution.py:292
  68.2 0.5 finish.1
  (16 shorter events, 0.4 us)
Async XLA Ops:
  0.6 1.0 %copy-start = (bf16[128,1024]{1,0:T(8,128)(2,1)S(1)}, bf16[128,1024]{1,0:T(8,128)(2,1)}, u32[]{:S(2)}) copy-start(bf16[128,1024]{1,0:T(8,128)(2,1)} %rows_ref.1) | copy-start | bytes 786436
  1.6 0.7 copy-start.1
  2.4 1.7 %collective-permute-start = (bf16[144,1024]{1,0:T(8,128)(2,1)S(1)}, bf16[144,1024]{1,0:T(8,128)(2,1)S(1)}, u32[]{:S(2)}, u32[]{:S(2)}) collective-permute-start(bf16[144,1024]{1,0:T(8,128)(2,1)S(1)} %prepare.1.a_ref.refs_0_), channel_id=1, source_target_pairs={{0,1},{1,0},{2,3},{3,2},{4,5},{5,4},{6,7},{7,6},{8,9},{9,8},{10,11... | collective-permute-start | bytes 884744 | tf_op jit(solution)/shard_map/ppermute | solution.py:40
  4.1 14.1 %collective-permute-start.1 = (bf16[272,1024]{1,0:T(8,128)(2,1)S(1)}, bf16[272,1024]{1,0:T(8,128)(2,1)S(1)}, u32[]{:S(2)}, u32[]{:S(2)}) collective-permute-start(bf16[272,1024]{1,0:T(8,128)(2,1)S(1)} %pack_keys.1.refs_1_.refs_5_.refs_6_), channel_id=1, source_target_pairs={{0,8},{1,57},{2,10},{3,59},{4,12},{5,61},{6,14},{7,63},{8,16},{9,1... | collective-permute-start | bytes 1671176 | tf_op jit(solution)/shard_map/ppermute | solution.py:40
  6.1 7.9 %collective-permute-start.2 = (bf16[144,1024]{1,0:T(8,128)(2,1)S(1)}, bf16[144,1024]{1,0:T(8,128)(2,1)S(1)}, u32[]{:S(2)}, u32[]{:S(2)}) collective-permute-start(bf16[144,1024]{1,0:T(8,128)(2,1)S(1)} %prepare.1.a_ref.refs_0_), channel_id=1, source_target_pairs={{0,64},{1,3},{2,66},{3,5},{4,68},{5,7},{6,70},{7,1},{8,72},{9,11},... | collective-permute-start | bytes 884744 | tf_op jit(solution)/shard_map/ppermute | solution.py:40
  7.6 9.2 %collective-permute-start.3 = (bf16[144,1024]{1,0:T(8,128)(2,1)S(1)}, bf16[144,1024]{1,0:T(8,128)(2,1)S(1)}, u32[]{:S(2)}, u32[]{:S(2)}) collective-permute-start(bf16[144,1024]{1,0:T(8,128)(2,1)S(1)} %prepare.1.a_ref.refs_0_), channel_id=1, source_target_pairs={{0,192},{1,7},{2,194},{3,1},{4,196},{5,3},{6,198},{7,5},{8,200},{9... | collective-permute-start | bytes 884744 | tf_op jit(solution)/shard_map/ppermute | solution.py:40
  9.3 8.8 %collective-permute-start.4 = (bf16[144,1024]{1,0:T(8,128)(2,1)S(1)}, bf16[144,1024]{1,0:T(8,128)(2,1)S(1)}, u32[]{:S(2)}, u32[]{:S(2)}) collective-permute-start(bf16[144,1024]{1,0:T(8,128)(2,1)S(1)} %prepare.1.a_ref.refs_0_), channel_id=1, source_target_pairs={{0,128},{1,5},{2,130},{3,7},{4,132},{5,1},{6,134},{7,3},{8,136},{9... | collective-permute-start | bytes 884744 | tf_op jit(solution)/shard_map/ppermute | solution.py:40
  18.2 10.2 %collective-permute-start.5 = (bf16[272,1024]{1,0:T(8,128)(2,1)S(1)}, bf16[272,1024]{1,0:T(8,128)(2,1)S(1)}, u32[]{:S(2)}, u32[]{:S(2)}) collective-permute-start(bf16[272,1024]{1,0:T(8,128)(2,1)S(1)} %collective-permute-done.1.refs_2_.refs_6_.refs_7_), channel_id=1, source_target_pairs={{0,8},{1,57},{2,10},{3,59},{4,12},{5,61},{6,14},{7,63},{8,16},{9,1... | collective-permute-start | bytes 1671176 | tf_op jit(solution)/shard_map/ppermute | solution.py:40
  21.4 16.4 %collective-permute-start.6 = (bf16[528,1024]{1,0:T(8,128)(2,1)S(1)}, bf16[528,1024]{1,0:T(8,128)(2,1)S(1)}, u32[]{:S(2)}, u32[]{:S(2)}) collective-permute-start(bf16[528,1024]{1,0:T(8,128)(2,1)S(1)} %pack_line.1.refs_0_), channel_id=1, source_target_pairs={{0,2},{1,65},{2,4},{3,67},{4,6},{5,69},{6,0},{7,71},{8,10},{9,73},... | collective-permute-start | bytes 3244040 | tf_op jit(solution)/shard_map/ppermute | solution.py:40
  23.0 15.2 %collective-permute-start.7 = (bf16[528,1024]{1,0:T(8,128)(2,1)S(1)}, bf16[528,1024]{1,0:T(8,128)(2,1)S(1)}, u32[]{:S(2)}, u32[]{:S(2)}) collective-permute-start(bf16[528,1024]{1,0:T(8,128)(2,1)S(1)} %pack_line.1.refs_0_), channel_id=1, source_target_pairs={{0,6},{1,193},{2,0},{3,195},{4,2},{5,197},{6,4},{7,199},{8,14},{9,... | collective-permute-start | bytes 3244040 | tf_op jit(solution)/shard_map/ppermute | solution.py:40
  25.6 5.8 %collective-permute-start.8 = (bf16[272,1024]{1,0:T(8,128)(2,1)S(1)}, bf16[272,1024]{1,0:T(8,128)(2,1)S(1)}, u32[]{:S(2)}, u32[]{:S(2)}) collective-permute-start(bf16[272,1024]{1,0:T(8,128)(2,1)S(1)} %collective-permute-done.1.refs_2_.refs_6_.refs_7_), channel_id=1, source_target_pairs={{0,1},{1,0},{2,3},{3,2},{4,5},{5,4},{6,7},{7,6},{8,9},{9,8},{10,11... | collective-permute-start | bytes 1671176 | tf_op jit(solution)/shard_map/ppermute | solution.py:40
  28.3 9.8 %collective-permute-start.9 = (bf16[272,1024]{1,0:T(8,128)(2,1)S(1)}, bf16[272,1024]{1,0:T(8,128)(2,1)S(1)}, u32[]{:S(2)}, u32[]{:S(2)}) collective-permute-start(bf16[272,1024]{1,0:T(8,128)(2,1)S(1)} %collective-permute-done.5.refs_1_.refs_7_.refs_9_), channel_id=1, source_target_pairs={{0,1},{1,0},{2,3},{3,2},{4,5},{5,4},{6,7},{7,6},{8,9},{9,8},{10,11... | collective-permute-start | bytes 1671176 | tf_op jit(solution)/shard_map/ppermute | solution.py:40
  28.3 13.3 %collective-permute-start.12 = (bf16[272,1024]{1,0:T(8,128)(2,1)S(1)}, bf16[272,1024]{1,0:T(8,128)(2,1)S(1)}, u32[]{:S(2)}, u32[]{:S(2)}) collective-permute-start(bf16[272,1024]{1,0:T(8,128)(2,1)S(1)} %collective-permute-done.5.refs_1_.refs_7_.refs_9_), channel_id=1, source_target_pairs={{0,8},{1,57},{2,10},{3,59},{4,12},{5,61},{6,14},{7,63},{8,16},{9,1... | collective-permute-start | bytes 1671176 | tf_op jit(solution)/shard_map/ppermute | solution.py:40
  38.2 10.8 %collective-permute-start.10 = (bf16[272,1024]{1,0:T(8,128)(2,1)S(1)}, bf16[272,1024]{1,0:T(8,128)(2,1)S(1)}, u32[]{:S(2)}, u32[]{:S(2)}) collective-permute-start(bf16[272,1024]{1,0:T(8,128)(2,1)S(1)} %half_near.1), channel_id=1, source_target_pairs={{0,2},{1,65},{2,4},{3,67},{4,6},{5,69},{6,0},{7,71},{8,10},{9,73},... | collective-permute-start | bytes 1671176 | tf_op jit(solution)/shard_map/ppermute | solution.py:40
  40.0 9.6 %collective-permute-start.11 = (bf16[272,1024]{1,0:T(8,128)(2,1)S(1)}, bf16[272,1024]{1,0:T(8,128)(2,1)S(1)}, u32[]{:S(2)}, u32[]{:S(2)}) collective-permute-start(bf16[272,1024]{1,0:T(8,128)(2,1)S(1)} %half_far.1), channel_id=1, source_target_pairs={{0,6},{1,193},{2,0},{3,195},{4,2},{5,197},{6,4},{7,199},{8,14},{9,... | collective-permute-start | bytes 1671176 | tf_op jit(solution)/shard_map/ppermute | solution.py:40
  41.7 8.0 %collective-permute-start.13 = (bf16[272,1024]{1,0:T(8,128)(2,1)S(1)}, bf16[272,1024]{1,0:T(8,128)(2,1)S(1)}, u32[]{:S(2)}, u32[]{:S(2)}) collective-permute-start(bf16[272,1024]{1,0:T(8,128)(2,1)S(1)} %collective-permute-done.12.refs_3_.refs_11_), channel_id=1, source_target_pairs={{0,1},{1,0},{2,3},{3,2},{4,5},{5,4},{6,7},{7,6},{8,9},{9,8},{10,11... | collective-permute-start | bytes 1671176 | tf_op jit(solution)/shard_map/ppermute | solution.py:40
  41.7 11.6 %collective-permute-start.14 = (bf16[272,1024]{1,0:T(8,128)(2,1)S(1)}, bf16[272,1024]{1,0:T(8,128)(2,1)S(1)}, u32[]{:S(2)}, u32[]{:S(2)}) collective-permute-start(bf16[272,1024]{1,0:T(8,128)(2,1)S(1)} %collective-permute-done.12.refs_3_.refs_11_), channel_id=1, source_target_pairs={{0,8},{1,57},{2,10},{3,59},{4,12},{5,61},{6,14},{7,63},{8,16},{9,1... | collective-permute-start | bytes 1671176 | tf_op jit(solution)/shard_map/ppermute | solution.py:40

commit v4 on v3

--- a/solution.py
+++ b/solution.py
@@ -101,6 +101,11 @@
     out_ref[PAIR:, 512:] = b_ref[ROWS:, 0:512]
 
 
+def first_half_kernel(keys_ref, out_ref):
+    out_ref[0:ROWS] = keys_ref[0:ROWS]
+    out_ref[ROWS:] = keys_ref[PAIR:]
+
+
 def pack_queries_kernel(*refs):
     out_ref = refs[-1]
     last = ROWS * (len(refs) - 1)
@@ -134,7 +139,7 @@
 
     for i, rows in enumerate(key_rows):
         for g in range(rows // 16):
-            lane = 64 * (g if rows == PAIR else g + 8)
+            lane = 64 * g
             values = k_refs[i][rows : rows + EXTRA, lane : lane + 1].astype(jnp.float32)
             column[i, 16 * g : 16 * g + 16, :] = jnp.broadcast_to(values, (16, 128))
 
@@ -161,10 +166,9 @@
                     row = lax.broadcasted_iota(jnp.int32, (rows, 128), 0)
                     lane = lax.broadcasted_iota(jnp.int32, (rows, 128), 1)
                     same = same & (row != lane)
-                part = jnp.where(same, part, LOWEST)
-                weight = jnp.exp2(part * (SCALE * LOG2E) - OFFSET * LOG2E)
-                tops.append(jnp.max(part.reshape(rows // 8, 8, 128), 0))
-                totals.append(jnp.sum(weight.reshape(rows // 8, 8, 128), 0))
+                power = part * (SCALE * LOG2E) + jnp.where(same, -OFFSET * LOG2E, LOWEST)
+                tops.append(jnp.max(power.reshape(rows // 8, 8, 128), 0))
+                totals.append(jnp.sum(jnp.exp2(power).reshape(rows // 8, 8, 128), 0))
             top = jnp.maximum(top, jnp.concatenate(tops, 1))
             total = total + jnp.concatenate(totals, 1)
         out_ref[q, 0:8] = top
@@ -222,7 +226,7 @@
     for i in range(1, NX * NY):
         top = jnp.maximum(top, parts_ref[2 * i : 2 * i + 1, :])
         total = total + parts_ref[2 * i + 1 : 2 * i + 2, :]
-    top_ref[...] = top * SCALE
+    top_ref[...] = (top + OFFSET * LOG2E) * (1.0 / LOG2E)
     soft_ref[...] = jnp.log1p(total)
 
 
@@ -240,53 +244,51 @@
 def per_device(rows, mark):
     together = lax.optimization_barrier
     mine = prepare(rows, mark)
+    keys = lambda first, second: pack(pack_keys_kernel, "pack_keys", PAIR, first, second)
     a = first_axis(mine, 1)
     b = first_axis(mine, -1)
+    d = first_axis(mine, 2)
     other = swap(mine)
-    z0 = pack(pack_keys_kernel, "pack_keys", PAIR, mine, other)
+    z0 = keys(mine, other)
     t1 = away(z0)
-    d = first_axis(mine, 2)
-    t1, a, b, d = together((t1, a, b, d))
-
-    t2 = away(t1)
     x = pack(pack_queries_kernel, "pack_line", 2 * PAIR, mine, a, b, d)
     e = second_axis(x, 1)
     f = second_axis(x, -1)
-    s1 = stage([x], [z0, t1], ((0, 1),) * 2, True, "stage_1")
+    t2 = away(t1)
+    s1 = stage([x], [z0, t1], ((0, 1),) * 2, True, "stage_1", 0)
     t2, s1 = together((t2, s1))
 
     t3 = away(t2)
     u1 = swap(t1)
     u2 = swap(t2)
-    s2 = stage([x], [t2], ((0,),) * 2, False, "stage_2")
-    e, f, u1, u2, s2 = together((e, f, u1, u2, s2))
+    s2 = stage([x], [t2, u1, u2], ((0, 1, 2),) * 2, False, "stage_2", 0)
+    e, f, s2 = together((e, f, s2))
 
     g1 = second_axis(pack(functools.partial(half_queries_kernel, 0), "half_near", PAIR, e), 1)
     g2 = second_axis(pack(functools.partial(half_queries_kernel, 1), "half_far", PAIR, f), -1)
-    s3 = stage(
-        [x, e, f], [u1, u2, z0, t1, t2], ((0, 1),) * 2 + ((0, 1, 2, 3, 4),) * 4, False, "stage_3"
-    )
-    t4 = away(t3)
+    s3 = stage([e], [z0, t1, u1, t2, u2], ((0, 1, 2, 3, 4),) * 2, False, "stage_3", 0)
+    t3, s3 = together((t3, s3))
+
+    t4 = away(pack(first_half_kernel, "first_half", ROWS, t3))
+    s4 = stage([f], [z0, t1, u1, t2, u2], ((0, 1, 2, 3, 4),) * 2, False, "stage_4", 0)
+    t3, s4 = together((t3, s4))
     u3 = swap(t3)
-    s4 = stage([x, e, f], [t3], ((0,),) * 6, False, "stage_4")
-    g1, g2, u3, s3, s4 = together((g1, g2, u3, s3, s4))
-
-    s5 = stage(
-        [x, e, f, g1, g2],
-        [u3, z0, t1, u1, t2, u2, t3],
-        ((0,),) * 6 + ((0, 1, 2, 3, 4, 5, 6),) * 2,
-        False,
-        "stage_5",
-    )
+    s4b = stage([x, e, f], [t3], ((0,),) * 6, False, "stage_4b")
+    g1, g2, s4, s4b = together((g1, g2, s4, s4b))
+    s5 = stage([g1, g2], [z0, t1, u1, t2, u2, t3], ((0, 1, 2, 3, 4, 5),) * 2, False, "stage_5", 0)
     t4, s5 = together((t4, s5))
-    s6 = stage([x, e, f, g1, g2], [t4], ((0,),) * 8, False, "stage_6")
+    queries = [x, e, f, g1, g2]
+    u4 = swap(t4)
+    s6 = stage(queries, [u3], ((0,),) * 8, False, "stage_6")
+    s7 = stage(queries, [keys(t4, u4)], ((0,),) * 8, False, "stage_7")
 
     near, far = ((0, 0), (-1, 0)), ((1, 0), (-2, 0))
     move = lambda pair, step: tuple((p, step) for p, _ in pair)
     chunks = [near, far, move(near, -1), move(far, -1), move(near, 1), move(far, 1), move(near, -2), move(far, 2)]
     steps = [s for pair in chunks for s in pair]
-    stages = [s1, s2, s3, s4, s5, s6]
-    plan = [[(i, q) for i, s in enumerate(stages) if q < s.shape[0]] for q in range(8)]
+    stages = [s1, s2, s3, s4, s4b, s5, s6, s7]
+    held = [(0, 1), (0, 1), (2, 3), (4, 5), range(6), (6, 7), range(8), range(8)]
+    plan = [[(i, list(h).index(q)) for i, h in enumerate(held) if q in h] for q in range(8)]
 
     parts = collect(plan, steps, stages)
     parts = lax.all_to_all(parts, ("x", "y"), split_axis=0, concat_axis=0, tiled=True)

time: 68.9 us -> 67.3 us (0.977)
  the two profiles are of different devices: /device:TPU:64 before, /device:TPU:1 now
where the time goes in v4:
time: 67.3 us; the launch traced here: 66.1 us
  starting transfers between devices  26.5 us (39%)
  waiting for transfers between devices  12.9 us (19%)
  Pallas kernels  12.8 us (19%)
  blocking collectives  11.5 us (17%)
  local copies, waits for them, and re-layouts  1.6 us (2%)
  between operations  0.79 us (1%)
    ppermute x16, starting transfers between devices, shift(): return lax.ppermute(value, AXES, pairs)  26.5 us
    ppermute x16, waiting for transfers between devices, shift(): return lax.ppermute(value, AXES, pairs)  12.9 us
    pallas_call x8, Pallas kernels, stage(): pl.pallas_call(functools.partial(stage_kernel, key_rows, chunk_counts, wo...  11.8 us
    all_to_all x1, blocking collectives, per_device(): lax.all_to_all(parts, ('x', 'y'), split_axis=0, concat_axis=0, tiled=True)  11.5 us
    unnamed x4, local copies, waits for them, and re-layouts  1.6 us
  transfers between devices with their start and end apart: 16, of which 8 were waited for; matrix products, arithmetic and copies ran while one was open for 0% of the time, Pallas kernels for 16%

profile of v4, /device:TPU:1, one launch (start us, length us, event | category | flops | bytes accessed | tf_op | source)
XLA Modules:
  0.0 66.1 jit_solution(13024275671034921987)
XLA Ops:
  0.6 0.9 %copy-done = bf16[128,1024]{1,0:T(8,128)(2,1)S(1)} copy-done((bf16[128,1024]{1,0:T(8,128)(2,1)S(1)}, bf16[128,1024]{1,0:T(8,128)(2,1)}, u32[]{:S(2)}) %copy-start) | copy-done | bytes 262168
  1.6 0.7 copy-done.1
  2.4 3.3 %collective-permute-start = (bf16[144,1024]{1,0:T(8,128)(2,1)S(1)}, bf16[144,1024]{1,0:T(8,128)(2,1)S(1)}, u32[]{:S(2)}, u32[]{:S(2)}) collective-permute-start(bf16[144,1024]{1,0:T(8,128)(2,1)S(1)} %prepare.1.a_ref.refs_0_), channel_id=1, source_target_pairs={{0,1},{1,0},{2,3},{3,2},{4,5},{5,4},{6,7},{7,6},{8,9},{9,8},{10,11... | collective-permute-start | bytes 884744 | tf_op jit(solution)/shard_map/ppermute | solution.py:40
  5.7 1.2 %collective-permute-done.b_ref = bf16[144,1024]{1,0:T(8,128)(2,1)S(1)} collective-permute-done((bf16[144,1024]{1,0:T(8,128)(2,1)S(1)}, bf16[144,1024]{1,0:T(8,128)(2,1)S(1)}, u32[]{:S(2)}, u32[]{:S(2)}) %collective-permute-start) | collective-permute-done | bytes 294944 | tf_op jit(solution)/shard_map/ppermute | solution.py:40
  7.0 3.9 %collective-permute-start.1 = (bf16[272,1024]{1,0:T(8,128)(2,1)S(1)}, bf16[272,1024]{1,0:T(8,128)(2,1)S(1)}, u32[]{:S(2)}, u32[]{:S(2)}) collective-permute-start(bf16[272,1024]{1,0:T(8,128)(2,1)S(1)} %pack_keys.2.refs_1_.refs_2_), channel_id=1, source_target_pairs={{0,8},{1,57},{2,10},{3,59},{4,12},{5,61},{6,14},{7,63},{8,16},{9,1... | collective-permute-start | bytes 1671176 | tf_op jit(solution)/shard_map/ppermute | solution.py:40
  10.9 1.3 %collective-permute-start.3 = (bf16[144,1024]{1,0:T(8,128)(2,1)S(1)}, bf16[144,1024]{1,0:T(8,128)(2,1)S(1)}, u32[]{:S(2)}, u32[]{:S(2)}) collective-permute-start(bf16[144,1024]{1,0:T(8,128)(2,1)S(1)} %prepare.1.a_ref.refs_0_), channel_id=1, source_target_pairs={{0,64},{1,3},{2,66},{3,5},{4,68},{5,7},{6,70},{7,1},{8,72},{9,11},... | collective-permute-start | bytes 884744 | tf_op jit(solution)/shard_map/ppermute | solution.py:40
  12.2 1.4 %collective-permute-start.4 = (bf16[144,1024]{1,0:T(8,128)(2,1)S(1)}, bf16[144,1024]{1,0:T(8,128)(2,1)S(1)}, u32[]{:S(2)}, u32[]{:S(2)}) collective-permute-start(bf16[144,1024]{1,0:T(8,128)(2,1)S(1)} %prepare.1.a_ref.refs_0_), channel_id=1, source_target_pairs={{0,192},{1,7},{2,194},{3,1},{4,196},{5,3},{6,198},{7,5},{8,200},{9... | collective-permute-start | bytes 884744 | tf_op jit(solution)/shard_map/ppermute | solution.py:40
  13.6 1.6 %collective-permute-start.5 = (bf16[144,1024]{1,0:T(8,128)(2,1)S(1)}, bf16[144,1024]{1,0:T(8,128)(2,1)S(1)}, u32[]{:S(2)}, u32[]{:S(2)}) collective-permute-start(bf16[144,1024]{1,0:T(8,128)(2,1)S(1)} %prepare.1.a_ref.refs_0_), channel_id=1, source_target_pairs={{0,128},{1,5},{2,130},{3,7},{4,132},{5,1},{6,134},{7,3},{8,136},{9... | collective-permute-start | bytes 884744 | tf_op jit(solution)/shard_map/ppermute | solution.py:40
  15.3 2.1 %collective-permute-done.1.refs_2_.refs_3_ = bf16[272,1024]{1,0:T(8,128)(2,1)S(1)} collective-permute-done((bf16[272,1024]{1,0:T(8,128)(2,1)S(1)}, bf16[272,1024]{1,0:T(8,128)(2,1)S(1)}, u32[]{:S(2)}, u32[]{:S(2)}) %collective-permute-start.1) | collective-permute-done | bytes 557088 | tf_op jit(solution)/shard_map/ppermute | solution.py:40
  17.3 3.4 %collective-permute-start.2 = (bf16[272,1024]{1,0:T(8,128)(2,1)S(1)}, bf16[272,1024]{1,0:T(8,128)(2,1)S(1)}, u32[]{:S(2)}, u32[]{:S(2)}) collective-permute-start(bf16[272,1024]{1,0:T(8,128)(2,1)S(1)} %collective-permute-done.1.refs_2_.refs_3_), channel_id=1, source_target_pairs={{0,8},{1,57},{2,10},{3,59},{4,12},{5,61},{6,14},{7,63},{8,16},{9,1... | collective-permute-start | bytes 1671176 | tf_op jit(solution)/shard_map/ppermute | solution.py:40
  20.8 1.3 %collective-permute-done.5.refs_3_ = bf16[144,1024]{1,0:T(8,128)(2,1)S(1)} collective-permute-done((bf16[144,1024]{1,0:T(8,128)(2,1)S(1)}, bf16[144,1024]{1,0:T(8,128)(2,1)S(1)}, u32[]{:S(2)}, u32[]{:S(2)}) %collective-permute-start.5) | collective-permute-done | bytes 294944 | tf_op jit(solution)/shard_map/ppermute | solution.py:40
  22.1 1.3 %collective-permute-start.6 = (bf16[528,1024]{1,0:T(8,128)(2,1)S(1)}, bf16[528,1024]{1,0:T(8,128)(2,1)S(1)}, u32[]{:S(2)}, u32[]{:S(2)}) collective-permute-start(bf16[528,1024]{1,0:T(8,128)(2,1)S(1)} %pack_line.1.refs_0_), channel_id=1, source_target_pairs={{0,2},{1,65},{2,4},{3,67},{4,6},{5,69},{6,0},{7,71},{8,10},{9,73},... | collective-permute-start | bytes 3244040 | tf_op jit(solution)/shard_map/ppermute | solution.py:40
  23.4 1.5 %collective-permute-start.7 = (bf16[528,1024]{1,0:T(8,128)(2,1)S(1)}, bf16[528,1024]{1,0:T(8,128)(2,1)S(1)}, u32[]{:S(2)}, u32[]{:S(2)}) collective-permute-start(bf16[528,1024]{1,0:T(8,128)(2,1)S(1)} %pack_line.1.refs_0_), channel_id=1, source_target_pairs={{0,6},{1,193},{2,0},{3,195},{4,2},{5,197},{6,4},{7,199},{8,14},{9,... | collective-permute-start | bytes 3244040 | tf_op jit(solution)/shard_map/ppermute | solution.py:40
  24.9 0.8 %stage_1.1.refs_0_ = f32[2,16,256]{2,1,0:T(8,128)S(1)} custom-call(bf16[528,1024]{1,0:T(8,128)(2,1)S(1)} %pack_line.1.refs_0_, bf16[272,1024]{1,0:T(8,128)(2,1)S(1)} %pack_keys.2.refs_1_.refs_2_, bf16[272,1024]{1,0:T(8,128)(2,1)S(1)} %collective-permute-done.1.refs_2_.refs_3_), custom_call_target="tpu_custom_call" | custom-call | tf_op jit(solution)/shard_map/stage_1/pallas_call | solution.py:182
  25.8 1.4 %collective-permute-done.2.refs_1_.refs_4_.refs_5_ = bf16[272,1024]{1,0:T(8,128)(2,1)S(1)} collective-permute-done((bf16[272,1024]{1,0:T(8,128)(2,1)S(1)}, bf16[272,1024]{1,0:T(8,128)(2,1)S(1)}, u32[]{:S(2)}, u32[]{:S(2)}) %collective-permute-start.2) | collective-permute-done | bytes 557088 | tf_op jit(solution)/shard_map/ppermute | solution.py:40
  27.2 2.5 %collective-permute-start.9 = (bf16[272,1024]{1,0:T(8,128)(2,1)S(1)}, bf16[272,1024]{1,0:T(8,128)(2,1)S(1)}, u32[]{:S(2)}, u32[]{:S(2)}) collective-permute-start(bf16[272,1024]{1,0:T(8,128)(2,1)S(1)} %collective-permute-done.2.refs_1_.refs_4_.refs_5_), channel_id=1, source_target_pairs={{0,1},{1,0},{2,3},{3,2},{4,5},{5,4},{6,7},{7,6},{8,9},{9,8},{10,11... | collective-permute-start | bytes 1671176 | tf_op jit(solution)/shard_map/ppermute | solution.py:40
  29.8 0.9 %collective-permute-start.10 = (bf16[272,1024]{1,0:T(8,128)(2,1)S(1)}, bf16[272,1024]{1,0:T(8,128)(2,1)S(1)}, u32[]{:S(2)}, u32[]{:S(2)}) collective-permute-start(bf16[272,1024]{1,0:T(8,128)(2,1)S(1)} %collective-permute-done.2.refs_1_.refs_4_.refs_5_), channel_id=1, source_target_pairs={{0,8},{1,57},{2,10},{3,59},{4,12},{5,61},{6,14},{7,63},{8,16},{9,1... | collective-permute-start | bytes 1671176 | tf_op jit(solution)/shard_map/ppermute | solution.py:40
  30.7 0.7 %collective-permute-done.9.refs_3_.refs_5_.refs_6_ = bf16[272,1024]{1,0:T(8,128)(2,1)S(1)} collective-permute-done((bf16[272,1024]{1,0:T(8,128)(2,1)S(1)}, bf16[272,1024]{1,0:T(8,128)(2,1)S(1)}, u32[]{:S(2)}, u32[]{:S(2)}) %collective-permute-start.9) | collective-permute-done | bytes 557088 | tf_op jit(solution)/shard_map/ppermute | solution.py:40
  31.4 1.1 %stage_2.1.refs_1_ = f32[2,16,256]{2,1,0:T(8,128)S(1)} custom-call(bf16[528,1024]{1,0:T(8,128)(2,1)S(1)} %pack_line.1.refs_0_, bf16[272,1024]{1,0:T(8,128)(2,1)S(1)} %collective-permute-done.2.refs_1_.refs_4_.refs_5_, bf16[272,1024]{1,0:T(8,128)(2,1)S(1)} %collective-permute-done.8.refs_2_.refs_3_.refs_4_, ...), custom_call_target="tpu_custom_call" | custom-call | tf_op jit(solution)/shard_map/stage_2/pallas_call | solution.py:182
  32.5 5.2 %collective-permute-done.6.refs_0_.whole_ref.refs_1_ = bf16[528,1024]{1,0:T(8,128)(2,1)S(1)} collective-permute-done((bf16[528,1024]{1,0:T(8,128)(2,1)S(1)}, bf16[528,1024]{1,0:T(8,128)(2,1)S(1)}, u32[]{:S(2)}, u32[]{:S(2)}) %collective-permute-start.6) | collective-permute-done | bytes 1081376 | tf_op jit(solution)/shard_map/ppermute | solution.py:40
  37.8 1.3 %collective-permute-start.11 = (bf16[272,1024]{1,0:T(8,128)(2,1)S(1)}, bf16[272,1024]{1,0:T(8,128)(2,1)S(1)}, u32[]{:S(2)}, u32[]{:S(2)}) collective-permute-start(bf16[272,1024]{1,0:T(8,128)(2,1)S(1)} %half_near.1), channel_id=1, source_target_pairs={{0,2},{1,65},{2,4},{3,67},{4,6},{5,69},{6,0},{7,71},{8,10},{9,73},... | collective-permute-start | bytes 1671176 | tf_op jit(solution)/shard_map/ppermute | solution.py:40
  39.1 1.7 %collective-permute-start.12 = (bf16[272,1024]{1,0:T(8,128)(2,1)S(1)}, bf16[272,1024]{1,0:T(8,128)(2,1)S(1)}, u32[]{:S(2)}, u32[]{:S(2)}) collective-permute-start(bf16[272,1024]{1,0:T(8,128)(2,1)S(1)} %half_far.1), channel_id=1, source_target_pairs={{0,6},{1,193},{2,0},{3,195},{4,2},{5,197},{6,4},{7,199},{8,14},{9,... | collective-permute-start | bytes 1671176 | tf_op jit(solution)/shard_map/ppermute | solution.py:40
  40.8 1.8 %stage_3.1.refs_2_ = f32[2,16,256]{2,1,0:T(8,128)S(1)} custom-call(bf16[528,1024]{1,0:T(8,128)(2,1)S(1)} %collective-permute-done.6.refs_0_.whole_ref.refs_1_, bf16[272,1024]{1,0:T(8,128)(2,1)S(1)} %pack_keys.2.refs_1_.refs_2_, bf16[272,1024]{1,0:T(8,128)(2,1)S(1)} %collective-permute-done.1.refs_2_.refs_3_, ...), custom_call_target="tpu_custom_call" | custom-call | tf_op jit(solution)/shard_map/stage_3/pallas_call | solution.py:182
  42.7 1.0 %collective-permute-start.13 = (bf16[144,1024]{1,0:T(8,128)(2,1)S(1)}, bf16[144,1024]{1,0:T(8,128)(2,1)S(1)}, u32[]{:S(2)}, u32[]{:S(2)}) collective-permute-start(bf16[144,1024]{1,0:T(8,128)(2,1)S(1)} %first_half.1), channel_id=1, source_target_pairs={{0,8},{1,57},{2,10},{3,59},{4,12},{5,61},{6,14},{7,63},{8,16},{9,1... | collective-permute-start | bytes 884744 | tf_op jit(solution)/shard_map/ppermute | solution.py:40
  43.7 1.8 %stage_4.1.refs_3_ = f32[2,16,256]{2,1,0:T(8,128)S(1)} custom-call(bf16[528,1024]{1,0:T(8,128)(2,1)S(1)} %collective-permute-done.7.whole_ref.refs_0_.refs_2_, bf16[272,1024]{1,0:T(8,128)(2,1)S(1)} %pack_keys.2.refs_1_.refs_2_, bf16[272,1024]{1,0:T(8,128)(2,1)S(1)} %collective-permute-done.1.refs_2_.refs_3_, ...), custom_call_target="tpu_custom_call" | custom-call | tf_op jit(solution)/shard_map/stage_4/pallas_call | solution.py:182
  45.9 1.2 %stage_4b.1.refs_4_ = f32[6,16,256]{2,1,0:T(8,128)S(1)} custom-call(bf16[528,1024]{1,0:T(8,128)(2,1)S(1)} %pack_line.1.refs_0_, bf16[528,1024]{1,0:T(8,128)(2,1)S(1)} %collective-permute-done.6.refs_0_.whole_ref.refs_1_, bf16[528,1024]{1,0:T(8,128)(2,1)S(1)} %collective-permute-done.7.whole_ref.refs_0_.refs_2_, ...), custom_call_target="tpu_custom_call" | custom-call | tf_op jit(solution)/shard_map/stage_4b/pallas_call | solution.py:182
  47.1 0.7 collective-permute-done.11.refs_0_.refs_3_
  48.0 2.1 %stage_5.1.refs_5_ = f32[2,16,256]{2,1,0:T(8,128)S(1)} custom-call(bf16[272,1024]{1,0:T(8,128)(2,1)S(1)} %collective-permute-done.11.refs_0_.refs_3_, bf16[272,1024]{1,0:T(8,128)(2,1)S(1)} %collective-permute-done.12.refs_1_.refs_4_, bf16[272,1024]{1,0:T(8,128)(2,1)S(1)} %pack_keys.2.refs_1_.refs_2_, ...), custom_call_target="tpu_custom_call" | custom-call | tf_op jit(solution)/shard_map/stage_5/pallas_call | solution.py:182
  50.1 0.7 %collective-permute-start.15 = (bf16[144,1024]{1,0:T(8,128)(2,1)S(1)}, bf16[144,1024]{1,0:T(8,128)(2,1)S(1)}, u32[]{:S(2)}, u32[]{:S(2)}) collective-permute-start(bf16[144,1024]{1,0:T(8,128)(2,1)S(1)} %collective-permute-done.13.a_ref), channel_id=1, source_target_pairs={{0,1},{1,0},{2,3},{3,2},{4,5},{5,4},{6,7},{7,6},{8,9},{9,8},{10,11... | collective-permute-start | bytes 884744 | tf_op jit(solution)/shard_map/ppermute | solution.py:40
  50.8 1.5 %stage_6.1.refs_6_ = f32[8,16,256]{2,1,0:T(8,128)S(1)} custom-call(bf16[528,1024]{1,0:T(8,128)(2,1)S(1)} %pack_line.1.refs_0_, bf16[528,1024]{1,0:T(8,128)(2,1)S(1)} %collective-permute-done.6.refs_0_.whole_ref.refs_1_, bf16[528,1024]{1,0:T(8,128)(2,1)S(1)} %collective-permute-done.7.whole_ref.refs_0_.refs_2_, ...), custom_call_target="tpu_custom_call" | custom-call | tf_op jit(solution)/shard_map/stage_6/pallas_call | solution.py:182
  52.4 1.5 %stage_7.1.refs_7_ = f32[8,16,256]{2,1,0:T(8,128)S(1)} custom-call(bf16[528,1024]{1,0:T(8,128)(2,1)S(1)} %pack_line.1.refs_0_, bf16[528,1024]{1,0:T(8,128)(2,1)S(1)} %collective-permute-done.6.refs_0_.whole_ref.refs_1_, bf16[528,1024]{1,0:T(8,128)(2,1)S(1)} %collective-permute-done.7.whole_ref.refs_0_.refs_2_, ...), custom_call_target="tpu_custom_call" | custom-call | tf_op jit(solution)/shard_map/stage_7/pallas_call | solution.py:182
  54.0 11.5 %all_to_all.11 = f32[16,2,128]{2,1,0:T(2,128)S(1)} all-to-all(f32[16,2,128]{2,1,0:T(2,128)S(1)} %bitcast.5), channel_id=1, replica_groups=mesh['x'=4,'z'=8,'y'=4,'c'=2] {'x','y'}, dimensions={0} | all-to-all | bytes 32768 | tf_op jit(solution)/shard_map/all_to_all | solution.py:294
  (22 shorter events, 1.8 us)
Async XLA Ops:
  0.6 1.0 %copy-start = (bf16[128,1024]{1,0:T(8,128)(2,1)S(1)}, bf16[128,1024]{1,0:T(8,128)(2,1)}, u32[]{:S(2)}) copy-start(bf16[128,1024]{1,0:T(8,128)(2,1)} %rows_ref.1) | copy-start | bytes 786436
  1.6 0.7 copy-start.1
  2.4 4.5 %collective-permute-start = (bf16[144,1024]{1,0:T(8,128)(2,1)S(1)}, bf16[144,1024]{1,0:T(8,128)(2,1)S(1)}, u32[]{:S(2)}, u32[]{:S(2)}) collective-permute-start(bf16[144,1024]{1,0:T(8,128)(2,1)S(1)} %prepare.1.a_ref.refs_0_), channel_id=1, source_target_pairs={{0,1},{1,0},{2,3},{3,2},{4,5},{5,4},{6,7},{7,6},{8,9},{9,8},{10,11... | collective-permute-start | bytes 884744 | tf_op jit(solution)/shard_map/ppermute | solution.py:40
  7.0 10.4 %collective-permute-start.1 = (bf16[272,1024]{1,0:T(8,128)(2,1)S(1)}, bf16[272,1024]{1,0:T(8,128)(2,1)S(1)}, u32[]{:S(2)}, u32[]{:S(2)}) collective-permute-start(bf16[272,1024]{1,0:T(8,128)(2,1)S(1)} %pack_keys.2.refs_1_.refs_2_), channel_id=1, source_target_pairs={{0,8},{1,57},{2,10},{3,59},{4,12},{5,61},{6,14},{7,63},{8,16},{9,1... | collective-permute-start | bytes 1671176 | tf_op jit(solution)/shard_map/ppermute | solution.py:40
  10.9 9.9 %collective-permute-start.3 = (bf16[144,1024]{1,0:T(8,128)(2,1)S(1)}, bf16[144,1024]{1,0:T(8,128)(2,1)S(1)}, u32[]{:S(2)}, u32[]{:S(2)}) collective-permute-start(bf16[144,1024]{1,0:T(8,128)(2,1)S(1)} %prepare.1.a_ref.refs_0_), channel_id=1, source_target_pairs={{0,64},{1,3},{2,66},{3,5},{4,68},{5,7},{6,70},{7,1},{8,72},{9,11},... | collective-permute-start | bytes 884744 | tf_op jit(solution)/shard_map/ppermute | solution.py:40
  12.2 8.6 %collective-permute-start.4 = (bf16[144,1024]{1,0:T(8,128)(2,1)S(1)}, bf16[144,1024]{1,0:T(8,128)(2,1)S(1)}, u32[]{:S(2)}, u32[]{:S(2)}) collective-permute-start(bf16[144,1024]{1,0:T(8,128)(2,1)S(1)} %prepare.1.a_ref.refs_0_), channel_id=1, source_target_pairs={{0,192},{1,7},{2,194},{3,1},{4,196},{5,3},{6,198},{7,5},{8,200},{9... | collective-permute-start | bytes 884744 | tf_op jit(solution)/shard_map/ppermute | solution.py:40
  13.6 8.4 %collective-permute-start.5 = (bf16[144,1024]{1,0:T(8,128)(2,1)S(1)}, bf16[144,1024]{1,0:T(8,128)(2,1)S(1)}, u32[]{:S(2)}, u32[]{:S(2)}) collective-permute-start(bf16[144,1024]{1,0:T(8,128)(2,1)S(1)} %prepare.1.a_ref.refs_0_), channel_id=1, source_target_pairs={{0,128},{1,5},{2,130},{3,7},{4,132},{5,1},{6,134},{7,3},{8,136},{9... | collective-permute-start | bytes 884744 | tf_op jit(solution)/shard_map/ppermute | solution.py:40
  17.3 9.9 %collective-permute-start.2 = (bf16[272,1024]{1,0:T(8,128)(2,1)S(1)}, bf16[272,1024]{1,0:T(8,128)(2,1)S(1)}, u32[]{:S(2)}, u32[]{:S(2)}) collective-permute-start(bf16[272,1024]{1,0:T(8,128)(2,1)S(1)} %collective-permute-done.1.refs_2_.refs_3_), channel_id=1, source_target_pairs={{0,8},{1,57},{2,10},{3,59},{4,12},{5,61},{6,14},{7,63},{8,16},{9,1... | collective-permute-start | bytes 1671176 | tf_op jit(solution)/shard_map/ppermute | solution.py:40
  22.1 15.6 %collective-permute-start.6 = (bf16[528,1024]{1,0:T(8,128)(2,1)S(1)}, bf16[528,1024]{1,0:T(8,128)(2,1)S(1)}, u32[]{:S(2)}, u32[]{:S(2)}) collective-permute-start(bf16[528,1024]{1,0:T(8,128)(2,1)S(1)} %pack_line.1.refs_0_), channel_id=1, source_target_pairs={{0,2},{1,65},{2,4},{3,67},{4,6},{5,69},{6,0},{7,71},{8,10},{9,73},... | collective-permute-start | bytes 3244040 | tf_op jit(solution)/shard_map/ppermute | solution.py:40
  23.4 14.3 %collective-permute-start.7 = (bf16[528,1024]{1,0:T(8,128)(2,1)S(1)}, bf16[528,1024]{1,0:T(8,128)(2,1)S(1)}, u32[]{:S(2)}, u32[]{:S(2)}) collective-permute-start(bf16[528,1024]{1,0:T(8,128)(2,1)S(1)} %pack_line.1.refs_0_), channel_id=1, source_target_pairs={{0,6},{1,193},{2,0},{3,195},{4,2},{5,197},{6,4},{7,199},{8,14},{9,... | collective-permute-start | bytes 3244040 | tf_op jit(solution)/shard_map/ppermute | solution.py:40
  25.7 4.9 %collective-permute-start.8 = (bf16[272,1024]{1,0:T(8,128)(2,1)S(1)}, bf16[272,1024]{1,0:T(8,128)(2,1)S(1)}, u32[]{:S(2)}, u32[]{:S(2)}) collective-permute-start(bf16[272,1024]{1,0:T(8,128)(2,1)S(1)} %collective-permute-done.1.refs_2_.refs_3_), channel_id=1, source_target_pairs={{0,1},{1,0},{2,3},{3,2},{4,5},{5,4},{6,7},{7,6},{8,9},{9,8},{10,11... | collective-permute-start | bytes 1671176 | tf_op jit(solution)/shard_map/ppermute | solution.py:40
  27.2 4.1 %collective-permute-start.9 = (bf16[272,1024]{1,0:T(8,128)(2,1)S(1)}, bf16[272,1024]{1,0:T(8,128)(2,1)S(1)}, u32[]{:S(2)}, u32[]{:S(2)}) collective-permute-start(bf16[272,1024]{1,0:T(8,128)(2,1)S(1)} %collective-permute-done.2.refs_1_.refs_4_.refs_5_), channel_id=1, source_target_pairs={{0,1},{1,0},{2,3},{3,2},{4,5},{5,4},{6,7},{7,6},{8,9},{9,8},{10,11... | collective-permute-start | bytes 1671176 | tf_op jit(solution)/shard_map/ppermute | solution.py:40
  29.8 12.8 %collective-permute-start.10 = (bf16[272,1024]{1,0:T(8,128)(2,1)S(1)}, bf16[272,1024]{1,0:T(8,128)(2,1)S(1)}, u32[]{:S(2)}, u32[]{:S(2)}) collective-permute-start(bf16[272,1024]{1,0:T(8,128)(2,1)S(1)} %collective-permute-done.2.refs_1_.refs_4_.refs_5_), channel_id=1, source_target_pairs={{0,8},{1,57},{2,10},{3,59},{4,12},{5,61},{6,14},{7,63},{8,16},{9,1... | collective-permute-start | bytes 1671176 | tf_op jit(solution)/shard_map/ppermute | solution.py:40
  37.8 10.0 %collective-permute-start.11 = (bf16[272,1024]{1,0:T(8,128)(2,1)S(1)}, bf16[272,1024]{1,0:T(8,128)(2,1)S(1)}, u32[]{:S(2)}, u32[]{:S(2)}) collective-permute-start(bf16[272,1024]{1,0:T(8,128)(2,1)S(1)} %half_near.1), channel_id=1, source_target_pairs={{0,2},{1,65},{2,4},{3,67},{4,6},{5,69},{6,0},{7,71},{8,10},{9,73},... | collective-permute-start | bytes 1671176 | tf_op jit(solution)/shard_map/ppermute | solution.py:40
  39.1 8.9 %collective-permute-start.12 = (bf16[272,1024]{1,0:T(8,128)(2,1)S(1)}, bf16[272,1024]{1,0:T(8,128)(2,1)S(1)}, u32[]{:S(2)}, u32[]{:S(2)}) collective-permute-start(bf16[272,1024]{1,0:T(8,128)(2,1)S(1)} %half_far.1), channel_id=1, source_target_pairs={{0,6},{1,193},{2,0},{3,195},{4,2},{5,197},{6,4},{7,199},{8,14},{9,... | collective-permute-start | bytes 1671176 | tf_op jit(solution)/shard_map/ppermute | solution.py:40
  42.7 7.5 %collective-permute-start.13 = (bf16[144,1024]{1,0:T(8,128)(2,1)S(1)}, bf16[144,1024]{1,0:T(8,128)(2,1)S(1)}, u32[]{:S(2)}, u32[]{:S(2)}) collective-permute-start(bf16[144,1024]{1,0:T(8,128)(2,1)S(1)} %first_half.1), channel_id=1, source_target_pairs={{0,8},{1,57},{2,10},{3,59},{4,12},{5,61},{6,14},{7,63},{8,16},{9,1... | collective-permute-start | bytes 884744 | tf_op jit(solution)/shard_map/ppermute | solution.py:40
  45.5 5.3 %collective-permute-start.14 = (bf16[272,1024]{1,0:T(8,128)(2,1)S(1)}, bf16[272,1024]{1,0:T(8,128)(2,1)S(1)}, u32[]{:S(2)}, u32[]{:S(2)}) collective-permute-start(bf16[272,1024]{1,0:T(8,128)(2,1)S(1)} %collective-permute-done.10.refs_3_.keys_ref.refs_7_), channel_id=1, source_target_pairs={{0,1},{1,0},{2,3},{3,2},{4,5},{5,4},{6,7},{7,6},{8,9},{9,8},{10,11... | collective-permute-start | bytes 1671176 | tf_op jit(solution)/shard_map/ppermute | solution.py:40
  50.1 2.2 %collective-permute-start.15 = (bf16[144,1024]{1,0:T(8,128)(2,1)S(1)}, bf16[144,1024]{1,0:T(8,128)(2,1)S(1)}, u32[]{:S(2)}, u32[]{:S(2)}) collective-permute-start(bf16[144,1024]{1,0:T(8,128)(2,1)S(1)} %collective-permute-done.13.a_ref), channel_id=1, source_target_pairs={{0,1},{1,0},{2,3},{3,2},{4,5},{5,4},{6,7},{7,6},{8,9},{9,8},{10,11... | collective-permute-start | bytes 884744 | tf_op jit(solution)/shard_map/ppermute | solution.py:40

commit v5 on v4

--- a/solution.py
+++ b/solution.py
@@ -251,7 +251,7 @@
     other = swap(mine)
     z0 = keys(mine, other)
     t1 = away(z0)
-    x = pack(pack_queries_kernel, "pack_line", 2 * PAIR, mine, a, b, d)
+    x = pack(pack_queries_kernel, "pack_line", 2 * PAIR, mine, d, a, b)
     e = second_axis(x, 1)
     f = second_axis(x, -1)
     t2 = away(t1)
@@ -282,7 +282,7 @@
     s6 = stage(queries, [u3], ((0,),) * 8, False, "stage_6")
     s7 = stage(queries, [keys(t4, u4)], ((0,),) * 8, False, "stage_7")
 
-    near, far = ((0, 0), (-1, 0)), ((1, 0), (-2, 0))
+    near, far = ((0, 0), (-2, 0)), ((-1, 0), (1, 0))
     move = lambda pair, step: tuple((p, step) for p, _ in pair)
     chunks = [near, far, move(near, -1), move(far, -1), move(near, 1), move(far, 1), move(near, -2), move(far, 2)]
     steps = [s for pair in chunks for s in pair]

time: 67.3 us -> 67.1 us (level)
  waiting for transfers between devices: 12.9 us -> 11.1 us
  starting transfers between devices: 26.5 us -> 27.7 us
    ppermute x16, waiting for transfers between devices: 12.9 us -> 11.1 us  [shift(): return lax.ppermute(value, AXES, pairs)]
    ppermute x16, starting transfers between devices: 26.5 us -> 27.7 us  [shift(): return lax.ppermute(value, AXES, pairs)]
  transfers between devices with their start and end apart: 16 -> 16, of which waited for: 8 -> 9; matrix products, arithmetic and copies ran while one was open for 0% -> 0% of each run, Pallas kernels for 16% -> 16%
where the time goes in v5:
time: 67.1 us; the launch traced here: 66.1 us
  starting transfers between devices  27.7 us (41%)
  Pallas kernels  12.8 us (19%)
  blocking collectives  12.1 us (18%)
  waiting for transfers between devices  11.1 us (17%)
  local copies, waits for them, and re-layouts  1.6 us (2%)
  between operations  0.79 us (1%)
    ppermute x16, starting transfers between devices, shift(): return lax.ppermute(value, AXES, pairs)  27.7 us
    all_to_all x1, blocking collectives, per_device(): lax.all_to_all(parts, ('x', 'y'), split_axis=0, concat_axis=0, tiled=True)  12.1 us
    pallas_call x8, Pallas kernels, stage(): pl.pallas_call(functools.partial(stage_kernel, key_rows, chunk_counts, wo...  11.8 us
    ppermute x16, waiting for transfers between devices, shift(): return lax.ppermute(value, AXES, pairs)  11.1 us
    unnamed x4, local copies, waits for them, and re-layouts  1.6 us
  transfers between devices with their start and end apart: 16, of which 9 were waited for; matrix products, arithmetic and copies ran while one was open for 0% of the time, Pallas kernels for 16%

profile of v5, /device:TPU:1, one launch (start us, length us, event | category | flops | bytes accessed | tf_op | source)
XLA Modules:
  0.0 66.1 jit_solution(12036178789466293619)
XLA Ops:
  0.6 0.9 %copy-done = bf16[128,1024]{1,0:T(8,128)(2,1)S(1)} copy-done((bf16[128,1024]{1,0:T(8,128)(2,1)S(1)}, bf16[128,1024]{1,0:T(8,128)(2,1)}, u32[]{:S(2)}) %copy-start) | copy-done | bytes 262168
  1.6 0.7 copy-done.1
  2.4 3.3 %collective-permute-start = (bf16[144,1024]{1,0:T(8,128)(2,1)S(1)}, bf16[144,1024]{1,0:T(8,128)(2,1)S(1)}, u32[]{:S(2)}, u32[]{:S(2)}) collective-permute-start(bf16[144,1024]{1,0:T(8,128)(2,1)S(1)} %prepare.1.a_ref.refs_0_), channel_id=1, source_target_pairs={{0,1},{1,0},{2,3},{3,2},{4,5},{5,4},{6,7},{7,6},{8,9},{9,8},{10,11... | collective-permute-start | bytes 884744 | tf_op jit(solution)/shard_map/ppermute | solution.py:40
  5.7 1.2 %collective-permute-done.b_ref = bf16[144,1024]{1,0:T(8,128)(2,1)S(1)} collective-permute-done((bf16[144,1024]{1,0:T(8,128)(2,1)S(1)}, bf16[144,1024]{1,0:T(8,128)(2,1)S(1)}, u32[]{:S(2)}, u32[]{:S(2)}) %collective-permute-start) | collective-permute-done | bytes 294944 | tf_op jit(solution)/shard_map/ppermute | solution.py:40
  7.0 3.9 %collective-permute-start.1 = (bf16[272,1024]{1,0:T(8,128)(2,1)S(1)}, bf16[272,1024]{1,0:T(8,128)(2,1)S(1)}, u32[]{:S(2)}, u32[]{:S(2)}) collective-permute-start(bf16[272,1024]{1,0:T(8,128)(2,1)S(1)} %pack_keys.2.refs_1_.refs_2_), channel_id=1, source_target_pairs={{0,8},{1,57},{2,10},{3,59},{4,12},{5,61},{6,14},{7,63},{8,16},{9,1... | collective-permute-start | bytes 1671176 | tf_op jit(solution)/shard_map/ppermute | solution.py:40
  10.9 2.9 %collective-permute-start.3 = (bf16[144,1024]{1,0:T(8,128)(2,1)S(1)}, bf16[144,1024]{1,0:T(8,128)(2,1)S(1)}, u32[]{:S(2)}, u32[]{:S(2)}) collective-permute-start(bf16[144,1024]{1,0:T(8,128)(2,1)S(1)} %prepare.1.a_ref.refs_0_), channel_id=1, source_target_pairs={{0,128},{1,5},{2,130},{3,7},{4,132},{5,1},{6,134},{7,3},{8,136},{9... | collective-permute-start | bytes 884744 | tf_op jit(solution)/shard_map/ppermute | solution.py:40
  14.2 2.3 %collective-permute-start.5 = (bf16[144,1024]{1,0:T(8,128)(2,1)S(1)}, bf16[144,1024]{1,0:T(8,128)(2,1)S(1)}, u32[]{:S(2)}, u32[]{:S(2)}) collective-permute-start(bf16[144,1024]{1,0:T(8,128)(2,1)S(1)} %prepare.1.a_ref.refs_0_), channel_id=1, source_target_pairs={{0,192},{1,7},{2,194},{3,1},{4,196},{5,3},{6,198},{7,5},{8,200},{9... | collective-permute-start | bytes 884744 | tf_op jit(solution)/shard_map/ppermute | solution.py:40
  16.5 0.9 %collective-permute-done.1.refs_2_.refs_3_ = bf16[272,1024]{1,0:T(8,128)(2,1)S(1)} collective-permute-done((bf16[272,1024]{1,0:T(8,128)(2,1)S(1)}, bf16[272,1024]{1,0:T(8,128)(2,1)S(1)}, u32[]{:S(2)}, u32[]{:S(2)}) %collective-permute-start.1) | collective-permute-done | bytes 557088 | tf_op jit(solution)/shard_map/ppermute | solution.py:40
  17.3 3.4 %collective-permute-start.2 = (bf16[272,1024]{1,0:T(8,128)(2,1)S(1)}, bf16[272,1024]{1,0:T(8,128)(2,1)S(1)}, u32[]{:S(2)}, u32[]{:S(2)}) collective-permute-start(bf16[272,1024]{1,0:T(8,128)(2,1)S(1)} %collective-permute-done.1.refs_2_.refs_3_), channel_id=1, source_target_pairs={{0,8},{1,57},{2,10},{3,59},{4,12},{5,61},{6,14},{7,63},{8,16},{9,1... | collective-permute-start | bytes 1671176 | tf_op jit(solution)/shard_map/ppermute | solution.py:40
  21.5 1.3 %collective-permute-start.6 = (bf16[528,1024]{1,0:T(8,128)(2,1)S(1)}, bf16[528,1024]{1,0:T(8,128)(2,1)S(1)}, u32[]{:S(2)}, u32[]{:S(2)}) collective-permute-start(bf16[528,1024]{1,0:T(8,128)(2,1)S(1)} %pack_line.1.refs_0_), channel_id=1, source_target_pairs={{0,2},{1,65},{2,4},{3,67},{4,6},{5,69},{6,0},{7,71},{8,10},{9,73},... | collective-permute-start | bytes 3244040 | tf_op jit(solution)/shard_map/ppermute | solution.py:40
  22.8 1.5 %collective-permute-start.7 = (bf16[528,1024]{1,0:T(8,128)(2,1)S(1)}, bf16[528,1024]{1,0:T(8,128)(2,1)S(1)}, u32[]{:S(2)}, u32[]{:S(2)}) collective-permute-start(bf16[528,1024]{1,0:T(8,128)(2,1)S(1)} %pack_line.1.refs_0_), channel_id=1, source_target_pairs={{0,6},{1,193},{2,0},{3,195},{4,2},{5,197},{6,4},{7,199},{8,14},{9,... | collective-permute-start | bytes 3244040 | tf_op jit(solution)/shard_map/ppermute | solution.py:40
  24.3 0.8 %stage_1.1.refs_0_ = f32[2,16,256]{2,1,0:T(8,128)S(1)} custom-call(bf16[528,1024]{1,0:T(8,128)(2,1)S(1)} %pack_line.1.refs_0_, bf16[272,1024]{1,0:T(8,128)(2,1)S(1)} %pack_keys.2.refs_1_.refs_2_, bf16[272,1024]{1,0:T(8,128)(2,1)S(1)} %collective-permute-done.1.refs_2_.refs_3_), custom_call_target="tpu_custom_call" | custom-call | tf_op jit(solution)/shard_map/stage_1/pallas_call | solution.py:182
  25.2 2.0 %collective-permute-done.2.refs_1_.refs_4_.refs_5_ = bf16[272,1024]{1,0:T(8,128)(2,1)S(1)} collective-permute-done((bf16[272,1024]{1,0:T(8,128)(2,1)S(1)}, bf16[272,1024]{1,0:T(8,128)(2,1)S(1)}, u32[]{:S(2)}, u32[]{:S(2)}) %collective-permute-start.2) | collective-permute-done | bytes 557088 | tf_op jit(solution)/shard_map/ppermute | solution.py:40
  27.2 2.5 %collective-permute-start.9 = (bf16[272,1024]{1,0:T(8,128)(2,1)S(1)}, bf16[272,1024]{1,0:T(8,128)(2,1)S(1)}, u32[]{:S(2)}, u32[]{:S(2)}) collective-permute-start(bf16[272,1024]{1,0:T(8,128)(2,1)S(1)} %collective-permute-done.2.refs_1_.refs_4_.refs_5_), channel_id=1, source_target_pairs={{0,1},{1,0},{2,3},{3,2},{4,5},{5,4},{6,7},{7,6},{8,9},{9,8},{10,11... | collective-permute-start | bytes 1671176 | tf_op jit(solution)/shard_map/ppermute | solution.py:40
  29.8 0.9 %collective-permute-start.10 = (bf16[272,1024]{1,0:T(8,128)(2,1)S(1)}, bf16[272,1024]{1,0:T(8,128)(2,1)S(1)}, u32[]{:S(2)}, u32[]{:S(2)}) collective-permute-start(bf16[272,1024]{1,0:T(8,128)(2,1)S(1)} %collective-permute-done.2.refs_1_.refs_4_.refs_5_), channel_id=1, source_target_pairs={{0,8},{1,57},{2,10},{3,59},{4,12},{5,61},{6,14},{7,63},{8,16},{9,1... | collective-permute-start | bytes 1671176 | tf_op jit(solution)/shard_map/ppermute | solution.py:40
  30.7 0.7 %collective-permute-done.9.refs_3_.refs_5_.refs_6_ = bf16[272,1024]{1,0:T(8,128)(2,1)S(1)} collective-permute-done((bf16[272,1024]{1,0:T(8,128)(2,1)S(1)}, bf16[272,1024]{1,0:T(8,128)(2,1)S(1)}, u32[]{:S(2)}, u32[]{:S(2)}) %collective-permute-start.9) | collective-permute-done | bytes 557088 | tf_op jit(solution)/shard_map/ppermute | solution.py:40
  31.4 1.1 %stage_2.1.refs_1_ = f32[2,16,256]{2,1,0:T(8,128)S(1)} custom-call(bf16[528,1024]{1,0:T(8,128)(2,1)S(1)} %pack_line.1.refs_0_, bf16[272,1024]{1,0:T(8,128)(2,1)S(1)} %collective-permute-done.2.refs_1_.refs_4_.refs_5_, bf16[272,1024]{1,0:T(8,128)(2,1)S(1)} %collective-permute-done.8.refs_2_.refs_3_.refs_4_, ...), custom_call_target="tpu_custom_call" | custom-call | tf_op jit(solution)/shard_map/stage_2/pallas_call | solution.py:182
  32.5 4.6 %collective-permute-done.6.refs_0_.whole_ref.refs_1_ = bf16[528,1024]{1,0:T(8,128)(2,1)S(1)} collective-permute-done((bf16[528,1024]{1,0:T(8,128)(2,1)S(1)}, bf16[528,1024]{1,0:T(8,128)(2,1)S(1)}, u32[]{:S(2)}, u32[]{:S(2)}) %collective-permute-start.6) | collective-permute-done | bytes 1081376 | tf_op jit(solution)/shard_map/ppermute | solution.py:40
  37.2 1.3 %collective-permute-start.11 = (bf16[272,1024]{1,0:T(8,128)(2,1)S(1)}, bf16[272,1024]{1,0:T(8,128)(2,1)S(1)}, u32[]{:S(2)}, u32[]{:S(2)}) collective-permute-start(bf16[272,1024]{1,0:T(8,128)(2,1)S(1)} %half_near.1), channel_id=1, source_target_pairs={{0,2},{1,65},{2,4},{3,67},{4,6},{5,69},{6,0},{7,71},{8,10},{9,73},... | collective-permute-start | bytes 1671176 | tf_op jit(solution)/shard_map/ppermute | solution.py:40
  38.5 1.7 %collective-permute-start.12 = (bf16[272,1024]{1,0:T(8,128)(2,1)S(1)}, bf16[272,1024]{1,0:T(8,128)(2,1)S(1)}, u32[]{:S(2)}, u32[]{:S(2)}) collective-permute-start(bf16[272,1024]{1,0:T(8,128)(2,1)S(1)} %half_far.1), channel_id=1, source_target_pairs={{0,6},{1,193},{2,0},{3,195},{4,2},{5,197},{6,4},{7,199},{8,14},{9,... | collective-permute-start | bytes 1671176 | tf_op jit(solution)/shard_map/ppermute | solution.py:40
  40.2 1.8 %stage_3.1.refs_2_ = f32[2,16,256]{2,1,0:T(8,128)S(1)} custom-call(bf16[528,1024]{1,0:T(8,128)(2,1)S(1)} %collective-permute-done.6.refs_0_.whole_ref.refs_1_, bf16[272,1024]{1,0:T(8,128)(2,1)S(1)} %pack_keys.2.refs_1_.refs_2_, bf16[272,1024]{1,0:T(8,128)(2,1)S(1)} %collective-permute-done.1.refs_2_.refs_3_, ...), custom_call_target="tpu_custom_call" | custom-call | tf_op jit(solution)/shard_map/stage_3/pallas_call | solution.py:182
  42.1 1.0 %collective-permute-start.13 = (bf16[144,1024]{1,0:T(8,128)(2,1)S(1)}, bf16[144,1024]{1,0:T(8,128)(2,1)S(1)}, u32[]{:S(2)}, u32[]{:S(2)}) collective-permute-start(bf16[144,1024]{1,0:T(8,128)(2,1)S(1)} %first_half.1), channel_id=1, source_target_pairs={{0,8},{1,57},{2,10},{3,59},{4,12},{5,61},{6,14},{7,63},{8,16},{9,1... | collective-permute-start | bytes 884744 | tf_op jit(solution)/shard_map/ppermute | solution.py:40
  43.1 1.8 %stage_4.1.refs_3_ = f32[2,16,256]{2,1,0:T(8,128)S(1)} custom-call(bf16[528,1024]{1,0:T(8,128)(2,1)S(1)} %collective-permute-done.7.whole_ref.refs_0_.refs_2_, bf16[272,1024]{1,0:T(8,128)(2,1)S(1)} %pack_keys.2.refs_1_.refs_2_, bf16[272,1024]{1,0:T(8,128)(2,1)S(1)} %collective-permute-done.1.refs_2_.refs_3_, ...), custom_call_target="tpu_custom_call" | custom-call | tf_op jit(solution)/shard_map/stage_4/pallas_call | solution.py:182
  44.9 0.4 collective-permute-start.14
  45.3 1.2 %stage_4b.1.refs_4_ = f32[6,16,256]{2,1,0:T(8,128)S(1)} custom-call(bf16[528,1024]{1,0:T(8,128)(2,1)S(1)} %pack_line.1.refs_0_, bf16[528,1024]{1,0:T(8,128)(2,1)S(1)} %collective-permute-done.6.refs_0_.whole_ref.refs_1_, bf16[528,1024]{1,0:T(8,128)(2,1)S(1)} %collective-permute-done.7.whole_ref.refs_0_.refs_2_, ...), custom_call_target="tpu_custom_call" | custom-call | tf_op jit(solution)/shard_map/stage_4b/pallas_call | solution.py:182
  46.5 0.6 collective-permute-done.11.refs_0_.refs_3_
  47.4 2.1 %stage_5.1.refs_5_ = f32[2,16,256]{2,1,0:T(8,128)S(1)} custom-call(bf16[272,1024]{1,0:T(8,128)(2,1)S(1)} %collective-permute-done.11.refs_0_.refs_3_, bf16[272,1024]{1,0:T(8,128)(2,1)S(1)} %collective-permute-done.12.refs_1_.refs_4_, bf16[272,1024]{1,0:T(8,128)(2,1)S(1)} %pack_keys.2.refs_1_.refs_2_, ...), custom_call_target="tpu_custom_call" | custom-call | tf_op jit(solution)/shard_map/stage_5/pallas_call | solution.py:182
  49.5 0.7 %collective-permute-start.15 = (bf16[144,1024]{1,0:T(8,128)(2,1)S(1)}, bf16[144,1024]{1,0:T(8,128)(2,1)S(1)}, u32[]{:S(2)}, u32[]{:S(2)}) collective-permute-start(bf16[144,1024]{1,0:T(8,128)(2,1)S(1)} %collective-permute-done.13.a_ref), channel_id=1, source_target_pairs={{0,1},{1,0},{2,3},{3,2},{4,5},{5,4},{6,7},{7,6},{8,9},{9,8},{10,11... | collective-permute-start | bytes 884744 | tf_op jit(solution)/shard_map/ppermute | solution.py:40
  50.2 1.5 %stage_6.1.refs_6_ = f32[8,16,256]{2,1,0:T(8,128)S(1)} custom-call(bf16[528,1024]{1,0:T(8,128)(2,1)S(1)} %pack_line.1.refs_0_, bf16[528,1024]{1,0:T(8,128)(2,1)S(1)} %collective-permute-done.6.refs_0_.whole_ref.refs_1_, bf16[528,1024]{1,0:T(8,128)(2,1)S(1)} %collective-permute-done.7.whole_ref.refs_0_.refs_2_, ...), custom_call_target="tpu_custom_call" | custom-call | tf_op jit(solution)/shard_map/stage_6/pallas_call | solution.py:182
  51.8 1.5 %stage_7.1.refs_7_ = f32[8,16,256]{2,1,0:T(8,128)S(1)} custom-call(bf16[528,1024]{1,0:T(8,128)(2,1)S(1)} %pack_line.1.refs_0_, bf16[528,1024]{1,0:T(8,128)(2,1)S(1)} %collective-permute-done.6.refs_0_.whole_ref.refs_1_, bf16[528,1024]{1,0:T(8,128)(2,1)S(1)} %collective-permute-done.7.whole_ref.refs_0_.refs_2_, ...), custom_call_target="tpu_custom_call" | custom-call | tf_op jit(solution)/shard_map/stage_7/pallas_call | solution.py:182
  53.4 12.1 %all_to_all.11 = f32[16,2,128]{2,1,0:T(2,128)S(1)} all-to-all(f32[16,2,128]{2,1,0:T(2,128)S(1)} %bitcast.5), channel_id=1, replica_groups=mesh['x'=4,'z'=8,'y'=4,'c'=2] {'x','y'}, dimensions={0} | all-to-all | bytes 32768 | tf_op jit(solution)/shard_map/all_to_all | solution.py:294
  65.5 0.5 finish.1
  (22 shorter events, 2.0 us)
Async XLA Ops:
  0.6 1.0 %copy-start = (bf16[128,1024]{1,0:T(8,128)(2,1)S(1)}, bf16[128,1024]{1,0:T(8,128)(2,1)}, u32[]{:S(2)}) copy-start(bf16[128,1024]{1,0:T(8,128)(2,1)} %rows_ref.1) | copy-start | bytes 786436
  1.6 0.7 copy-start.1
  2.4 4.5 %collective-permute-start = (bf16[144,1024]{1,0:T(8,128)(2,1)S(1)}, bf16[144,1024]{1,0:T(8,128)(2,1)S(1)}, u32[]{:S(2)}, u32[]{:S(2)}) collective-permute-start(bf16[144,1024]{1,0:T(8,128)(2,1)S(1)} %prepare.1.a_ref.refs_0_), channel_id=1, source_target_pairs={{0,1},{1,0},{2,3},{3,2},{4,5},{5,4},{6,7},{7,6},{8,9},{9,8},{10,11... | collective-permute-start | bytes 884744 | tf_op jit(solution)/shard_map/ppermute | solution.py:40
  7.0 10.4 %collective-permute-start.1 = (bf16[272,1024]{1,0:T(8,128)(2,1)S(1)}, bf16[272,1024]{1,0:T(8,128)(2,1)S(1)}, u32[]{:S(2)}, u32[]{:S(2)}) collective-permute-start(bf16[272,1024]{1,0:T(8,128)(2,1)S(1)} %pack_keys.2.refs_1_.refs_2_), channel_id=1, source_target_pairs={{0,8},{1,57},{2,10},{3,59},{4,12},{5,61},{6,14},{7,63},{8,16},{9,1... | collective-permute-start | bytes 1671176 | tf_op jit(solution)/shard_map/ppermute | solution.py:40
  10.9 9.9 %collective-permute-start.3 = (bf16[144,1024]{1,0:T(8,128)(2,1)S(1)}, bf16[144,1024]{1,0:T(8,128)(2,1)S(1)}, u32[]{:S(2)}, u32[]{:S(2)}) collective-permute-start(bf16[144,1024]{1,0:T(8,128)(2,1)S(1)} %prepare.1.a_ref.refs_0_), channel_id=1, source_target_pairs={{0,128},{1,5},{2,130},{3,7},{4,132},{5,1},{6,134},{7,3},{8,136},{9... | collective-permute-start | bytes 884744 | tf_op jit(solution)/shard_map/ppermute | solution.py:40
  13.8 7.3 %collective-permute-start.4 = (bf16[144,1024]{1,0:T(8,128)(2,1)S(1)}, bf16[144,1024]{1,0:T(8,128)(2,1)S(1)}, u32[]{:S(2)}, u32[]{:S(2)}) collective-permute-start(bf16[144,1024]{1,0:T(8,128)(2,1)S(1)} %prepare.1.a_ref.refs_0_), channel_id=1, source_target_pairs={{0,64},{1,3},{2,66},{3,5},{4,68},{5,7},{6,70},{7,1},{8,72},{9,11},... | collective-permute-start | bytes 884744 | tf_op jit(solution)/shard_map/ppermute | solution.py:40
  14.2 7.3 %collective-permute-start.5 = (bf16[144,1024]{1,0:T(8,128)(2,1)S(1)}, bf16[144,1024]{1,0:T(8,128)(2,1)S(1)}, u32[]{:S(2)}, u32[]{:S(2)}) collective-permute-start(bf16[144,1024]{1,0:T(8,128)(2,1)S(1)} %prepare.1.a_ref.refs_0_), channel_id=1, source_target_pairs={{0,192},{1,7},{2,194},{3,1},{4,196},{5,3},{6,198},{7,5},{8,200},{9... | collective-permute-start | bytes 884744 | tf_op jit(solution)/shard_map/ppermute | solution.py:40
  17.3 9.9 %collective-permute-start.2 = (bf16[272,1024]{1,0:T(8,128)(2,1)S(1)}, bf16[272,1024]{1,0:T(8,128)(2,1)S(1)}, u32[]{:S(2)}, u32[]{:S(2)}) collective-permute-start(bf16[272,1024]{1,0:T(8,128)(2,1)S(1)} %collective-permute-done.1.refs_2_.refs_3_), channel_id=1, source_target_pairs={{0,8},{1,57},{2,10},{3,59},{4,12},{5,61},{6,14},{7,63},{8,16},{9,1... | collective-permute-start | bytes 1671176 | tf_op jit(solution)/shard_map/ppermute | solution.py:40
  21.5 15.6 %collective-permute-start.6 = (bf16[528,1024]{1,0:T(8,128)(2,1)S(1)}, bf16[528,1024]{1,0:T(8,128)(2,1)S(1)}, u32[]{:S(2)}, u32[]{:S(2)}) collective-permute-start(bf16[528,1024]{1,0:T(8,128)(2,1)S(1)} %pack_line.1.refs_0_), channel_id=1, source_target_pairs={{0,2},{1,65},{2,4},{3,67},{4,6},{5,69},{6,0},{7,71},{8,10},{9,73},... | collective-permute-start | bytes 3244040 | tf_op jit(solution)/shard_map/ppermute | solution.py:40
  22.8 14.3 %collective-permute-start.7 = (bf16[528,1024]{1,0:T(8,128)(2,1)S(1)}, bf16[528,1024]{1,0:T(8,128)(2,1)S(1)}, u32[]{:S(2)}, u32[]{:S(2)}) collective-permute-start(bf16[528,1024]{1,0:T(8,128)(2,1)S(1)} %pack_line.1.refs_0_), channel_id=1, source_target_pairs={{0,6},{1,193},{2,0},{3,195},{4,2},{5,197},{6,4},{7,199},{8,14},{9,... | collective-permute-start | bytes 3244040 | tf_op jit(solution)/shard_map/ppermute | solution.py:40
  25.1 5.5 %collective-permute-start.8 = (bf16[272,1024]{1,0:T(8,128)(2,1)S(1)}, bf16[272,1024]{1,0:T(8,128)(2,1)S(1)}, u32[]{:S(2)}, u32[]{:S(2)}) collective-permute-start(bf16[272,1024]{1,0:T(8,128)(2,1)S(1)} %collective-permute-done.1.refs_2_.refs_3_), channel_id=1, source_target_pairs={{0,1},{1,0},{2,3},{3,2},{4,5},{5,4},{6,7},{7,6},{8,9},{9,8},{10,11... | collective-permute-start | bytes 1671176 | tf_op jit(solution)/shard_map/ppermute | solution.py:40
  27.2 4.1 %collective-permute-start.9 = (bf16[272,1024]{1,0:T(8,128)(2,1)S(1)}, bf16[272,1024]{1,0:T(8,128)(2,1)S(1)}, u32[]{:S(2)}, u32[]{:S(2)}) collective-permute-start(bf16[272,1024]{1,0:T(8,128)(2,1)S(1)} %collective-permute-done.2.refs_1_.refs_4_.refs_5_), channel_id=1, source_target_pairs={{0,1},{1,0},{2,3},{3,2},{4,5},{5,4},{6,7},{7,6},{8,9},{9,8},{10,11... | collective-permute-start | bytes 1671176 | tf_op jit(solution)/shard_map/ppermute | solution.py:40
  29.8 12.2 %collective-permute-start.10 = (bf16[272,1024]{1,0:T(8,128)(2,1)S(1)}, bf16[272,1024]{1,0:T(8,128)(2,1)S(1)}, u32[]{:S(2)}, u32[]{:S(2)}) collective-permute-start(bf16[272,1024]{1,0:T(8,128)(2,1)S(1)} %collective-permute-done.2.refs_1_.refs_4_.refs_5_), channel_id=1, source_target_pairs={{0,8},{1,57},{2,10},{3,59},{4,12},{5,61},{6,14},{7,63},{8,16},{9,1... | collective-permute-start | bytes 1671176 | tf_op jit(solution)/shard_map/ppermute | solution.py:40
  37.2 10.0 %collective-permute-start.11 = (bf16[272,1024]{1,0:T(8,128)(2,1)S(1)}, bf16[272,1024]{1,0:T(8,128)(2,1)S(1)}, u32[]{:S(2)}, u32[]{:S(2)}) collective-permute-start(bf16[272,1024]{1,0:T(8,128)(2,1)S(1)} %half_near.1), channel_id=1, source_target_pairs={{0,2},{1,65},{2,4},{3,67},{4,6},{5,69},{6,0},{7,71},{8,10},{9,73},... | collective-permute-start | bytes 1671176 | tf_op jit(solution)/shard_map/ppermute | solution.py:40
  38.5 8.9 %collective-permute-start.12 = (bf16[272,1024]{1,0:T(8,128)(2,1)S(1)}, bf16[272,1024]{1,0:T(8,128)(2,1)S(1)}, u32[]{:S(2)}, u32[]{:S(2)}) collective-permute-start(bf16[272,1024]{1,0:T(8,128)(2,1)S(1)} %half_far.1), channel_id=1, source_target_pairs={{0,6},{1,193},{2,0},{3,195},{4,2},{5,197},{6,4},{7,199},{8,14},{9,... | collective-permute-start | bytes 1671176 | tf_op jit(solution)/shard_map/ppermute | solution.py:40
  42.1 7.5 %collective-permute-start.13 = (bf16[144,1024]{1,0:T(8,128)(2,1)S(1)}, bf16[144,1024]{1,0:T(8,128)(2,1)S(1)}, u32[]{:S(2)}, u32[]{:S(2)}) collective-permute-start(bf16[144,1024]{1,0:T(8,128)(2,1)S(1)} %first_half.1), channel_id=1, source_target_pairs={{0,8},{1,57},{2,10},{3,59},{4,12},{5,61},{6,14},{7,63},{8,16},{9,1... | collective-permute-start | bytes 884744 | tf_op jit(solution)/shard_map/ppermute | solution.py:40
  44.9 5.4 %collective-permute-start.14 = (bf16[272,1024]{1,0:T(8,128)(2,1)S(1)}, bf16[272,1024]{1,0:T(8,128)(2,1)S(1)}, u32[]{:S(2)}, u32[]{:S(2)}) collective-permute-start(bf16[272,1024]{1,0:T(8,128)(2,1)S(1)} %collective-permute-done.10.refs_3_.keys_ref.refs_7_), channel_id=1, source_target_pairs={{0,1},{1,0},{2,3},{3,2},{4,5},{5,4},{6,7},{7,6},{8,9},{9,8},{10,11... | collective-permute-start | bytes 1671176 | tf_op jit(solution)/shard_map/ppermute | solution.py:40
  49.5 2.2 %collective-permute-start.15 = (bf16[144,1024]{1,0:T(8,128)(2,1)S(1)}, bf16[144,1024]{1,0:T(8,128)(2,1)S(1)}, u32[]{:S(2)}, u32[]{:S(2)}) collective-permute-start(bf16[144,1024]{1,0:T(8,128)(2,1)S(1)} %collective-permute-done.13.a_ref), channel_id=1, source_target_pairs={{0,1},{1,0},{2,3},{3,2},{4,5},{5,4},{6,7},{7,6},{8,9},{9,8},{10,11... | collective-permute-start | bytes 884744 | tf_op jit(solution)/shard_map/ppermute | solution.py:40

commit v6 on v4

--- a/solution.py
+++ b/solution.py
@@ -254,12 +254,14 @@
     x = pack(pack_queries_kernel, "pack_line", 2 * PAIR, mine, a, b, d)
     e = second_axis(x, 1)
     f = second_axis(x, -1)
+    s0 = stage([x], [z0], ((0,),) * 2, True, "stage_0", 3000000000)
+    t1, s0 = together((t1, s0))
     t2 = away(t1)
-    s1 = stage([x], [z0, t1], ((0, 1),) * 2, True, "stage_1", 0)
-    t2, s1 = together((t2, s1))
+    u1 = swap(t1)
+    s1 = stage([x], [t1], ((0,),) * 2, False, "stage_1", 10000000000)
+    t2, u1, s1 = together((t2, u1, s1))
 
     t3 = away(t2)
-    u1 = swap(t1)
     u2 = swap(t2)
     s2 = stage([x], [t2, u1, u2], ((0, 1, 2),) * 2, False, "stage_2", 0)
     e, f, s2 = together((e, f, s2))
@@ -286,8 +288,8 @@
     move = lambda pair, step: tuple((p, step) for p, _ in pair)
     chunks = [near, far, move(near, -1), move(far, -1), move(near, 1), move(far, 1), move(near, -2), move(far, 2)]
     steps = [s for pair in chunks for s in pair]
-    stages = [s1, s2, s3, s4, s4b, s5, s6, s7]
-    held = [(0, 1), (0, 1), (2, 3), (4, 5), range(6), (6, 7), range(8), range(8)]
+    stages = [s0, s1, s2, s3, s4, s4b, s5, s6, s7]
+    held = [(0, 1), (0, 1), (0, 1), (2, 3), (4, 5), range(6), (6, 7), range(8), range(8)]
     plan = [[(i, list(h).index(q)) for i, h in enumerate(held) if q in h] for q in range(8)]
 
     parts = collect(plan, steps, stages)

time: 67.3 us -> 67.7 us (level); the launches traced: 66.1 us -> 67.5 us
  starting transfers between devices: 26.5 us -> 30.6 us
  waiting for transfers between devices: 12.9 us -> 10 us
    ppermute x16, starting transfers between devices: 26.5 us -> 30.6 us  [shift(): return lax.ppermute(value, AXES, pairs)]
    ppermute x16, waiting for transfers between devices: 12.9 us -> 10 us  [shift(): return lax.ppermute(value, AXES, pairs)]
    pallas_call x8 -> x9, Pallas kernels: 11.8 us -> 11.9 us  [stage(): pl.pallas_call(functools.partial(stage_kernel, key_rows, chunk_counts, wo...]
  transfers between devices with their start and end apart: 16 -> 16, of which waited for: 8 -> 4; matrix products, arithmetic and copies ran while one was open for 0% -> 0% of each run, Pallas kernels for 16% -> 16%
where the time goes in v6:
time: 67.7 us; the launch traced here: 67.5 us
  starting transfers between devices  30.6 us (45%)
  Pallas kernels  13 us (19%)
  blocking collectives  11.5 us (17%)
  waiting for transfers between devices  10 us (15%)
  local copies, waits for them, and re-layouts  1.6 us (2%)
  between operations  0.82 us (1%)
    ppermute x16, starting transfers between devices, shift(): return lax.ppermute(value, AXES, pairs)  30.6 us
    pallas_call x9, Pallas kernels, stage(): pl.pallas_call(functools.partial(stage_kernel, key_rows, chunk_counts, wo...  11.9 us
    all_to_all x1, blocking collectives, per_device(): lax.all_to_all(parts, ('x', 'y'), split_axis=0, concat_axis=0, tiled=True)  11.5 us
    ppermute x16, waiting for transfers between devices, shift(): return lax.ppermute(value, AXES, pairs)  10 us
    unnamed x4, local copies, waits for them, and re-layouts  1.6 us
  transfers between devices with their start and end apart: 16, of which 4 were waited for; matrix products, arithmetic and copies ran while one was open for 0% of the time, Pallas kernels for 16%

profile of v6, /device:TPU:1, one launch (start us, length us, event | category | flops | bytes accessed | tf_op | source)
XLA Modules:
  0.0 67.5 jit_solution(8736104487157617780)
XLA Ops:
  0.6 0.9 %copy-done = bf16[128,1024]{1,0:T(8,128)(2,1)S(1)} copy-done((bf16[128,1024]{1,0:T(8,128)(2,1)S(1)}, bf16[128,1024]{1,0:T(8,128)(2,1)}, u32[]{:S(2)}) %copy-start) | copy-done | bytes 262168
  1.6 0.7 copy-done.1
  2.2 0.1 prepare.1.a_ref.refs_0_
  2.4 3.3 %collective-permute-start = (bf16[144,1024]{1,0:T(8,128)(2,1)S(1)}, bf16[144,1024]{1,0:T(8,128)(2,1)S(1)}, u32[]{:S(2)}, u32[]{:S(2)}) collective-permute-start(bf16[144,1024]{1,0:T(8,128)(2,1)S(1)} %prepare.1.a_ref.refs_0_), channel_id=1, source_target_pairs={{0,1},{1,0},{2,3},{3,2},{4,5},{5,4},{6,7},{7,6},{8,9},{9,8},{10,11... | collective-permute-start | bytes 884744 | tf_op jit(solution)/shard_map/ppermute | solution.py:40
  5.7 2.7 %collective-permute-start.3 = (bf16[144,1024]{1,0:T(8,128)(2,1)S(1)}, bf16[144,1024]{1,0:T(8,128)(2,1)S(1)}, u32[]{:S(2)}, u32[]{:S(2)}) collective-permute-start(bf16[144,1024]{1,0:T(8,128)(2,1)S(1)} %prepare.1.a_ref.refs_0_), channel_id=1, source_target_pairs={{0,192},{1,7},{2,194},{3,1},{4,196},{5,3},{6,198},{7,5},{8,200},{9... | collective-permute-start | bytes 884744 | tf_op jit(solution)/shard_map/ppermute | solution.py:40
  8.4 5.6 %collective-permute-start.1 = (bf16[272,1024]{1,0:T(8,128)(2,1)S(1)}, bf16[272,1024]{1,0:T(8,128)(2,1)S(1)}, u32[]{:S(2)}, u32[]{:S(2)}) collective-permute-start(bf16[272,1024]{1,0:T(8,128)(2,1)S(1)} %pack_keys.2.refs_1_.refs_2_), channel_id=1, source_target_pairs={{0,8},{1,57},{2,10},{3,59},{4,12},{5,61},{6,14},{7,63},{8,16},{9,1... | collective-permute-start | bytes 1671176 | tf_op jit(solution)/shard_map/ppermute | solution.py:40
  14.0 1.9 %collective-permute-done.2.refs_1_ = bf16[144,1024]{1,0:T(8,128)(2,1)S(1)} collective-permute-done((bf16[144,1024]{1,0:T(8,128)(2,1)S(1)}, bf16[144,1024]{1,0:T(8,128)(2,1)S(1)}, u32[]{:S(2)}, u32[]{:S(2)}) %collective-permute-start.2) | collective-permute-done | bytes 294944 | tf_op jit(solution)/shard_map/ppermute | solution.py:40
  16.0 0.5 collective-permute-start.7
  16.5 2.3 %collective-permute-start.8 = (bf16[528,1024]{1,0:T(8,128)(2,1)S(1)}, bf16[528,1024]{1,0:T(8,128)(2,1)S(1)}, u32[]{:S(2)}, u32[]{:S(2)}) collective-permute-start(bf16[528,1024]{1,0:T(8,128)(2,1)S(1)} %pack_line.1.refs_0_), channel_id=1, source_target_pairs={{0,6},{1,193},{2,0},{3,195},{4,2},{5,197},{6,4},{7,199},{8,14},{9,... | collective-permute-start | bytes 3244040 | tf_op jit(solution)/shard_map/ppermute | solution.py:40
  18.8 0.5 stage_0.1.refs_0_
  19.3 1.2 %collective-permute-done.1.refs_1_.refs_2_.refs_3_ = bf16[272,1024]{1,0:T(8,128)(2,1)S(1)} collective-permute-done((bf16[272,1024]{1,0:T(8,128)(2,1)S(1)}, bf16[272,1024]{1,0:T(8,128)(2,1)S(1)}, u32[]{:S(2)}, u32[]{:S(2)}) %collective-permute-start.1) | collective-permute-done | bytes 557088 | tf_op jit(solution)/shard_map/ppermute | solution.py:40
  20.5 3.9 %collective-permute-start.5 = (bf16[272,1024]{1,0:T(8,128)(2,1)S(1)}, bf16[272,1024]{1,0:T(8,128)(2,1)S(1)}, u32[]{:S(2)}, u32[]{:S(2)}) collective-permute-start(bf16[272,1024]{1,0:T(8,128)(2,1)S(1)} %collective-permute-done.1.refs_1_.refs_2_.refs_3_), channel_id=1, source_target_pairs={{0,8},{1,57},{2,10},{3,59},{4,12},{5,61},{6,14},{7,63},{8,16},{9,1... | collective-permute-start | bytes 1671176 | tf_op jit(solution)/shard_map/ppermute | solution.py:40
  24.4 0.5 stage_1.1.refs_1_
  24.9 6.0 %collective-permute-done.5.refs_1_.refs_4_.refs_5_ = bf16[272,1024]{1,0:T(8,128)(2,1)S(1)} collective-permute-done((bf16[272,1024]{1,0:T(8,128)(2,1)S(1)}, bf16[272,1024]{1,0:T(8,128)(2,1)S(1)}, u32[]{:S(2)}, u32[]{:S(2)}) %collective-permute-start.5) | collective-permute-done | bytes 557088 | tf_op jit(solution)/shard_map/ppermute | solution.py:40
  30.9 2.6 %collective-permute-start.9 = (bf16[272,1024]{1,0:T(8,128)(2,1)S(1)}, bf16[272,1024]{1,0:T(8,128)(2,1)S(1)}, u32[]{:S(2)}, u32[]{:S(2)}) collective-permute-start(bf16[272,1024]{1,0:T(8,128)(2,1)S(1)} %collective-permute-done.5.refs_1_.refs_4_.refs_5_), channel_id=1, source_target_pairs={{0,1},{1,0},{2,3},{3,2},{4,5},{5,4},{6,7},{7,6},{8,9},{9,8},{10,11... | collective-permute-start | bytes 1671176 | tf_op jit(solution)/shard_map/ppermute | solution.py:40
  33.5 1.7 %collective-permute-start.10 = (bf16[272,1024]{1,0:T(8,128)(2,1)S(1)}, bf16[272,1024]{1,0:T(8,128)(2,1)S(1)}, u32[]{:S(2)}, u32[]{:S(2)}) collective-permute-start(bf16[272,1024]{1,0:T(8,128)(2,1)S(1)} %collective-permute-done.5.refs_1_.refs_4_.refs_5_), channel_id=1, source_target_pairs={{0,8},{1,57},{2,10},{3,59},{4,12},{5,61},{6,14},{7,63},{8,16},{9,1... | collective-permute-start | bytes 1671176 | tf_op jit(solution)/shard_map/ppermute | solution.py:40
  35.2 1.1 %stage_2.1.refs_2_ = f32[2,16,256]{2,1,0:T(8,128)S(1)} custom-call(bf16[528,1024]{1,0:T(8,128)(2,1)S(1)} %pack_line.1.refs_0_, bf16[272,1024]{1,0:T(8,128)(2,1)S(1)} %collective-permute-done.5.refs_1_.refs_4_.refs_5_, bf16[272,1024]{1,0:T(8,128)(2,1)S(1)} %collective-permute-done.6.refs_2_.refs_3_.refs_4_, ...), custom_call_target="tpu_custom_call" | custom-call | tf_op jit(solution)/shard_map/stage_2/pallas_call | solution.py:182
  36.4 1.2 %collective-permute-start.11 = (bf16[272,1024]{1,0:T(8,128)(2,1)S(1)}, bf16[272,1024]{1,0:T(8,128)(2,1)S(1)}, u32[]{:S(2)}, u32[]{:S(2)}) collective-permute-start(bf16[272,1024]{1,0:T(8,128)(2,1)S(1)} %half_near.1), channel_id=1, source_target_pairs={{0,2},{1,65},{2,4},{3,67},{4,6},{5,69},{6,0},{7,71},{8,10},{9,73},... | collective-permute-start | bytes 1671176 | tf_op jit(solution)/shard_map/ppermute | solution.py:40
  37.7 1.8 %collective-permute-start.12 = (bf16[272,1024]{1,0:T(8,128)(2,1)S(1)}, bf16[272,1024]{1,0:T(8,128)(2,1)S(1)}, u32[]{:S(2)}, u32[]{:S(2)}) collective-permute-start(bf16[272,1024]{1,0:T(8,128)(2,1)S(1)} %half_far.1), channel_id=1, source_target_pairs={{0,6},{1,193},{2,0},{3,195},{4,2},{5,197},{6,4},{7,199},{8,14},{9,... | collective-permute-start | bytes 1671176 | tf_op jit(solution)/shard_map/ppermute | solution.py:40
  39.5 1.8 %stage_3.1.refs_3_ = f32[2,16,256]{2,1,0:T(8,128)S(1)} custom-call(bf16[528,1024]{1,0:T(8,128)(2,1)S(1)} %collective-permute-done.7.refs_0_.whole_ref.refs_1_, bf16[272,1024]{1,0:T(8,128)(2,1)S(1)} %pack_keys.2.refs_1_.refs_2_, bf16[272,1024]{1,0:T(8,128)(2,1)S(1)} %collective-permute-done.1.refs_1_.refs_2_.refs_3_, ...), custom_call_target="tpu_custom_call" | custom-call | tf_op jit(solution)/shard_map/stage_3/pallas_call | solution.py:182
  41.3 0.9 %collective-permute-done.10.refs_3_.keys_ref.refs_7_ = bf16[272,1024]{1,0:T(8,128)(2,1)S(1)} collective-permute-done((bf16[272,1024]{1,0:T(8,128)(2,1)S(1)}, bf16[272,1024]{1,0:T(8,128)(2,1)S(1)}, u32[]{:S(2)}, u32[]{:S(2)}) %collective-permute-start.10) | collective-permute-done | bytes 557088 | tf_op jit(solution)/shard_map/ppermute | solution.py:40
  42.2 3.0 %collective-permute-start.13 = (bf16[144,1024]{1,0:T(8,128)(2,1)S(1)}, bf16[144,1024]{1,0:T(8,128)(2,1)S(1)}, u32[]{:S(2)}, u32[]{:S(2)}) collective-permute-start(bf16[144,1024]{1,0:T(8,128)(2,1)S(1)} %first_half.1), channel_id=1, source_target_pairs={{0,8},{1,57},{2,10},{3,59},{4,12},{5,61},{6,14},{7,63},{8,16},{9,1... | collective-permute-start | bytes 884744 | tf_op jit(solution)/shard_map/ppermute | solution.py:40
  45.2 1.8 %stage_4.1.refs_4_ = f32[2,16,256]{2,1,0:T(8,128)S(1)} custom-call(bf16[528,1024]{1,0:T(8,128)(2,1)S(1)} %collective-permute-done.8.whole_ref.refs_0_.refs_2_, bf16[272,1024]{1,0:T(8,128)(2,1)S(1)} %pack_keys.2.refs_1_.refs_2_, bf16[272,1024]{1,0:T(8,128)(2,1)S(1)} %collective-permute-done.1.refs_1_.refs_2_.refs_3_, ...), custom_call_target="tpu_custom_call" | custom-call | tf_op jit(solution)/shard_map/stage_4/pallas_call | solution.py:182
  47.0 0.1 collective-permute-start.14
  47.1 1.2 %stage_4b.1.refs_5_ = f32[6,16,256]{2,1,0:T(8,128)S(1)} custom-call(bf16[528,1024]{1,0:T(8,128)(2,1)S(1)} %pack_line.1.refs_0_, bf16[528,1024]{1,0:T(8,128)(2,1)S(1)} %collective-permute-done.7.refs_0_.whole_ref.refs_1_, bf16[528,1024]{1,0:T(8,128)(2,1)S(1)} %collective-permute-done.8.whole_ref.refs_0_.refs_2_, ...), custom_call_target="tpu_custom_call" | custom-call | tf_op jit(solution)/shard_map/stage_4b/pallas_call | solution.py:182
  48.3 2.1 %stage_5.1.refs_6_ = f32[2,16,256]{2,1,0:T(8,128)S(1)} custom-call(bf16[272,1024]{1,0:T(8,128)(2,1)S(1)} %collective-permute-done.11.refs_0_.refs_3_, bf16[272,1024]{1,0:T(8,128)(2,1)S(1)} %collective-permute-done.12.refs_1_.refs_4_, bf16[272,1024]{1,0:T(8,128)(2,1)S(1)} %pack_keys.2.refs_1_.refs_2_, ...), custom_call_target="tpu_custom_call" | custom-call | tf_op jit(solution)/shard_map/stage_5/pallas_call | solution.py:182
  50.4 1.9 %collective-permute-start.15 = (bf16[144,1024]{1,0:T(8,128)(2,1)S(1)}, bf16[144,1024]{1,0:T(8,128)(2,1)S(1)}, u32[]{:S(2)}, u32[]{:S(2)}) collective-permute-start(bf16[144,1024]{1,0:T(8,128)(2,1)S(1)} %collective-permute-done.13.a_ref), channel_id=1, source_target_pairs={{0,1},{1,0},{2,3},{3,2},{4,5},{5,4},{6,7},{7,6},{8,9},{9,8},{10,11... | collective-permute-start | bytes 884744 | tf_op jit(solution)/shard_map/ppermute | solution.py:40
  52.3 1.5 %stage_6.1.refs_7_ = f32[8,16,256]{2,1,0:T(8,128)S(1)} custom-call(bf16[528,1024]{1,0:T(8,128)(2,1)S(1)} %pack_line.1.refs_0_, bf16[528,1024]{1,0:T(8,128)(2,1)S(1)} %collective-permute-done.7.refs_0_.whole_ref.refs_1_, bf16[528,1024]{1,0:T(8,128)(2,1)S(1)} %collective-permute-done.8.whole_ref.refs_0_.refs_2_, ...), custom_call_target="tpu_custom_call" | custom-call | tf_op jit(solution)/shard_map/stage_6/pallas_call | solution.py:182
  53.8 1.5 %stage_7.1.refs_8_ = f32[8,16,256]{2,1,0:T(8,128)S(1)} custom-call(bf16[528,1024]{1,0:T(8,128)(2,1)S(1)} %pack_line.1.refs_0_, bf16[528,1024]{1,0:T(8,128)(2,1)S(1)} %collective-permute-done.7.refs_0_.whole_ref.refs_1_, bf16[528,1024]{1,0:T(8,128)(2,1)S(1)} %collective-permute-done.8.whole_ref.refs_0_.refs_2_, ...), custom_call_target="tpu_custom_call" | custom-call | tf_op jit(solution)/shard_map/stage_7/pallas_call | solution.py:182
  55.3 0.1 collect.1
  55.4 11.5 %all_to_all.11 = f32[16,2,128]{2,1,0:T(2,128)S(1)} all-to-all(f32[16,2,128]{2,1,0:T(2,128)S(1)} %bitcast.5), channel_id=1, replica_groups=mesh['x'=4,'z'=8,'y'=4,'c'=2] {'x','y'}, dimensions={0} | all-to-all | bytes 32768 | tf_op jit(solution)/shard_map/all_to_all | solution.py:296
  67.0 0.5 finish.1
  (23 shorter events, 0.3 us)
Async XLA Ops:
  0.6 1.0 %copy-start = (bf16[128,1024]{1,0:T(8,128)(2,1)S(1)}, bf16[128,1024]{1,0:T(8,128)(2,1)}, u32[]{:S(2)}) copy-start(bf16[128,1024]{1,0:T(8,128)(2,1)} %rows_ref.1) | copy-start | bytes 786436
  1.6 0.7 copy-start.1
  2.4 6.0 %collective-permute-start = (bf16[144,1024]{1,0:T(8,128)(2,1)S(1)}, bf16[144,1024]{1,0:T(8,128)(2,1)S(1)}, u32[]{:S(2)}, u32[]{:S(2)}) collective-permute-start(bf16[144,1024]{1,0:T(8,128)(2,1)S(1)} %prepare.1.a_ref.refs_0_), channel_id=1, source_target_pairs={{0,1},{1,0},{2,3},{3,2},{4,5},{5,4},{6,7},{7,6},{8,9},{9,8},{10,11... | collective-permute-start | bytes 884744 | tf_op jit(solution)/shard_map/ppermute | solution.py:40
  5.7 10.2 %collective-permute-start.2 = (bf16[144,1024]{1,0:T(8,128)(2,1)S(1)}, bf16[144,1024]{1,0:T(8,128)(2,1)S(1)}, u32[]{:S(2)}, u32[]{:S(2)}) collective-permute-start(bf16[144,1024]{1,0:T(8,128)(2,1)S(1)} %prepare.1.a_ref.refs_0_), channel_id=1, source_target_pairs={{0,64},{1,3},{2,66},{3,5},{4,68},{5,7},{6,70},{7,1},{8,72},{9,11},... | collective-permute-start | bytes 884744 | tf_op jit(solution)/shard_map/ppermute | solution.py:40
  5.7 10.2 %collective-permute-start.3 = (bf16[144,1024]{1,0:T(8,128)(2,1)S(1)}, bf16[144,1024]{1,0:T(8,128)(2,1)S(1)}, u32[]{:S(2)}, u32[]{:S(2)}) collective-permute-start(bf16[144,1024]{1,0:T(8,128)(2,1)S(1)} %prepare.1.a_ref.refs_0_), channel_id=1, source_target_pairs={{0,192},{1,7},{2,194},{3,1},{4,196},{5,3},{6,198},{7,5},{8,200},{9... | collective-permute-start | bytes 884744 | tf_op jit(solution)/shard_map/ppermute | solution.py:40
  8.4 7.6 %collective-permute-start.4 = (bf16[144,1024]{1,0:T(8,128)(2,1)S(1)}, bf16[144,1024]{1,0:T(8,128)(2,1)S(1)}, u32[]{:S(2)}, u32[]{:S(2)}) collective-permute-start(bf16[144,1024]{1,0:T(8,128)(2,1)S(1)} %prepare.1.a_ref.refs_0_), channel_id=1, source_target_pairs={{0,128},{1,5},{2,130},{3,7},{4,132},{5,1},{6,134},{7,3},{8,136},{9... | collective-permute-start | bytes 884744 | tf_op jit(solution)/shard_map/ppermute | solution.py:40
  8.4 12.1 %collective-permute-start.1 = (bf16[272,1024]{1,0:T(8,128)(2,1)S(1)}, bf16[272,1024]{1,0:T(8,128)(2,1)S(1)}, u32[]{:S(2)}, u32[]{:S(2)}) collective-permute-start(bf16[272,1024]{1,0:T(8,128)(2,1)S(1)} %pack_keys.2.refs_1_.refs_2_), channel_id=1, source_target_pairs={{0,8},{1,57},{2,10},{3,59},{4,12},{5,61},{6,14},{7,63},{8,16},{9,1... | collective-permute-start | bytes 1671176 | tf_op jit(solution)/shard_map/ppermute | solution.py:40
  16.0 20.4 %collective-permute-start.7 = (bf16[528,1024]{1,0:T(8,128)(2,1)S(1)}, bf16[528,1024]{1,0:T(8,128)(2,1)S(1)}, u32[]{:S(2)}, u32[]{:S(2)}) collective-permute-start(bf16[528,1024]{1,0:T(8,128)(2,1)S(1)} %pack_line.1.refs_0_), channel_id=1, source_target_pairs={{0,2},{1,65},{2,4},{3,67},{4,6},{5,69},{6,0},{7,71},{8,10},{9,73},... | collective-permute-start | bytes 3244040 | tf_op jit(solution)/shard_map/ppermute | solution.py:40
  16.5 19.9 %collective-permute-start.8 = (bf16[528,1024]{1,0:T(8,128)(2,1)S(1)}, bf16[528,1024]{1,0:T(8,128)(2,1)S(1)}, u32[]{:S(2)}, u32[]{:S(2)}) collective-permute-start(bf16[528,1024]{1,0:T(8,128)(2,1)S(1)} %pack_line.1.refs_0_), channel_id=1, source_target_pairs={{0,6},{1,193},{2,0},{3,195},{4,2},{5,197},{6,4},{7,199},{8,14},{9,... | collective-permute-start | bytes 3244040 | tf_op jit(solution)/shard_map/ppermute | solution.py:40
  20.5 10.4 %collective-permute-start.5 = (bf16[272,1024]{1,0:T(8,128)(2,1)S(1)}, bf16[272,1024]{1,0:T(8,128)(2,1)S(1)}, u32[]{:S(2)}, u32[]{:S(2)}) collective-permute-start(bf16[272,1024]{1,0:T(8,128)(2,1)S(1)} %collective-permute-done.1.refs_1_.refs_2_.refs_3_), channel_id=1, source_target_pairs={{0,8},{1,57},{2,10},{3,59},{4,12},{5,61},{6,14},{7,63},{8,16},{9,1... | collective-permute-start | bytes 1671176 | tf_op jit(solution)/shard_map/ppermute | solution.py:40
  24.4 6.5 %collective-permute-start.6 = (bf16[272,1024]{1,0:T(8,128)(2,1)S(1)}, bf16[272,1024]{1,0:T(8,128)(2,1)S(1)}, u32[]{:S(2)}, u32[]{:S(2)}) collective-permute-start(bf16[272,1024]{1,0:T(8,128)(2,1)S(1)} %collective-permute-done.1.refs_1_.refs_2_.refs_3_), channel_id=1, source_target_pairs={{0,1},{1,0},{2,3},{3,2},{4,5},{5,4},{6,7},{7,6},{8,9},{9,8},{10,11... | collective-permute-start | bytes 1671176 | tf_op jit(solution)/shard_map/ppermute | solution.py:40
  30.9 4.3 %collective-permute-start.9 = (bf16[272,1024]{1,0:T(8,128)(2,1)S(1)}, bf16[272,1024]{1,0:T(8,128)(2,1)S(1)}, u32[]{:S(2)}, u32[]{:S(2)}) collective-permute-start(bf16[272,1024]{1,0:T(8,128)(2,1)S(1)} %collective-permute-done.5.refs_1_.refs_4_.refs_5_), channel_id=1, source_target_pairs={{0,1},{1,0},{2,3},{3,2},{4,5},{5,4},{6,7},{7,6},{8,9},{9,8},{10,11... | collective-permute-start | bytes 1671176 | tf_op jit(solution)/shard_map/ppermute | solution.py:40
  33.5 8.7 %collective-permute-start.10 = (bf16[272,1024]{1,0:T(8,128)(2,1)S(1)}, bf16[272,1024]{1,0:T(8,128)(2,1)S(1)}, u32[]{:S(2)}, u32[]{:S(2)}) collective-permute-start(bf16[272,1024]{1,0:T(8,128)(2,1)S(1)} %collective-permute-done.5.refs_1_.refs_4_.refs_5_), channel_id=1, source_target_pairs={{0,8},{1,57},{2,10},{3,59},{4,12},{5,61},{6,14},{7,63},{8,16},{9,1... | collective-permute-start | bytes 1671176 | tf_op jit(solution)/shard_map/ppermute | solution.py:40
  36.4 11.8 %collective-permute-start.11 = (bf16[272,1024]{1,0:T(8,128)(2,1)S(1)}, bf16[272,1024]{1,0:T(8,128)(2,1)S(1)}, u32[]{:S(2)}, u32[]{:S(2)}) collective-permute-start(bf16[272,1024]{1,0:T(8,128)(2,1)S(1)} %half_near.1), channel_id=1, source_target_pairs={{0,2},{1,65},{2,4},{3,67},{4,6},{5,69},{6,0},{7,71},{8,10},{9,73},... | collective-permute-start | bytes 1671176 | tf_op jit(solution)/shard_map/ppermute | solution.py:40
  37.7 10.6 %collective-permute-start.12 = (bf16[272,1024]{1,0:T(8,128)(2,1)S(1)}, bf16[272,1024]{1,0:T(8,128)(2,1)S(1)}, u32[]{:S(2)}, u32[]{:S(2)}) collective-permute-start(bf16[272,1024]{1,0:T(8,128)(2,1)S(1)} %half_far.1), channel_id=1, source_target_pairs={{0,6},{1,193},{2,0},{3,195},{4,2},{5,197},{6,4},{7,199},{8,14},{9,... | collective-permute-start | bytes 1671176 | tf_op jit(solution)/shard_map/ppermute | solution.py:40
  42.2 8.2 %collective-permute-start.13 = (bf16[144,1024]{1,0:T(8,128)(2,1)S(1)}, bf16[144,1024]{1,0:T(8,128)(2,1)S(1)}, u32[]{:S(2)}, u32[]{:S(2)}) collective-permute-start(bf16[144,1024]{1,0:T(8,128)(2,1)S(1)} %first_half.1), channel_id=1, source_target_pairs={{0,8},{1,57},{2,10},{3,59},{4,12},{5,61},{6,14},{7,63},{8,16},{9,1... | collective-permute-start | bytes 884744 | tf_op jit(solution)/shard_map/ppermute | solution.py:40
  47.0 5.3 %collective-permute-start.14 = (bf16[272,1024]{1,0:T(8,128)(2,1)S(1)}, bf16[272,1024]{1,0:T(8,128)(2,1)S(1)}, u32[]{:S(2)}, u32[]{:S(2)}) collective-permute-start(bf16[272,1024]{1,0:T(8,128)(2,1)S(1)} %collective-permute-done.10.refs_3_.keys_ref.refs_7_), channel_id=1, source_target_pairs={{0,1},{1,0},{2,3},{3,2},{4,5},{5,4},{6,7},{7,6},{8,9},{9,8},{10,11... | collective-permute-start | bytes 1671176 | tf_op jit(solution)/shard_map/ppermute | solution.py:40
  50.4 3.4 %collective-permute-start.15 = (bf16[144,1024]{1,0:T(8,128)(2,1)S(1)}, bf16[144,1024]{1,0:T(8,128)(2,1)S(1)}, u32[]{:S(2)}, u32[]{:S(2)}) collective-permute-start(bf16[144,1024]{1,0:T(8,128)(2,1)S(1)} %collective-permute-done.13.a_ref), channel_id=1, source_target_pairs={{0,1},{1,0},{2,3},{3,2},{4,5},{5,4},{6,7},{7,6},{8,9},{9,8},{10,11... | collective-permute-start | bytes 884744 | tf_op jit(solution)/shard_map/ppermute | solution.py:40

commit v7 on v6

--- a/solution.py
+++ b/solution.py
@@ -251,7 +251,7 @@
     other = swap(mine)
     z0 = keys(mine, other)
     t1 = away(z0)
-    x = pack(pack_queries_kernel, "pack_line", 2 * PAIR, mine, a, b, d)
+    x = pack(pack_queries_kernel, "pack_line", 2 * PAIR, mine, d, a, b)
     e = second_axis(x, 1)
     f = second_axis(x, -1)
     s0 = stage([x], [z0], ((0,),) * 2, True, "stage_0", 3000000000)
@@ -284,7 +284,7 @@
     s6 = stage(queries, [u3], ((0,),) * 8, False, "stage_6")
     s7 = stage(queries, [keys(t4, u4)], ((0,),) * 8, False, "stage_7")
 
-    near, far = ((0, 0), (-1, 0)), ((1, 0), (-2, 0))
+    near, far = ((0, 0), (-2, 0)), ((-1, 0), (1, 0))
     move = lambda pair, step: tuple((p, step) for p, _ in pair)
     chunks = [near, far, move(near, -1), move(far, -1), move(near, 1), move(far, 1), move(near, -2), move(far, 2)]
     steps = [s for pair in chunks for s in pair]

time: 67.7 us -> 67.8 us (level)
  waiting for transfers between devices: 10 us -> 11.2 us
  blocking collectives: 11.5 us -> 10.5 us
    ppermute x16, waiting for transfers between devices: 10 us -> 11.2 us  [shift(): return lax.ppermute(value, AXES, pairs)]
    all_to_all x1, blocking collectives: 11.5 us -> 10.5 us  [per_device(): lax.all_to_all(parts, ('x', 'y'), split_axis=0, concat_axis=0, tiled=True)]
  transfers between devices with their start and end apart: 16 -> 16, of which waited for: 4 -> 5; matrix products, arithmetic and copies ran while one was open for 0% -> 0% of each run, Pallas kernels for 16% -> 16%
where the time goes in v7:
time: 67.8 us; the launch traced here: 67.6 us
  starting transfers between devices  30.5 us (45%)
  Pallas kernels  13 us (19%)
  waiting for transfers between devices  11.2 us (17%)
  blocking collectives  10.5 us (15%)
  local copies, waits for them, and re-layouts  1.6 us (2%)
  between operations  0.82 us (1%)
    ppermute x16, starting transfers between devices, shift(): return lax.ppermute(value, AXES, pairs)  30.5 us
    pallas_call x9, Pallas kernels, stage(): pl.pallas_call(functools.partial(stage_kernel, key_rows, chunk_counts, wo...  12 us
    ppermute x16, waiting for transfers between devices, shift(): return lax.ppermute(value, AXES, pairs)  11.2 us
    all_to_all x1, blocking collectives, per_device(): lax.all_to_all(parts, ('x', 'y'), split_axis=0, concat_axis=0, tiled=True)  10.5 us
    unnamed x4, local copies, waits for them, and re-layouts  1.6 us
  transfers between devices with their start and end apart: 16, of which 5 were waited for; matrix products, arithmetic and copies ran while one was open for 0% of the time, Pallas kernels for 16%

profile of v7, /device:TPU:1, one launch (start us, length us, event | category | flops | bytes accessed | tf_op | source)
XLA Modules:
  0.0 67.6 jit_solution(8146016780625383962)
XLA Ops:
  0.6 0.9 %copy-done = bf16[128,1024]{1,0:T(8,128)(2,1)S(1)} copy-done((bf16[128,1024]{1,0:T(8,128)(2,1)S(1)}, bf16[128,1024]{1,0:T(8,128)(2,1)}, u32[]{:S(2)}) %copy-start) | copy-done | bytes 262168
  1.6 0.7 copy-done.1
  2.4 3.3 %collective-permute-start = (bf16[144,1024]{1,0:T(8,128)(2,1)S(1)}, bf16[144,1024]{1,0:T(8,128)(2,1)S(1)}, u32[]{:S(2)}, u32[]{:S(2)}) collective-permute-start(bf16[144,1024]{1,0:T(8,128)(2,1)S(1)} %prepare.1.a_ref.refs_0_), channel_id=1, source_target_pairs={{0,1},{1,0},{2,3},{3,2},{4,5},{5,4},{6,7},{7,6},{8,9},{9,8},{10,11... | collective-permute-start | bytes 884744 | tf_op jit(solution)/shard_map/ppermute | solution.py:40
  5.7 1.2 %collective-permute-start.2 = (bf16[144,1024]{1,0:T(8,128)(2,1)S(1)}, bf16[144,1024]{1,0:T(8,128)(2,1)S(1)}, u32[]{:S(2)}, u32[]{:S(2)}) collective-permute-start(bf16[144,1024]{1,0:T(8,128)(2,1)S(1)} %prepare.1.a_ref.refs_0_), channel_id=1, source_target_pairs={{0,128},{1,5},{2,130},{3,7},{4,132},{5,1},{6,134},{7,3},{8,136},{9... | collective-permute-start | bytes 884744 | tf_op jit(solution)/shard_map/ppermute | solution.py:40
  6.9 0.4 collective-permute-start.3
  7.3 2.3 %collective-permute-start.4 = (bf16[144,1024]{1,0:T(8,128)(2,1)S(1)}, bf16[144,1024]{1,0:T(8,128)(2,1)S(1)}, u32[]{:S(2)}, u32[]{:S(2)}) collective-permute-start(bf16[144,1024]{1,0:T(8,128)(2,1)S(1)} %prepare.1.a_ref.refs_0_), channel_id=1, source_target_pairs={{0,192},{1,7},{2,194},{3,1},{4,196},{5,3},{6,198},{7,5},{8,200},{9... | collective-permute-start | bytes 884744 | tf_op jit(solution)/shard_map/ppermute | solution.py:40
  9.6 5.7 %collective-permute-start.1 = (bf16[272,1024]{1,0:T(8,128)(2,1)S(1)}, bf16[272,1024]{1,0:T(8,128)(2,1)S(1)}, u32[]{:S(2)}, u32[]{:S(2)}) collective-permute-start(bf16[272,1024]{1,0:T(8,128)(2,1)S(1)} %pack_keys.2.refs_1_.refs_2_), channel_id=1, source_target_pairs={{0,8},{1,57},{2,10},{3,59},{4,12},{5,61},{6,14},{7,63},{8,16},{9,1... | collective-permute-start | bytes 1671176 | tf_op jit(solution)/shard_map/ppermute | solution.py:40
  15.3 1.0 %collective-permute-done.3.refs_2_ = bf16[144,1024]{1,0:T(8,128)(2,1)S(1)} collective-permute-done((bf16[144,1024]{1,0:T(8,128)(2,1)S(1)}, bf16[144,1024]{1,0:T(8,128)(2,1)S(1)}, u32[]{:S(2)}, u32[]{:S(2)}) %collective-permute-start.3) | collective-permute-done | bytes 294944 | tf_op jit(solution)/shard_map/ppermute | solution.py:40
  16.3 0.3 collective-permute-start.7
  16.6 2.4 %collective-permute-start.8 = (bf16[528,1024]{1,0:T(8,128)(2,1)S(1)}, bf16[528,1024]{1,0:T(8,128)(2,1)S(1)}, u32[]{:S(2)}, u32[]{:S(2)}) collective-permute-start(bf16[528,1024]{1,0:T(8,128)(2,1)S(1)} %pack_line.1.refs_0_), channel_id=1, source_target_pairs={{0,6},{1,193},{2,0},{3,195},{4,2},{5,197},{6,4},{7,199},{8,14},{9,... | collective-permute-start | bytes 3244040 | tf_op jit(solution)/shard_map/ppermute | solution.py:40
  19.1 0.5 stage_0.1.refs_0_
  19.6 2.2 %collective-permute-done.1.refs_1_.refs_2_.refs_3_ = bf16[272,1024]{1,0:T(8,128)(2,1)S(1)} collective-permute-done((bf16[272,1024]{1,0:T(8,128)(2,1)S(1)}, bf16[272,1024]{1,0:T(8,128)(2,1)S(1)}, u32[]{:S(2)}, u32[]{:S(2)}) %collective-permute-start.1) | collective-permute-done | bytes 557088 | tf_op jit(solution)/shard_map/ppermute | solution.py:40
  21.7 3.1 %collective-permute-start.5 = (bf16[272,1024]{1,0:T(8,128)(2,1)S(1)}, bf16[272,1024]{1,0:T(8,128)(2,1)S(1)}, u32[]{:S(2)}, u32[]{:S(2)}) collective-permute-start(bf16[272,1024]{1,0:T(8,128)(2,1)S(1)} %collective-permute-done.1.refs_1_.refs_2_.refs_3_), channel_id=1, source_target_pairs={{0,8},{1,57},{2,10},{3,59},{4,12},{5,61},{6,14},{7,63},{8,16},{9,1... | collective-permute-start | bytes 1671176 | tf_op jit(solution)/shard_map/ppermute | solution.py:40
  24.9 0.5 stage_1.1.refs_1_
  25.4 6.0 %collective-permute-done.5.refs_1_.refs_4_.refs_5_ = bf16[272,1024]{1,0:T(8,128)(2,1)S(1)} collective-permute-done((bf16[272,1024]{1,0:T(8,128)(2,1)S(1)}, bf16[272,1024]{1,0:T(8,128)(2,1)S(1)}, u32[]{:S(2)}, u32[]{:S(2)}) %collective-permute-start.5) | collective-permute-done | bytes 557088 | tf_op jit(solution)/shard_map/ppermute | solution.py:40
  31.3 3.2 %collective-permute-start.9 = (bf16[272,1024]{1,0:T(8,128)(2,1)S(1)}, bf16[272,1024]{1,0:T(8,128)(2,1)S(1)}, u32[]{:S(2)}, u32[]{:S(2)}) collective-permute-start(bf16[272,1024]{1,0:T(8,128)(2,1)S(1)} %collective-permute-done.5.refs_1_.refs_4_.refs_5_), channel_id=1, source_target_pairs={{0,1},{1,0},{2,3},{3,2},{4,5},{5,4},{6,7},{7,6},{8,9},{9,8},{10,11... | collective-permute-start | bytes 1671176 | tf_op jit(solution)/shard_map/ppermute | solution.py:40
  34.6 0.5 collective-permute-start.10
  35.1 1.1 %collective-permute-done.9.refs_3_.refs_5_.refs_6_ = bf16[272,1024]{1,0:T(8,128)(2,1)S(1)} collective-permute-done((bf16[272,1024]{1,0:T(8,128)(2,1)S(1)}, bf16[272,1024]{1,0:T(8,128)(2,1)S(1)}, u32[]{:S(2)}, u32[]{:S(2)}) %collective-permute-start.9) | collective-permute-done | bytes 557088 | tf_op jit(solution)/shard_map/ppermute | solution.py:40
  36.1 1.1 %stage_2.1.refs_2_ = f32[2,16,256]{2,1,0:T(8,128)S(1)} custom-call(bf16[528,1024]{1,0:T(8,128)(2,1)S(1)} %pack_line.1.refs_0_, bf16[272,1024]{1,0:T(8,128)(2,1)S(1)} %collective-permute-done.5.refs_1_.refs_4_.refs_5_, bf16[272,1024]{1,0:T(8,128)(2,1)S(1)} %collective-permute-done.6.refs_2_.refs_3_.refs_4_, ...), custom_call_target="tpu_custom_call" | custom-call | tf_op jit(solution)/shard_map/stage_2/pallas_call | solution.py:182
  37.5 2.9 %collective-permute-start.12 = (bf16[272,1024]{1,0:T(8,128)(2,1)S(1)}, bf16[272,1024]{1,0:T(8,128)(2,1)S(1)}, u32[]{:S(2)}, u32[]{:S(2)}) collective-permute-start(bf16[272,1024]{1,0:T(8,128)(2,1)S(1)} %half_far.1), channel_id=1, source_target_pairs={{0,6},{1,193},{2,0},{3,195},{4,2},{5,197},{6,4},{7,199},{8,14},{9,... | collective-permute-start | bytes 1671176 | tf_op jit(solution)/shard_map/ppermute | solution.py:40
  40.4 1.8 %stage_3.1.refs_3_ = f32[2,16,256]{2,1,0:T(8,128)S(1)} custom-call(bf16[528,1024]{1,0:T(8,128)(2,1)S(1)} %collective-permute-done.7.refs_0_.whole_ref.refs_1_, bf16[272,1024]{1,0:T(8,128)(2,1)S(1)} %pack_keys.2.refs_1_.refs_2_, bf16[272,1024]{1,0:T(8,128)(2,1)S(1)} %collective-permute-done.1.refs_1_.refs_2_.refs_3_, ...), custom_call_target="tpu_custom_call" | custom-call | tf_op jit(solution)/shard_map/stage_3/pallas_call | solution.py:182
  42.2 1.0 %collective-permute-done.10.refs_3_.keys_ref.refs_7_ = bf16[272,1024]{1,0:T(8,128)(2,1)S(1)} collective-permute-done((bf16[272,1024]{1,0:T(8,128)(2,1)S(1)}, bf16[272,1024]{1,0:T(8,128)(2,1)S(1)}, u32[]{:S(2)}, u32[]{:S(2)}) %collective-permute-start.10) | collective-permute-done | bytes 557088 | tf_op jit(solution)/shard_map/ppermute | solution.py:40
  43.3 1.8 %collective-permute-start.13 = (bf16[144,1024]{1,0:T(8,128)(2,1)S(1)}, bf16[144,1024]{1,0:T(8,128)(2,1)S(1)}, u32[]{:S(2)}, u32[]{:S(2)}) collective-permute-start(bf16[144,1024]{1,0:T(8,128)(2,1)S(1)} %first_half.1), channel_id=1, source_target_pairs={{0,8},{1,57},{2,10},{3,59},{4,12},{5,61},{6,14},{7,63},{8,16},{9,1... | collective-permute-start | bytes 884744 | tf_op jit(solution)/shard_map/ppermute | solution.py:40
  45.1 1.8 %stage_4.1.refs_4_ = f32[2,16,256]{2,1,0:T(8,128)S(1)} custom-call(bf16[528,1024]{1,0:T(8,128)(2,1)S(1)} %collective-permute-done.8.whole_ref.refs_0_.refs_2_, bf16[272,1024]{1,0:T(8,128)(2,1)S(1)} %pack_keys.2.refs_1_.refs_2_, bf16[272,1024]{1,0:T(8,128)(2,1)S(1)} %collective-permute-done.1.refs_1_.refs_2_.refs_3_, ...), custom_call_target="tpu_custom_call" | custom-call | tf_op jit(solution)/shard_map/stage_4/pallas_call | solution.py:182
  46.9 0.4 collective-permute-start.14
  47.3 1.2 %stage_4b.1.refs_5_ = f32[6,16,256]{2,1,0:T(8,128)S(1)} custom-call(bf16[528,1024]{1,0:T(8,128)(2,1)S(1)} %pack_line.1.refs_0_, bf16[528,1024]{1,0:T(8,128)(2,1)S(1)} %collective-permute-done.7.refs_0_.whole_ref.refs_1_, bf16[528,1024]{1,0:T(8,128)(2,1)S(1)} %collective-permute-done.8.whole_ref.refs_0_.refs_2_, ...), custom_call_target="tpu_custom_call" | custom-call | tf_op jit(solution)/shard_map/stage_4b/pallas_call | solution.py:182
  48.5 2.1 %stage_5.1.refs_6_ = f32[2,16,256]{2,1,0:T(8,128)S(1)} custom-call(bf16[272,1024]{1,0:T(8,128)(2,1)S(1)} %collective-permute-done.11.refs_0_.refs_3_, bf16[272,1024]{1,0:T(8,128)(2,1)S(1)} %collective-permute-done.12.refs_1_.refs_4_, bf16[272,1024]{1,0:T(8,128)(2,1)S(1)} %pack_keys.2.refs_1_.refs_2_, ...), custom_call_target="tpu_custom_call" | custom-call | tf_op jit(solution)/shard_map/stage_5/pallas_call | solution.py:182
  50.6 2.7 %collective-permute-start.15 = (bf16[144,1024]{1,0:T(8,128)(2,1)S(1)}, bf16[144,1024]{1,0:T(8,128)(2,1)S(1)}, u32[]{:S(2)}, u32[]{:S(2)}) collective-permute-start(bf16[144,1024]{1,0:T(8,128)(2,1)S(1)} %collective-permute-done.13.a_ref), channel_id=1, source_target_pairs={{0,1},{1,0},{2,3},{3,2},{4,5},{5,4},{6,7},{7,6},{8,9},{9,8},{10,11... | collective-permute-start | bytes 884744 | tf_op jit(solution)/shard_map/ppermute | solution.py:40
  53.4 1.5 %stage_6.1.refs_7_ = f32[8,16,256]{2,1,0:T(8,128)S(1)} custom-call(bf16[528,1024]{1,0:T(8,128)(2,1)S(1)} %pack_line.1.refs_0_, bf16[528,1024]{1,0:T(8,128)(2,1)S(1)} %collective-permute-done.7.refs_0_.whole_ref.refs_1_, bf16[528,1024]{1,0:T(8,128)(2,1)S(1)} %collective-permute-done.8.whole_ref.refs_0_.refs_2_, ...), custom_call_target="tpu_custom_call" | custom-call | tf_op jit(solution)/shard_map/stage_6/pallas_call | solution.py:182
  54.9 1.5 %stage_7.1.refs_8_ = f32[8,16,256]{2,1,0:T(8,128)S(1)} custom-call(bf16[528,1024]{1,0:T(8,128)(2,1)S(1)} %pack_line.1.refs_0_, bf16[528,1024]{1,0:T(8,128)(2,1)S(1)} %collective-permute-done.7.refs_0_.whole_ref.refs_1_, bf16[528,1024]{1,0:T(8,128)(2,1)S(1)} %collective-permute-done.8.whole_ref.refs_0_.refs_2_, ...), custom_call_target="tpu_custom_call" | custom-call | tf_op jit(solution)/shard_map/stage_7/pallas_call | solution.py:182
  56.5 10.5 %all_to_all.11 = f32[16,2,128]{2,1,0:T(2,128)S(1)} all-to-all(f32[16,2,128]{2,1,0:T(2,128)S(1)} %bitcast.5), channel_id=1, replica_groups=mesh['x'=4,'z'=8,'y'=4,'c'=2] {'x','y'}, dimensions={0} | all-to-all | bytes 32768 | tf_op jit(solution)/shard_map/all_to_all | solution.py:296
  67.1 0.5 finish.1
  (23 shorter events, 0.6 us)
Async XLA Ops:
  0.6 1.0 %copy-start = (bf16[128,1024]{1,0:T(8,128)(2,1)S(1)}, bf16[128,1024]{1,0:T(8,128)(2,1)}, u32[]{:S(2)}) copy-start(bf16[128,1024]{1,0:T(8,128)(2,1)} %rows_ref.1) | copy-start | bytes 786436
  1.6 0.7 copy-start.1
  2.4 7.2 %collective-permute-start = (bf16[144,1024]{1,0:T(8,128)(2,1)S(1)}, bf16[144,1024]{1,0:T(8,128)(2,1)S(1)}, u32[]{:S(2)}, u32[]{:S(2)}) collective-permute-start(bf16[144,1024]{1,0:T(8,128)(2,1)S(1)} %prepare.1.a_ref.refs_0_), channel_id=1, source_target_pairs={{0,1},{1,0},{2,3},{3,2},{4,5},{5,4},{6,7},{7,6},{8,9},{9,8},{10,11... | collective-permute-start | bytes 884744 | tf_op jit(solution)/shard_map/ppermute | solution.py:40
  5.7 9.6 %collective-permute-start.2 = (bf16[144,1024]{1,0:T(8,128)(2,1)S(1)}, bf16[144,1024]{1,0:T(8,128)(2,1)S(1)}, u32[]{:S(2)}, u32[]{:S(2)}) collective-permute-start(bf16[144,1024]{1,0:T(8,128)(2,1)S(1)} %prepare.1.a_ref.refs_0_), channel_id=1, source_target_pairs={{0,128},{1,5},{2,130},{3,7},{4,132},{5,1},{6,134},{7,3},{8,136},{9... | collective-permute-start | bytes 884744 | tf_op jit(solution)/shard_map/ppermute | solution.py:40
  6.9 9.4 %collective-permute-start.3 = (bf16[144,1024]{1,0:T(8,128)(2,1)S(1)}, bf16[144,1024]{1,0:T(8,128)(2,1)S(1)}, u32[]{:S(2)}, u32[]{:S(2)}) collective-permute-start(bf16[144,1024]{1,0:T(8,128)(2,1)S(1)} %prepare.1.a_ref.refs_0_), channel_id=1, source_target_pairs={{0,64},{1,3},{2,66},{3,5},{4,68},{5,7},{6,70},{7,1},{8,72},{9,11},... | collective-permute-start | bytes 884744 | tf_op jit(solution)/shard_map/ppermute | solution.py:40
  7.3 9.0 %collective-permute-start.4 = (bf16[144,1024]{1,0:T(8,128)(2,1)S(1)}, bf16[144,1024]{1,0:T(8,128)(2,1)S(1)}, u32[]{:S(2)}, u32[]{:S(2)}) collective-permute-start(bf16[144,1024]{1,0:T(8,128)(2,1)S(1)} %prepare.1.a_ref.refs_0_), channel_id=1, source_target_pairs={{0,192},{1,7},{2,194},{3,1},{4,196},{5,3},{6,198},{7,5},{8,200},{9... | collective-permute-start | bytes 884744 | tf_op jit(solution)/shard_map/ppermute | solution.py:40
  9.6 12.1 %collective-permute-start.1 = (bf16[272,1024]{1,0:T(8,128)(2,1)S(1)}, bf16[272,1024]{1,0:T(8,128)(2,1)S(1)}, u32[]{:S(2)}, u32[]{:S(2)}) collective-permute-start(bf16[272,1024]{1,0:T(8,128)(2,1)S(1)} %pack_keys.2.refs_1_.refs_2_), channel_id=1, source_target_pairs={{0,8},{1,57},{2,10},{3,59},{4,12},{5,61},{6,14},{7,63},{8,16},{9,1... | collective-permute-start | bytes 1671176 | tf_op jit(solution)/shard_map/ppermute | solution.py:40
  16.3 21.0 %collective-permute-start.7 = (bf16[528,1024]{1,0:T(8,128)(2,1)S(1)}, bf16[528,1024]{1,0:T(8,128)(2,1)S(1)}, u32[]{:S(2)}, u32[]{:S(2)}) collective-permute-start(bf16[528,1024]{1,0:T(8,128)(2,1)S(1)} %pack_line.1.refs_0_), channel_id=1, source_target_pairs={{0,2},{1,65},{2,4},{3,67},{4,6},{5,69},{6,0},{7,71},{8,10},{9,73},... | collective-permute-start | bytes 3244040 | tf_op jit(solution)/shard_map/ppermute | solution.py:40
  16.6 20.7 %collective-permute-start.8 = (bf16[528,1024]{1,0:T(8,128)(2,1)S(1)}, bf16[528,1024]{1,0:T(8,128)(2,1)S(1)}, u32[]{:S(2)}, u32[]{:S(2)}) collective-permute-start(bf16[528,1024]{1,0:T(8,128)(2,1)S(1)} %pack_line.1.refs_0_), channel_id=1, source_target_pairs={{0,6},{1,193},{2,0},{3,195},{4,2},{5,197},{6,4},{7,199},{8,14},{9,... | collective-permute-start | bytes 3244040 | tf_op jit(solution)/shard_map/ppermute | solution.py:40
  21.7 9.6 %collective-permute-start.5 = (bf16[272,1024]{1,0:T(8,128)(2,1)S(1)}, bf16[272,1024]{1,0:T(8,128)(2,1)S(1)}, u32[]{:S(2)}, u32[]{:S(2)}) collective-permute-start(bf16[272,1024]{1,0:T(8,128)(2,1)S(1)} %collective-permute-done.1.refs_1_.refs_2_.refs_3_), channel_id=1, source_target_pairs={{0,8},{1,57},{2,10},{3,59},{4,12},{5,61},{6,14},{7,63},{8,16},{9,1... | collective-permute-start | bytes 1671176 | tf_op jit(solution)/shard_map/ppermute | solution.py:40
  24.9 6.5 %collective-permute-start.6 = (bf16[272,1024]{1,0:T(8,128)(2,1)S(1)}, bf16[272,1024]{1,0:T(8,128)(2,1)S(1)}, u32[]{:S(2)}, u32[]{:S(2)}) collective-permute-start(bf16[272,1024]{1,0:T(8,128)(2,1)S(1)} %collective-permute-done.1.refs_1_.refs_2_.refs_3_), channel_id=1, source_target_pairs={{0,1},{1,0},{2,3},{3,2},{4,5},{5,4},{6,7},{7,6},{8,9},{9,8},{10,11... | collective-permute-start | bytes 1671176 | tf_op jit(solution)/shard_map/ppermute | solution.py:40
  31.3 4.8 %collective-permute-start.9 = (bf16[272,1024]{1,0:T(8,128)(2,1)S(1)}, bf16[272,1024]{1,0:T(8,128)(2,1)S(1)}, u32[]{:S(2)}, u32[]{:S(2)}) collective-permute-start(bf16[272,1024]{1,0:T(8,128)(2,1)S(1)} %collective-permute-done.5.refs_1_.refs_4_.refs_5_), channel_id=1, source_target_pairs={{0,1},{1,0},{2,3},{3,2},{4,5},{5,4},{6,7},{7,6},{8,9},{9,8},{10,11... | collective-permute-start | bytes 1671176 | tf_op jit(solution)/shard_map/ppermute | solution.py:40
  34.6 8.7 %collective-permute-start.10 = (bf16[272,1024]{1,0:T(8,128)(2,1)S(1)}, bf16[272,1024]{1,0:T(8,128)(2,1)S(1)}, u32[]{:S(2)}, u32[]{:S(2)}) collective-permute-start(bf16[272,1024]{1,0:T(8,128)(2,1)S(1)} %collective-permute-done.5.refs_1_.refs_4_.refs_5_), channel_id=1, source_target_pairs={{0,8},{1,57},{2,10},{3,59},{4,12},{5,61},{6,14},{7,63},{8,16},{9,1... | collective-permute-start | bytes 1671176 | tf_op jit(solution)/shard_map/ppermute | solution.py:40
  37.4 11.1 %collective-permute-start.11 = (bf16[272,1024]{1,0:T(8,128)(2,1)S(1)}, bf16[272,1024]{1,0:T(8,128)(2,1)S(1)}, u32[]{:S(2)}, u32[]{:S(2)}) collective-permute-start(bf16[272,1024]{1,0:T(8,128)(2,1)S(1)} %half_near.1), channel_id=1, source_target_pairs={{0,2},{1,65},{2,4},{3,67},{4,6},{5,69},{6,0},{7,71},{8,10},{9,73},... | collective-permute-start | bytes 1671176 | tf_op jit(solution)/shard_map/ppermute | solution.py:40
  37.5 11.0 %collective-permute-start.12 = (bf16[272,1024]{1,0:T(8,128)(2,1)S(1)}, bf16[272,1024]{1,0:T(8,128)(2,1)S(1)}, u32[]{:S(2)}, u32[]{:S(2)}) collective-permute-start(bf16[272,1024]{1,0:T(8,128)(2,1)S(1)} %half_far.1), channel_id=1, source_target_pairs={{0,6},{1,193},{2,0},{3,195},{4,2},{5,197},{6,4},{7,199},{8,14},{9,... | collective-permute-start | bytes 1671176 | tf_op jit(solution)/shard_map/ppermute | solution.py:40
  43.3 7.3 %collective-permute-start.13 = (bf16[144,1024]{1,0:T(8,128)(2,1)S(1)}, bf16[144,1024]{1,0:T(8,128)(2,1)S(1)}, u32[]{:S(2)}, u32[]{:S(2)}) collective-permute-start(bf16[144,1024]{1,0:T(8,128)(2,1)S(1)} %first_half.1), channel_id=1, source_target_pairs={{0,8},{1,57},{2,10},{3,59},{4,12},{5,61},{6,14},{7,63},{8,16},{9,1... | collective-permute-start | bytes 884744 | tf_op jit(solution)/shard_map/ppermute | solution.py:40
  46.9 6.5 %collective-permute-start.14 = (bf16[272,1024]{1,0:T(8,128)(2,1)S(1)}, bf16[272,1024]{1,0:T(8,128)(2,1)S(1)}, u32[]{:S(2)}, u32[]{:S(2)}) collective-permute-start(bf16[272,1024]{1,0:T(8,128)(2,1)S(1)} %collective-permute-done.10.refs_3_.keys_ref.refs_7_), channel_id=1, source_target_pairs={{0,1},{1,0},{2,3},{3,2},{4,5},{5,4},{6,7},{7,6},{8,9},{9,8},{10,11... | collective-permute-start | bytes 1671176 | tf_op jit(solution)/shard_map/ppermute | solution.py:40
  50.6 4.2 %collective-permute-start.15 = (bf16[144,1024]{1,0:T(8,128)(2,1)S(1)}, bf16[144,1024]{1,0:T(8,128)(2,1)S(1)}, u32[]{:S(2)}, u32[]{:S(2)}) collective-permute-start(bf16[144,1024]{1,0:T(8,128)(2,1)S(1)} %collective-permute-done.13.a_ref), channel_id=1, source_target_pairs={{0,1},{1,0},{2,3},{3,2},{4,5},{5,4},{6,7},{7,6},{8,9},{9,8},{10,11... | collective-permute-start | bytes 884744 | tf_op jit(solution)/shard_map/ppermute | solution.py:40
